TPU v7x, 32 devices: a whole 2x2x4 slice. The times are simulated.
32 devices in a mesh: dp: 8 (over y, x, core), tensor: 4 (over z).
Axes of the slice: x: 2, y: 2, z: 4, core: 2. Of those that a mesh axis runs over, the one named last changes fastest.
Arguments:
- inputs: bfloat16 [8192, 768], P(('dp', 'tensor')), may hold values from -6 to 6
- cotangent: bfloat16 [8192, 768], P(('dp', 'tensor')), may hold values from -6 to 6
- lengths: int32 [16], P('dp'), may hold values from 1 to 512, 5120 in all
- w_query: bfloat16 [768, 768], P(None, 'tensor'), may hold values from -0.21875 to 0.21875
- w_key: bfloat16 [768, 768], P(None, 'tensor'), may hold values from -0.21875 to 0.21875
- w_value: bfloat16 [768, 768], P(None, 'tensor'), may hold values from -0.21875 to 0.21875
- b_query: float32 [768], P('tensor'), may hold values from -3 to 3
- b_value: float32 [768], P('tensor'), may hold values from -2 to 2
- w_output: bfloat16 [768, 768], P('tensor'), may hold values from -1.75 to 1.75
- b_output: float32 [768], replicated, may hold values from -2 to 2
- gain_one: float32 [768], replicated, may hold values from 0.5 to 1.5
- shift_one: float32 [768], replicated, may hold values from -2 to 2
- w_hidden: bfloat16 [768, 3072], P(None, 'tensor'), may hold values from -0.21875 to 0.21875
- b_hidden: float32 [3072], P('tensor'), may hold values from -3 to 3
- w_back: bfloat16 [3072, 768], P('tensor'), may hold values from -0.109375 to 0.109375
- b_back: float32 [768], replicated, may hold values from -2 to 2
- gain_two: float32 [768], replicated, may hold values from 0.5 to 1.5
- shift_two: float32 [768], replicated, may hold values from -2 to 2
Outputs:
- outputs: bfloat16 [8192, 768], P(('dp', 'tensor'))
- input_grad: bfloat16 [8192, 768], P(('dp', 'tensor'))
- grad_w_query: float32 [768, 768], P(None, 'tensor')
- grad_w_key: float32 [768, 768], P(None, 'tensor')
- grad_w_value: float32 [768, 768], P(None, 'tensor')
- grad_b_query: float32 [768], P('tensor')
- grad_b_value: float32 [768], P('tensor')
- grad_w_output: float32 [768, 768], P('tensor')
- grad_b_output: float32 [768], replicated
- grad_gain_one: float32 [768], replicated
- grad_shift_one: float32 [768], replicated
- grad_w_hidden: float32 [768, 3072], P(None, 'tensor')
- grad_b_hidden: float32 [3072], P('tensor')
- grad_w_back: float32 [3072, 768], P('tensor')
- grad_b_back: float32 [768], replicated
- grad_gain_two: float32 [768], replicated
- grad_shift_two: float32 [768], replicated
Inputs may be any that keep to these rules, and one draw needn't show every extreme that they name: lengths[s] counts the live rows at the start of slot s; the longest is exactly 512.
All inputs are finite; a program needn't handle non-finite values. No bound on the sum of `lengths` on one device may be relied on, other than what follows from the above.
Results may differ from a plain program's by a relative error of at most 0.02.
Values may be sent and summed in bfloat16 or wider, within the bound.
No kernel may reach another device: no remote copies, remote signals or barrier semaphores. Data moves between devices by JAX's collectives and lax.ppermute only.
A program may use at most 128 MiB of HBM per device.

v0:
```python
import functools

import jax
import jax.numpy as jnp
from jax import lax
from jax.experimental import pallas as pl
from jax.experimental.pallas import tpu as pltpu
from jax.sharding import PartitionSpec as P

HD = 64
LANES = 128
PLANE = 8
CORE, XBIT, YBIT = 1, 2, 4
BF16, F32 = jnp.bfloat16, jnp.float32


def dot_nn(a, b):
    return lax.dot_general(a, b, (((1,), (0,)), ((), ())), preferred_element_type=F32)


def dot_nt(a, b):
    return lax.dot_general(a, b, (((1,), (1,)), ((), ())), preferred_element_type=F32)


def dot_tn(a, b):
    return lax.dot_general(a, b, (((0,), (0,)), ((), ())), preferred_element_type=F32)


def swap(v, axis, bit):
    count = lax.axis_size(axis)
    return lax.ppermute(v, axis, [(i, i ^ bit) for i in range(count)])


def pack_kernel(moves, count, place_ref, *refs):
    out_ref, sem = refs[-2], refs[-1]
    core, chip = place_ref[0], place_ref[1]
    copies = []
    for k, (which, source, target) in enumerate(moves):
        src = refs[which].at[source(core, chip)]
        dst = out_ref.at[target]
        copies.append(pltpu.make_async_copy(src, dst, sem.at[k]))
    for copy in copies:
        copy.start()
    for copy in copies:
        copy.wait()


def pack(where, shape, moves, arrays, earlier=()):
    space = pl.BlockSpec(memory_space=pl.ANY)
    return pl.pallas_call(
        functools.partial(pack_kernel, moves, len(arrays)),
        in_specs=[pl.BlockSpec(memory_space=pltpu.SMEM)] + [space] * (len(arrays) + len(earlier)),
        out_specs=pl.BlockSpec(memory_space=pltpu.VMEM),
        out_shape=jax.ShapeDtypeStruct(shape, BF16),
        scratch_shapes=[pltpu.SemaphoreType.DMA((len(moves),))],
        compiler_params=pltpu.CompilerParams(vmem_limit_bytes=16 * 1024 * 1024),
    )(where, *arrays, *earlier)


def at(*index):
    return lambda core, chip: index


def stacked(where, arrays, rows, earlier=()):
    top = pl.ds(0, rows)
    moves = [(i, at(top), (i,)) for i in range(len(arrays))]
    return pack(where, (len(arrays), rows) + arrays[0].shape[1:], moves, arrays, earlier)


def from_shards(v):
    return [swap(v, "tensor", k) for k in range(1, lax.axis_size("tensor"))]


def halves_from_chips(where, v, between=()):
    v_x, v_y = swap(v, "dp", XBIT), swap(v, "dp", YBIT)
    half = v.shape[1] // 2
    low, high = (slice(None), pl.ds(0, half)), (slice(None), pl.ds(half, half))
    shape = (v.shape[0], half) + v.shape[2:]
    v_xy = swap(pack(where, shape, [(0, at(*low), ())], [v_x], between), "dp", YBIT)
    v_yx = swap(pack(where, shape, [(0, at(*high), ())], [v_y], between), "dp", XBIT)
    return [v, v_x, v_y, v_xy, v_yx]


def from_chips(v):
    return [v] + [swap(v, "dp", bits) for bits in (XBIT, YBIT, XBIT | YBIT)]


def add(a, b):
    return (a.astype(F32) + b.astype(F32)).astype(BF16)


def shards_reduce(pieces):
    total = pieces[0].astype(F32)
    for k in range(1, len(pieces)):
        total = total + swap(pieces[k], "tensor", k).astype(F32)
    step = PLANE
    while step < lax.axis_size("dp"):
        total = total + swap(total, "dp", step)
        step *= 2
    return total.astype(BF16)


def relative(v, axis, where_me):
    size = v.shape[axis]
    bits = size.bit_length() - 1
    shape = v.shape
    v = v.reshape(shape[:axis] + (2,) * bits + shape[axis + 1 :])
    for b in range(bits):
        on = (where_me >> (bits - 1 - b)) & 1
        v = jnp.where(on == 1, jnp.flip(v, axis + b), v)
    return v.reshape(shape)


def qkv_kernel(
    place_ref, own, other, x_ref, xo_ref, bq_ref, bv_ref, q_ref, k_ref, v_ref, *refs
):
    weights, sem = refs[:4], refs[4]
    core = place_ref[0]
    rows, width = x_ref.shape

    def copies(src, group):
        return [
            pltpu.make_async_copy(
                src.at[j, :, m], weights[2 * group + m].at[:, :, j], sem.at[group, m, j]
            )
            for m in range(2)
            for j in range(4)
        ]

    for group in (0, 1):

        @pl.when(core == group)
        def _():
            for copy in copies(own, group):
                copy.start()

        @pl.when(core != group)
        def _():
            for copy in copies(other, group):
                copy.start()

    def landed(group):
        @pl.when(core == group)
        def _():
            for copy in copies(own, group):
                copy.wait()

        @pl.when(core != group)
        def _():
            for copy in copies(other, group):
                copy.wait()

    landed(0)
    x, xo = x_ref[...], xo_ref[...]
    q_ref[...] = (dot_nt(x, weights[0][...].reshape(width, width)) + bq_ref[...]).astype(BF16)
    w = weights[1][...].reshape(width, width)
    k_ref[:rows] = dot_nt(x, w).astype(BF16)
    k_ref[rows:] = dot_nt(xo, w).astype(BF16)
    landed(1)
    w = weights[2][...].reshape(width, width)
    v_ref[:rows] = (dot_nt(x, w) + bv_ref[...]).astype(BF16)
    v_ref[rows:] = (dot_nt(xo, w) + bv_ref[...]).astype(BF16)


def project(where, own, other, x, xo, bq, bv):
    rows, width = x.shape
    _, shards, _, heads, part, _ = own.shape
    vmem = pl.BlockSpec(memory_space=pltpu.VMEM)
    space = pl.BlockSpec(memory_space=pl.ANY)
    weight = jax.ShapeDtypeStruct((shards, heads, 4, part, width), BF16)
    return pl.pallas_call(
        qkv_kernel,
        in_specs=[pl.BlockSpec(memory_space=pltpu.SMEM), space, space] + [vmem] * 4,
        out_specs=[vmem] * 7,
        out_shape=[
            jax.ShapeDtypeStruct((rows, width), BF16),
            jax.ShapeDtypeStruct((2 * rows, width), BF16),
            jax.ShapeDtypeStruct((2 * rows, width), BF16),
        ]
        + [weight] * 4,
        scratch_shapes=[pltpu.SemaphoreType.DMA((2, 2, 4))],
        compiler_params=pltpu.CompilerParams(vmem_limit_bytes=40 * 1024 * 1024),
        cost_estimate=pl.CostEstimate(flops=4 * 10**9, bytes_accessed=10**7, transcendentals=0),
    )(where, own, other, x, xo, bq, bv)


def att_out_kernel(place_ref, own_ref, other_ref, gq_ref, gk_ref, gv_ref, go_ref, extra_ref):
    core, chip = place_ref[0], place_ref[1]
    head_cols, width = go_ref.shape
    heads, part = head_cols // HD, HD // 4
    rows = own_ref.shape[1]
    for group in (0, 1):
        blocks = []
        for c in range(4):
            block = jnp.where(core == group, own_ref[c ^ chip], other_ref[c ^ chip])
            spot = (group * 4 + c) * rows
            extra_ref[spot : spot + rows] = block[:, width:].astype(F32)
            blocks.append(block[:, :width])
        for m in range(2):
            pieces = [
                blocks[c][(m * heads + h) * part : (m * heads + h + 1) * part]
                for h in range(heads)
                for c in range(4)
            ]
            whole = jnp.concatenate(pieces, axis=0).astype(F32)
            if group == 1 and m == 1:
                go_ref[...] = whole
            else:
                (gq_ref, gk_ref, gv_ref)[2 * group + m][...] = whole.T


def att_outputs(where, own, other, head_cols, width):
    vmem = pl.BlockSpec(memory_space=pltpu.VMEM)
    turned = jax.ShapeDtypeStruct((width, head_cols), F32)
    return pl.pallas_call(
        att_out_kernel,
        in_specs=[pl.BlockSpec(memory_space=pltpu.SMEM), vmem, vmem],
        out_specs=[vmem] * 5,
        out_shape=[
            turned,
            turned,
            turned,
            jax.ShapeDtypeStruct((head_cols, width), F32),
            jax.ShapeDtypeStruct((2 * 4 * own.shape[1], own.shape[2] - width), F32),
        ],
        compiler_params=pltpu.CompilerParams(vmem_limit_bytes=32 * 1024 * 1024),
    )(where, own, other)


def ffn_out_kernel(place_ref, own_ref, other_ref, back_ref, hid_ref):
    core, chip = place_ref[0], place_ref[1]
    rows = own_ref.shape[2]
    blocks = []
    for group in (0, 1):
        for c in range(4):
            block = jnp.where(core == group, own_ref[c ^ chip], other_ref[c ^ chip])
            spot = (group * 4 + c) * rows
            back_ref[spot : spot + rows] = block[0].astype(F32)
            blocks.append(block[1])
    hid_ref[...] = jnp.concatenate(blocks, axis=0).astype(F32).T


def ffn_outputs(where, own, other, hidden, width):
    vmem = pl.BlockSpec(memory_space=pltpu.VMEM)
    return pl.pallas_call(
        ffn_out_kernel,
        in_specs=[pl.BlockSpec(memory_space=pltpu.SMEM), vmem, vmem],
        out_specs=[vmem] * 2,
        out_shape=[
            jax.ShapeDtypeStruct((hidden, width), F32),
            jax.ShapeDtypeStruct((width, hidden), F32),
        ],
        compiler_params=pltpu.CompilerParams(vmem_limit_bytes=32 * 1024 * 1024),
    )(where, own, other)


def live_keys(place_ref, keys, half_rows):
    spot = lax.broadcasted_iota(jnp.int32, (keys, 1), 0)
    first = place_ref[1]
    spot = jnp.where(spot < half_rows, spot + first, spot - first)
    return spot < place_ref[0]


def attend_kernel(place_ref, q_ref, k_ref, v_ref, _, out_ref, lse_ref, *, half_rows):
    rows, keys = q_ref.shape[0], k_ref.shape[0]
    q = q_ref[...] * jnp.asarray(0.125, BF16)
    k = k_ref[...]
    v_turned = v_ref[...].T
    live = live_keys(place_ref, keys, half_rows)
    lane = lax.broadcasted_iota(jnp.int32, (rows, LANES), 1)
    outs, sums = [], []
    for h in range(LANES // HD):
        qh = jnp.where((lane // HD) == h, q, jnp.zeros_like(q))
        s = jnp.where(live, dot_nt(k, qh), -1e30)
        top = jnp.max(s, axis=0, keepdims=True)
        e = jnp.exp(s - top)
        total = jnp.sum(e, axis=0, keepdims=True)
        p = (e * (1.0 / total)).astype(BF16)
        outs.append(dot_nn(v_turned, p)[h * HD : (h + 1) * HD])
        sums.append(top + jnp.log(total))
    out_ref[...] = jnp.concatenate(outs, axis=0).T.astype(BF16)
    lse_ref[...] = jnp.concatenate(sums + [jnp.zeros((6, rows), F32)], axis=0)


def attend_back_kernel(
    place_ref, q_ref, k_ref, v_ref, lse_ref, do_ref, _, dq_ref, dk_ref, dv_ref, *, half_rows
):
    rows, keys = q_ref.shape[0], k_ref.shape[0]
    k, v, do = k_ref[...], v_ref[...], do_ref[...]
    q = q_ref[...] * jnp.asarray(0.125, BF16)
    k_turned = k.T
    live = live_keys(place_ref, keys, half_rows)
    lane = lax.broadcasted_iota(jnp.int32, (rows, LANES), 1)
    dqs, dks, dvs = [], [], []
    for h in range(LANES // HD):
        mine = (lane // HD) == h
        qh = jnp.where(mine, q, jnp.zeros_like(q))
        doh = jnp.where(mine, do, jnp.zeros_like(do))
        s = jnp.where(live, dot_nt(k, qh), -1e30)
        p = jnp.exp(s - lse_ref[h : h + 1, :])
        dp = dot_nt(v, doh)
        inner = jnp.sum(p * dp, axis=0, keepdims=True)
        ds = (p * (dp - inner)).astype(BF16)
        dqs.append(dot_nn(k_turned, ds)[h * HD : (h + 1) * HD])
        dks.append(dot_nn(ds, qh))
        dvs.append(dot_nn(p.astype(BF16), doh))
    dq_ref[...] = (jnp.concatenate(dqs, axis=0).T * 0.125).astype(BF16)
    dk_ref[...] = (dks[0] + dks[1]).astype(BF16)
    dv_ref[...] = (dvs[0] + dvs[1]).astype(BF16)


def attend(place, q, k, v, earlier):
    rows, width = q.shape
    keys = k.shape[0]
    q_spec = pl.BlockSpec((rows, LANES), lambda i: (0, i))
    k_spec = pl.BlockSpec((keys, LANES), lambda i: (0, i))
    lse_spec = pl.BlockSpec((8, rows), lambda i: (i, 0))
    pairs = width // LANES
    return pl.pallas_call(
        functools.partial(attend_kernel, half_rows=rows),
        grid=(pairs,),
        in_specs=[
            pl.BlockSpec(memory_space=pltpu.SMEM),
            q_spec,
            k_spec,
            k_spec,
            pl.BlockSpec(memory_space=pl.ANY),
        ],
        out_specs=[q_spec, lse_spec],
        out_shape=[
            jax.ShapeDtypeStruct((rows, width), BF16),
            jax.ShapeDtypeStruct((8 * pairs, rows), F32),
        ],
        compiler_params=pltpu.CompilerParams(vmem_limit_bytes=32 * 1024 * 1024),
        cost_estimate=pl.CostEstimate(
            flops=70 * rows * keys * width, bytes_accessed=8 * rows * width, transcendentals=0
        ),
    )(place, q, k, v, earlier)


def attend_back(place, q, k, v, lse, do, earlier):
    rows, width = q.shape
    keys = k.shape[0]
    q_spec = pl.BlockSpec((rows, LANES), lambda i: (0, i))
    k_spec = pl.BlockSpec((keys, LANES), lambda i: (0, i))
    lse_spec = pl.BlockSpec((8, rows), lambda i: (i, 0))
    return pl.pallas_call(
        functools.partial(attend_back_kernel, half_rows=rows),
        grid=(width // LANES,),
        in_specs=[
            pl.BlockSpec(memory_space=pltpu.SMEM),
            q_spec,
            k_spec,
            k_spec,
            lse_spec,
            q_spec,
            pl.BlockSpec(memory_space=pl.ANY),
        ],
        out_specs=[q_spec, k_spec, k_spec],
        out_shape=[
            jax.ShapeDtypeStruct((rows, width), BF16),
            jax.ShapeDtypeStruct((keys, width), BF16),
            jax.ShapeDtypeStruct((keys, width), BF16),
        ],
        compiler_params=pltpu.CompilerParams(vmem_limit_bytes=32 * 1024 * 1024),
        cost_estimate=pl.CostEstimate(
            flops=90 * rows * keys * width, bytes_accessed=16 * rows * width, transcendentals=0
        ),
    )(place, q, k, v, lse, do, earlier)


def weights_kernel(
    core_ref,
    dq_ref,
    dk_ref,
    dv_ref,
    context_ref,
    ga_ref,
    x_ref,
    xo_ref,
    extra_ref,
    keep_ref,
    send_ref,
):
    rows, width = dq_ref.shape
    shards = keep_ref.shape[1]
    group = width // shards
    heads = group // HD
    part = HD // 4
    core = core_ref[0]
    span = 2 * group
    lane = lax.broadcasted_iota(jnp.int32, (part, LANES), 1)
    spots = lax.broadcasted_iota(jnp.int32, (8, LANES), 0)
    spots = (spots == lax.broadcasted_iota(jnp.int32, (8, LANES), 1)).astype(BF16)
    extra_all = dot_tn(extra_ref[...], spots)
    att_rows = keep_ref.shape[2]

    def put(which, m, left_ref, rights, with_sum):
        ones = jnp.ones((rows, LANES), BF16)
        for first in range(0, width, span):
            out, sums = None, None
            for k, right in enumerate(rights):
                left = left_ref[k * rows : (k + 1) * rows, first : first + span]
                more = dot_tn(left, right[...])
                out = more if out is None else out + more
                if with_sum:
                    more = dot_tn(left, ones)
                    sums = more if sums is None else sums + more

            def store(dst, base):
                for at in range(0, span, part):
                    row = first + at
                    shard, rest = row // group, row % group
                    head, j = rest // HD, (rest % HD) // part
                    spot = (m * heads + head) * part
                    dst[j, shard, spot : spot + part, :width] = out[at : at + part].astype(BF16)
                    line = base + (j * shards + shard) * att_rows + spot
                    tail = extra_all[line : line + part]
                    if with_sum:
                        tail = jnp.where(lane == 0, sums[at : at + part], tail)
                    dst[j, shard, spot : spot + part, width:] = tail.astype(BF16)

            @pl.when(core == which)
            def _():
                store(keep_ref, 0)

            @pl.when(core != which)
            def _():
                store(send_ref, 4 * shards * att_rows)

    put(0, 0, dq_ref, [x_ref], True)
    put(0, 1, dk_ref, [x_ref, xo_ref], False)
    put(1, 0, dv_ref, [x_ref, xo_ref], True)
    put(1, 1, context_ref, [ga_ref], False)


def attention_weight_grads(core, dq, dk, dv, context, ga, x, xo, extra, shards):
    width = dq.shape[1]
    full = jax.ShapeDtypeStruct((4, shards, width // (2 * shards), width + LANES), BF16)
    vmem = pl.BlockSpec(memory_space=pltpu.VMEM)
    return pl.pallas_call(
        weights_kernel,
        in_specs=[pl.BlockSpec(memory_space=pltpu.SMEM)] + [vmem] * 8,
        out_specs=[vmem, vmem],
        out_shape=[full, full],
        compiler_params=pltpu.CompilerParams(vmem_limit_bytes=40 * 1024 * 1024),
        cost_estimate=pl.CostEstimate(
            flops=6 * 10**9, bytes_accessed=12 * 10**6, transcendentals=0
        ),
    )(core, dq, dk, dv, context, ga, x, xo, extra)


def whole_call(kernel, outs, args, flops):
    vmem = pl.BlockSpec(memory_space=pltpu.VMEM)
    return pl.pallas_call(
        kernel,
        in_specs=[vmem] * len(args),
        out_specs=[vmem] * len(outs),
        out_shape=[jax.ShapeDtypeStruct(shape, dtype) for shape, dtype in outs],
        compiler_params=pltpu.CompilerParams(vmem_limit_bytes=48 * 1024 * 1024),
        cost_estimate=pl.CostEstimate(flops=flops, bytes_accessed=10**6, transcendentals=0),
    )(*args)


def normalize(z):
    center = z - jnp.mean(z, axis=-1, keepdims=True)
    spread = jnp.mean(center * center, axis=-1, keepdims=True)
    scale = lax.rsqrt(spread + 1e-05)
    return center * scale, scale


def norm_back(grad, zhat, scale, gain):
    e = grad * gain
    inner = jnp.mean(e * zhat, axis=-1, keepdims=True)
    return (e - jnp.mean(e, axis=-1, keepdims=True) - zhat * inner) * scale


def column_sums(v):
    return jnp.sum(v, axis=0, keepdims=True)


def mid_kernel(context_ref, wo_ref, x_ref, b_ref, gain_ref, shift_ref, mid_ref, zhat_ref, scale_ref):
    z = dot_nn(context_ref[...], wo_ref[...]) + b_ref[...] + x_ref[...].astype(F32)
    zhat, scale = normalize(z)
    mid_ref[...] = (zhat * gain_ref[...] + shift_ref[...]).astype(BF16)
    zhat_ref[...] = zhat
    scale_ref[...] = jnp.broadcast_to(scale, scale_ref.shape)


def hidden_kernel(mid_ref, w_ref, b_ref, act_ref, slope_ref):
    block = 512
    for first in range(0, w_ref.shape[0], block):
        cols = slice(first, first + block)
        act, slope = gelu_pair(dot_nt(mid_ref[...], w_ref[cols]) + b_ref[:, cols])
        act_ref[:, cols] = act.astype(BF16)
        slope_ref[:, cols] = slope.astype(BF16)


def branch_kernel(
    act_own_ref,
    act_other_ref,
    w_own_ref,
    w_other_ref,
    mid_ref,
    b_ref,
    gain_ref,
    shift_ref,
    cotangent_ref,
    out_ref,
    grad_ref,
    low_ref,
    sums_ref,
):
    z = dot_nn(act_own_ref[...], w_own_ref[...]) + dot_nn(act_other_ref[...], w_other_ref[...])
    zhat, scale = normalize(z + b_ref[...] + mid_ref[...].astype(F32))
    out_ref[...] = (zhat * gain_ref[...] + shift_ref[...]).astype(BF16)
    c = cotangent_ref[...].astype(F32)
    grad = norm_back(c, zhat, scale, gain_ref[...])
    low = grad.astype(BF16)
    grad_ref[...] = grad
    low_ref[...] = low
    sums_ref[...] = jnp.concatenate(
        [column_sums(low.astype(F32)), column_sums(c * zhat), column_sums(c)], axis=0
    )


def pair_grads_kernel(left_own_ref, left_other_ref, right_ref, keep_ref, send_ref):
    send_ref[...] = dot_tn(left_other_ref[...], right_ref[...]).astype(BF16)
    keep_ref[...] = dot_tn(left_own_ref[...], right_ref[...]).astype(BF16)


def pre_kernel(
    low_ref, w_own_ref, w_other_ref, slope_own_ref, slope_other_ref, own_ref, other_ref, sums_ref
):
    half = own_ref.shape[1]
    for k, (w, slope, out) in enumerate(
        ((w_own_ref, slope_own_ref, own_ref), (w_other_ref, slope_other_ref, other_ref))
    ):
        grad = (dot_nt(low_ref[...], w[...]) * slope[...].astype(F32)).astype(BF16)
        out[...] = grad
        sums_ref[:, k * half : (k + 1) * half] = column_sums(grad.astype(F32))


def first_kernel(
    pre_own_ref,
    pre_other_ref,
    w_own_ref,
    w_other_ref,
    grad_ref,
    zhat_ref,
    scale_ref,
    gain_ref,
    wo_ref,
    first_ref,
    low_ref,
    context_ref,
    sums_ref,
):
    grad = dot_nn(pre_own_ref[...], w_own_ref[...]) + dot_nn(pre_other_ref[...], w_other_ref[...])
    grad = grad + grad_ref[...]
    zhat = zhat_ref[...]
    first = norm_back(grad, zhat, scale_ref[:, :1], gain_ref[...])
    low = first.astype(BF16)
    first_ref[...] = first
    low_ref[...] = low
    context_ref[...] = dot_nt(low, wo_ref[...]).astype(BF16)
    sums_ref[...] = jnp.concatenate(
        [column_sums(low.astype(F32)), column_sums(grad * zhat), column_sums(grad)], axis=0
    )


def gelu_pair(v):
    cdf = 0.5 * (1.0 + lax.erf(v * (0.5**0.5)))
    density = jnp.exp(-0.5 * v * v) * 0.3989422804014327
    return v * cdf, cdf + v * density


def local(
    inputs,
    cotangent,
    lengths,
    w_query,
    w_key,
    w_value,
    b_query,
    b_value,
    w_output,
    b_output,
    gain_one,
    shift_one,
    w_hidden,
    b_hidden,
    w_back,
    b_back,
    gain_two,
    shift_two,
):
    rows, width = inputs.shape
    shards = lax.axis_size("tensor")
    head_cols = w_query.shape[1]
    hidden = w_hidden.shape[1]
    heads = head_cols // HD
    part = HD // 4
    ffn_rows = hidden // PLANE
    per_slot = shards // lengths.shape[0]
    assert per_slot == 2 and shards == 4 and lax.axis_size("dp") % PLANE == 0
    dp = lax.axis_index("dp")
    core = dp & 1
    chip = (((dp >> 2) & 1) << 1) | ((dp >> 1) & 1)
    me = core * 4 + chip
    t = lax.axis_index("tensor")

    where = jnp.stack([core, chip]).astype(jnp.int32)
    att_rows = 2 * heads * part
    far = pl.ds(1, shards - 1)

    by_head = (heads, 4, part, width)
    pair = [
        jnp.where(core == 0, w_query, w_value).T.reshape(by_head),
        jnp.where(core == 0, w_key.T, w_output).reshape(by_head),
    ]
    hid_near = lax.dynamic_slice_in_dim(w_hidden, core * (hidden // 2), hidden // 2, 1)
    hid_near = hid_near.T.reshape(4, ffn_rows, width)
    back_near = w_back.reshape(PLANE, ffn_rows, width)
    bias = jnp.concatenate([b_query, b_value, b_hidden]).reshape(-1, LANES)
    bias_high = lax.reduce_precision(bias, 8, 7)
    bias_rows = jnp.concatenate([bias_high, bias - bias_high]).astype(BF16).reshape(-1, width)
    bias_rows = jnp.pad(bias_rows, ((0, 16 - bias_rows.shape[0]), (0, 0)))

    def near_heads(j):
        return lambda core, chip: (slice(None), chip ^ j)

    def near_hid(j):
        return lambda core, chip: (chip ^ j,)

    def near_back(j):
        return lambda core, chip: (core * 4 + (chip ^ j),)

    att_send = pack(
        where, (2, heads, part, width), [(0, near_heads(0), (0,)), (1, near_heads(0), (1,))], pair
    )
    att_z = from_shards(att_send.reshape(att_rows, width))
    packed = pack(
        where,
        (ffn_rows + 16, width),
        [(0, near_hid(0), (pl.ds(0, ffn_rows),)), (1, at(), (pl.ds(ffn_rows, 16),))],
        [hid_near, bias_rows],
        att_z,
    )
    hid_z = from_shards(packed)
    rows_other = swap(pack(where, inputs.shape, [(0, at(), ())], [inputs], hid_z[:1]), "tensor", 1)
    back_send = pack(where, (ffn_rows, width), [(0, near_back(0), ())], [back_near], hid_z)
    back_z = from_shards(back_send)

    att_far = from_chips(stacked(where, att_z, att_rows))
    shape = (4, shards, 2, heads, part, width)
    moves = [(m, near_heads(j), (j, 0, m)) for j in range(4) for m in range(2)]
    moves += [(2 + j, at(), (j, far)) for j in range(4)]
    att_far = [v.reshape(shards - 1, 2, heads, part, width) for v in att_far]
    att_own = pack(where, shape, moves, pair + att_far, hid_z)
    att_swap = swap(att_own, "dp", CORE)

    def ffn_half(near, near_index, far_slices, earlier):
        halves = [pl.ds(0, ffn_rows // 2), pl.ds(ffn_rows // 2, ffn_rows // 2)]
        moves = [(0, near_index(j), (j, 0)) for j in range(4)]
        moves += [(1 + j, at(), (j, far)) for j in range(3)]
        moves += [(4 + k, at(), (3, far, halves[k])) for k in range(2)]
        own = pack(where, (4, shards, ffn_rows, width), moves, [near] + far_slices, earlier)
        own = own.reshape(-1, width)
        return own, swap(own, "dp", CORE)

    hid_far = halves_from_chips(where, stacked(where, hid_z, ffn_rows, att_far[1:]))
    hid_own, hid_swap = ffn_half(hid_near, near_hid, hid_far, ())

    bias = jnp.stack([packed[ffn_rows:]] + [v[ffn_rows:] for v in hid_z]).astype(F32)
    bias = bias.reshape(shards, -1)
    count = 2 * head_cols + hidden
    bias = bias[:, :count] + bias[:, count : 2 * count]

    def relative_heads(v):
        return relative(v.reshape(shards * heads, 4, part), 1, chip).reshape(-1)

    bq = relative_heads(bias[:, :head_cols])
    bv = relative_heads(bias[:, head_cols : 2 * head_cols])
    bh = relative(bias[:, 2 * head_cols :].reshape(shards, PLANE, ffn_rows), 1, me)
    bh = bh.transpose(1, 0, 2).reshape(2, 4 * hidden // 2)

    queries, key_rows, values, wq, wk, wv, wo = project(
        where, att_own, att_swap, inputs, rows_other, bq[None], bv[None]
    )
    wq, wk, wv, wo = (w.reshape(shards * head_cols, width) for w in (wq, wk, wv, wo))
    place = jnp.stack([lengths[t // per_slot], (t % per_slot) * rows]).astype(jnp.int32)
    back_stack = stacked(where, back_z, ffn_rows, (queries, hid_far[1], hid_far[2]))
    context, logsum = attend(place, queries, key_rows, values, back_stack)
    back_far = halves_from_chips(where, back_stack, (context,))
    back_own, back_swap = ffn_half(back_near, near_back, back_far, ())
    full, low = ((rows, width), F32), ((rows, width), BF16)
    half_low = ((rows, 2 * hidden), BF16)
    three = ((3, width), F32)
    mid, zhat_one, scale_one = whole_call(
        mid_kernel,
        [low, full, ((rows, LANES), F32)],
        (context, wo, inputs, b_output[None], gain_one[None], shift_one[None]),
        10**9,
    )
    act_own, slope_own = whole_call(
        hidden_kernel, [half_low, half_low], (mid, hid_own, bh[:1]), 3 * 10**9
    )
    act_swap, slope_swap = whole_call(
        hidden_kernel, [half_low, half_low], (mid, hid_swap, bh[1:]), 3 * 10**9
    )
    outputs, grad_second, grad_branch, sums_two = whole_call(
        branch_kernel,
        [low, full, low, three],
        (
            act_own,
            act_swap,
            back_own,
            back_swap,
            mid,
            b_back[None],
            gain_two[None],
            shift_two[None],
            cotangent,
        ),
        3 * 10**9,
    )

    quarter = (2, 2, shards, ffn_rows, width)
    pair_out = [((2 * hidden, width), BF16)] * 2
    back_keep, back_send = whole_call(
        pair_grads_kernel, pair_out, (act_own, act_swap, grad_branch), 2 * 10**9
    )
    back_part = add(back_keep, swap(back_send, "dp", CORE)).reshape(quarter)
    pre_own, pre_swap, grad_b_hidden = whole_call(
        pre_kernel,
        [half_low, half_low, ((1, 4 * hidden), F32)],
        (grad_branch, back_own, back_swap, slope_own, slope_swap),
        2 * 10**9,
    )
    hid_keep, hid_send = whole_call(pair_grads_kernel, pair_out, (pre_own, pre_swap, mid), 2 * 10**9)
    hid_part = add(hid_keep, swap(hid_send, "dp", CORE)).reshape(quarter)
    back_x = swap(back_part[:, 1], "dp", XBIT)
    hid_y = swap(hid_part[1], "dp", YBIT)
    grad_first, grad_attn, grad_context, sums_one = whole_call(
        first_kernel,
        [full, low, low, three],
        (
            pre_own,
            pre_swap,
            hid_own,
            hid_swap,
            grad_second,
            zhat_one,
            scale_one,
            gain_one[None],
            wo,
        ),
        3 * 10**9,
    )
    grad_queries, grad_keys, grad_values = attend_back(
        place, queries, key_rows, values, logsum, grad_context, hid_part
    )

    whole = jnp.concatenate([sums_one, sums_two], axis=0)
    whole = relative(whole.reshape(6, PLANE, 1, ffn_rows), 1, me)
    whole = jnp.broadcast_to(whole, (6, PLANE, shards, ffn_rows)).reshape(6, -1)
    extra = jnp.concatenate([jnp.zeros_like(grad_b_hidden), grad_b_hidden, whole], axis=0)
    extra = extra.astype(BF16)
    att_keep, att_send = attention_weight_grads(
        core.astype(jnp.int32).reshape(1),
        grad_queries,
        grad_keys,
        grad_values,
        context,
        grad_attn,
        inputs,
        rows_other,
        extra,
        shards,
    )
    wide = att_keep.shape[-1]
    att_part = add(att_keep, swap(att_send, "dp", CORE)).reshape(2, 2, shards, -1, wide)

    total = dot_nn(grad_keys, wk) + dot_nn(grad_values, wv)
    returned = swap(total[rows:].astype(BF16), "tensor", 1).astype(F32)
    input_grad = (total[:rows] + dot_nn(grad_queries, wq) + returned + grad_first).astype(BF16)

    back_part = add(back_part[:, 0], back_x)
    hid_part = add(hid_part[0], hid_y)

    def later(v):
        return pack(where, v.shape, [(0, at(), ())], [v], (att_send,))

    back_sum = add(back_part[0], swap(later(back_part[1]), "dp", YBIT))
    hid_sum = add(hid_part[0], swap(later(hid_part[1]), "dp", XBIT))
    two = shards // 2
    att_a, att_b = att_part[:, :, :two], att_part[:, :, two:]
    att_a = add(att_a[:, 0], swap(att_a[:, 1], "dp", XBIT))
    att_b = add(att_b[0], swap(att_b[1], "dp", YBIT))
    att_a = add(att_a[0], swap(att_a[1], "dp", YBIT))
    att_b = add(att_b[0], swap(att_b[1], "dp", XBIT))
    ffn_sum = shards_reduce([jnp.stack([back_sum[k], hid_sum[k]]) for k in range(shards)])
    halves = [pl.ds(0, ffn_rows // 2), pl.ds(ffn_rows // 2, ffn_rows // 2)]
    moves = [(j, at(), (j,)) for j in range(3)]
    moves += [(3 + k, at(), (3, slice(None), halves[k])) for k in range(2)]
    ffn_out = pack(where, (4, 2, ffn_rows, width), moves, halves_from_chips(where, ffn_sum))
    back_out, hid_out = ffn_outputs(where, ffn_out, swap(ffn_out, "dp", CORE), hidden, width)
    att_sum = shards_reduce([(att_a if k < two else att_b)[k % two] for k in range(shards)])
    att_out = stacked(where, from_chips(att_sum), att_rows)
    gq, gk, gv, go, vectors = att_outputs(
        where, att_out, swap(att_out, "dp", CORE), head_cols, width
    )
    vectors = vectors[:, :8].T
    sums = vectors[0].reshape(2, 4, 2, heads, part)

    def head_sums(g):
        return sums[g, :, 0].transpose(1, 0, 2).reshape(-1)

    return (
        outputs,
        input_grad,
        gq,
        gk,
        gv,
        head_sums(0),
        head_sums(1),
        go,
        vectors[2],
        vectors[3],
        vectors[4],
        hid_out,
        vectors[1],
        back_out,
        vectors[5],
        vectors[6],
        vectors[7],
    )


def solution(mesh):
    rows = P(("dp", "tensor"), None)
    columns, depth, vector = P(None, "tensor"), P("tensor", None), P("tensor")
    return jax.shard_map(
        local,
        mesh=mesh,
        in_specs=(
            rows,
            rows,
            P("dp"),
            columns,
            columns,
            columns,
            vector,
            vector,
            depth,
            P(),
            P(),
            P(),
            columns,
            vector,
            depth,
            P(),
            P(),
            P(),
        ),
        out_specs=(
            rows,
            rows,
            columns,
            columns,
            columns,
            vector,
            vector,
            depth,
            P(),
            P(),
            P(),
            columns,
            vector,
            depth,
            P(),
            P(),
            P(),
        ),
        check_vma=False,
    )
```

profile of v0, /device:TPU:0, one launch (start us, length us, event | category | flops | bytes accessed | tf_op | source)
XLA Modules:
  0.0 291.9 jit_solution(15921310890528239181)
XLA Ops:
  3.5 3.1 %collective-permute-start = (bf16[96,768]{1,0:T(8,128)(2,1)S(1)}, bf16[96,768]{1,0:T(8,128)(2,1)S(1)}, u32[]{:S(2)}, u32[]{:S(2)}) collective-permute-start(bf16[96,768]{1,0:T(8,128)(2,1)S(1)} %bitcast.156), channel_id=1, source_target_pairs={{0,1},{1,0},{2,3},{3,2},{4,5},{5,4},{6,7},{7,6},{8,9},{9,8},{10,11... | collective-permute-start | bytes 442376 | tf_op jit(solution)/shard_map/ppermute | solution.py:31
  12.6 7.9 %collective-permute-done.1.refs_1_.refs_3_ = bf16[96,768]{1,0:T(8,128)(2,1)S(1)} collective-permute-done((bf16[96,768]{1,0:T(8,128)(2,1)S(1)}, bf16[96,768]{1,0:T(8,128)(2,1)S(1)}, u32[]{:S(2)}, u32[]{:S(2)}) %collective-permute-start.1) | collective-permute-done | bytes 147488 | tf_op jit(solution)/shard_map/ppermute | solution.py:31
  31.2 3.9 %collective-permute-done.6.refs_6_.refs_1_.refs_0_ = bf16[112,768]{1,0:T(8,128)(2,1)S(1)} collective-permute-done((bf16[112,768]{1,0:T(8,128)(2,1)S(1)}, bf16[112,768]{1,0:T(8,128)(2,1)S(1)}, u32[]{:S(2)}, u32[]{:S(2)}) %collective-permute-start.6) | collective-permute-done | bytes 172064 | tf_op jit(solution)/shard_map/ppermute | solution.py:31
  37.4 6.9 %collective-permute-done.7.refs_7_.refs_2_.refs_1_ = bf16[112,768]{1,0:T(8,128)(2,1)S(1)} collective-permute-done((bf16[112,768]{1,0:T(8,128)(2,1)S(1)}, bf16[112,768]{1,0:T(8,128)(2,1)S(1)}, u32[]{:S(2)}, u32[]{:S(2)}) %collective-permute-start.7) | collective-permute-done | bytes 172064 | tf_op jit(solution)/shard_map/ppermute | solution.py:31
  44.4 3.3 %shard_map.308.own = bf16[4,4,2,3,16,768]{5,4,3,2,1,0:T(8,128)(2,1)} custom-call(s32[2]{0:T(128)S(1)} %pad_add_fusion.1.place_ref, bf16[3,4,16,768]{3,2,1,0:T(8,128)(2,1)S(1)} %bitcast.144, bf16[3,4,16,768]{3,2,1,0:T(8,128)(2,1)S(1)} %bitcast.146, bf16[3,2,3,16,768]{4,3,2,1,0:T(8,128)(2,1)S(1)} %bitcast.153, bf16[3,2,3,16,768]{4,3,2,1,0:T(8,128)(2,1)S(1)} %bitcast.147, ...), custom_call_target="tpu_custom_call" | custom-call | tf_op jit(solution)/shard_map/pallas_call | solution.py:50
  68.4 4.4 %collective-permute-done.14.refs_4_.refs_0_.refs_2_ = bf16[3,96,768]{2,1,0:T(8,128)(2,1)S(1)} collective-permute-done((bf16[3,96,768]{2,1,0:T(8,128)(2,1)S(1)}, bf16[3,96,768]{2,1,0:T(8,128)(2,1)S(1)}, u32[]{:S(2)}, u32[]{:S(2)}) %collective-permute-start.14) | collective-permute-done | bytes 442400 | tf_op jit(solution)/shard_map/ppermute | solution.py:31
  86.3 4.6 %shard_map.318 = bf16[4,4,96,768]{3,2,1,0:T(8,128)(2,1)} custom-call(s32[2]{0:T(128)S(1)} %pad_add_fusion.1.place_ref, bf16[4,96,768]{2,1,0:T(8,128)(2,1)S(1)} %bitcast.140, bf16[3,96,768]{2,1,0:T(8,128)(2,1)S(1)} %shard_map.312.refs_1_, bf16[3,96,768]{2,1,0:T(8,128)(2,1)S(1)} %collective-permute-done.14.refs_4_.refs_0_.refs_2_, ...), custom_call_target="tpu_custom_call" | custom-call | tf_op jit(solution)/shard_map/pallas_call | solution.py:50
  91.0 4.8 %shard_map.310 = (bf16[256,768]{1,0:T(8,128)(2,1)S(1)}, bf16[512,768]{1,0:T(8,128)(2,1)S(1)}, bf16[512,768]{1,0:T(8,128)(2,1)S(1)}, bf16[4,3,4,16,768]{4,3,2,1,0...) custom-call(s32[2]{0:T(128)S(1)} %pad_add_fusion.1.place_ref, ...), custom_call_target="tpu_custom_call" | custom-call | flops 4000000000 | bytes 10000000 | tf_op jit(solution)/shard_map/pallas_call | solution.py:171
  99.1 8.2 %shard_map.314 = (bf16[256,768]{1,0:T(8,128)(2,1)S(1)}, f32[48,256]{1,0:T(8,128)S(1)}) custom-call(s32[2]{0:T(128)S(1)} %pad_add_fusion.place_ref, bf16[256,768]{1,0:T(8,128)(2,1)S(1)} %get-tuple-element.60.refs_3_.q_ref, bf16[512,768]{1,0:T(8,128)(2,1)S(1)} %get-tuple-element.61.k_ref, bf16[512,768]{1,0:T(8,128)(2,1)S(1)} %get-tuple-element.62.v_ref, ...), custom_call_target="tpu_custom_call" | custom-call | flops 7046430720 | bytes 1572864 | tf_op jit(solution)/shard_map/pallas_call | solution.py:319
  113.3 4.2 %collective-permute-done.21.refs_4_ = bf16[3,48,768]{2,1,0:T(8,128)(2,1)S(1)} collective-permute-done((bf16[3,48,768]{2,1,0:T(8,128)(2,1)S(1)}, bf16[3,48,768]{2,1,0:T(8,128)(2,1)S(1)}, u32[]{:S(2)}, u32[]{:S(2)}) %collective-permute-start.21) | collective-permute-done | bytes 221216 | tf_op jit(solution)/shard_map/ppermute | solution.py:31
  118.5 3.9 %shard_map.323 = bf16[4,4,96,768]{3,2,1,0:T(8,128)(2,1)} custom-call(s32[2]{0:T(128)S(1)} %pad_add_fusion.1.place_ref, bf16[8,96,768]{2,1,0:T(8,128)(2,1)S(1)} %bitcast.142, bf16[3,96,768]{2,1,0:T(8,128)(2,1)S(1)} %shard_map.313._.refs_1_, bf16[3,96,768]{2,1,0:T(8,128)(2,1)S(1)} %collective-permute-done.19.refs_0_.refs_2_, ...), custom_call_target="tpu_custom_call" | custom-call | tf_op jit(solution)/shard_map/pallas_call | solution.py:50
  131.0 5.0 %shard_map.324 = (bf16[256,768]{1,0:T(8,128)(2,1)}, f32[256,768]{1,0:T(8,128)S(1)}, bf16[256,768]{1,0:T(8,128)(2,1)S(1)}, f32[3,768]{1,0:T(4,128)S(1)}) custom-call(bf16[256,1536]{1,0:T(8,128)(2,1)S(1)} %get-tuple-element.66.act_own_ref.left_own_ref, bf16[256,1536]{1,0:T(8,128)(2,1)S(1)} %get-tuple-element.67.act_other_ref.left_other_ref, ...), custom_call_target="tpu_custom_call" | custom-call | flops 3000000000 | bytes 1000000 | tf_op jit(solution)/shard_map/pallas_call | solution.py:455
  136.0 3.9 %shard_map.325 = (bf16[256,1536]{1,0:T(8,128)(2,1)S(1)}, bf16[256,1536]{1,0:T(8,128)(2,1)S(1)}, f32[1,3072]{1,0:T(1,128)S(1)}) custom-call(bf16[256,768]{1,0:T(8,128)(2,1)S(1)} %get-tuple-element.70.low_ref.right_ref, bf16[1536,768]{1,0:T(8,128)(2,1)} %bitcast.22.w_own_ref, bf16[1536,768]{1,0:T(8,128)(2,1)} %collective-permute-done.23.w_other_ref, ...), custom_call_target="tpu_custom_call" | custom-call | flops 2000000000 | bytes 1000000 | tf_op jit(solution)/shard_map/pallas_call | solution.py:455
  146.1 5.0 %shard_map.326 = (f32[256,768]{1,0:T(8,128)S(1)}, bf16[256,768]{1,0:T(8,128)(2,1)S(1)}, bf16[256,768]{1,0:T(8,128)(2,1)S(1)}, f32[3,768]{1,0:T(4,128)S(1)}) custom-call(bf16[256,1536]{1,0:T(8,128)(2,1)S(1)} %get-tuple-element.73.pre_own_ref.left_own_ref, bf16[256,1536]{1,0:T(8,128)(2,1)S(1)} %get-tuple-element.74.pre_other_ref.left_other_ref, ...), custom_call_target="tpu_custom_call" | custom-call | flops 3000000000 | bytes 1000000 | tf_op jit(solution)/shard_map/pallas_call | solution.py:455
  170.9 8.9 %shard_map.328 = (bf16[256,768]{1,0:T(8,128)(2,1)S(1)}, bf16[512,768]{1,0:T(8,128)(2,1)S(1)}, bf16[512,768]{1,0:T(8,128)(2,1)S(1)}) custom-call(s32[2]{0:T(128)S(1)} %copy-done.31, bf16[256,768]{1,0:T(8,128)(2,1)S(1)} %copy-done.16, bf16[512,768]{1,0:T(8,128)(2,1)S(1)} %copy-done.37, bf16[512,768]{1,0:T(8,128)(2,1)S(1)} %copy-done.39, ...), custom_call_target="tpu_custom_call" | custom-call | flops 9059696640 | bytes 3145728 | tf_op jit(solution)/shard_map/pallas_call | solution.py:347
  179.8 5.7 %shard_map.329 = (bf16[4,4,96,896]{3,2,1,0:T(8,128)(2,1)S(1)}, bf16[4,4,96,896]{3,2,1,0:T(8,128)(2,1)S(1)}) custom-call(s32[1]{0:T(128)} %bitcast.1.core_ref, bf16[256,768]{1,0:T(8,128)(2,1)S(1)} %get-tuple-element.85.dq_ref, bf16[512,768]{1,0:T(8,128)(2,1)S(1)} %get-tuple-element.81.dk_ref, bf16[512,768]{1,0:T(8,128)(2,1)S(1)} %get-tuple-element.83.dv_ref, ...), custom_call_target="tpu_custom_call" | custom-call | flops 6000000000 | bytes 12000000 | tf_op jit(solution)/shard_map/pallas_call | solution.py:441
  185.7 7.8 %collective-permute-done.41 = bf16[2,4,96,768]{3,2,1,0:T(8,128)(2,1)S(1)} collective-permute-done((bf16[2,4,96,768]{3,2,1,0:T(8,128)(2,1)S(1)}, bf16[2,4,96,768]{3,2,1,0:T(8,128)(2,1)S(1)}, u32[]{:S(2)}, u32[]{:S(2)}) %collective-permute-start.41) | collective-permute-done | bytes 1179680 | tf_op jit(solution)/shard_map/ppermute | solution.py:31
  199.0 11.0 %collective-permute-done.42 = bf16[4,96,768]{2,1,0:T(8,128)(2,1)S(1)} collective-permute-done((bf16[4,96,768]{2,1,0:T(8,128)(2,1)S(1)}, bf16[4,96,768]{2,1,0:T(8,128)(2,1)S(1)}, u32[]{:S(2)}, u32[]{:S(2)}) %collective-permute-start.42) | collective-permute-done | bytes 589856 | tf_op jit(solution)/shard_map/ppermute | solution.py:31
  221.0 4.3 %collective-permute-done.45 = bf16[2,96,768]{2,1,0:T(8,128)(2,1)S(1)} collective-permute-done((bf16[2,96,768]{2,1,0:T(8,128)(2,1)S(1)}, bf16[2,96,768]{2,1,0:T(8,128)(2,1)S(1)}, u32[]{:S(2)}, u32[]{:S(2)}) %collective-permute-start.45) | collective-permute-done | bytes 294944 | tf_op jit(solution)/shard_map/ppermute | solution.py:31
  225.2 12.4 %collective-permute-done.44 = bf16[2,96,768]{2,1,0:T(8,128)(2,1)S(1)} collective-permute-done((bf16[2,96,768]{2,1,0:T(8,128)(2,1)S(1)}, bf16[2,96,768]{2,1,0:T(8,128)(2,1)S(1)}, u32[]{:S(2)}, u32[]{:S(2)}) %collective-permute-start.44) | collective-permute-done | bytes 294944 | tf_op jit(solution)/shard_map/ppermute | solution.py:31
  241.3 6.5 %collective-permute-done.46.refs_0_.refs_1_ = bf16[2,96,768]{2,1,0:T(8,128)(2,1)S(1)} collective-permute-done((bf16[2,96,768]{2,1,0:T(8,128)(2,1)S(1)}, bf16[2,96,768]{2,1,0:T(8,128)(2,1)S(1)}, u32[]{:S(2)}, u32[]{:S(2)}) %collective-permute-start.46) | collective-permute-done | bytes 294944 | tf_op jit(solution)/shard_map/ppermute | solution.py:31
  255.8 3.2 %collective-permute-done.28 = bf16[2,96,896]{2,1,0:T(8,128)(2,1)S(1)} collective-permute-done((bf16[2,96,896]{2,1,0:T(8,128)(2,1)S(1)}, bf16[2,96,896]{2,1,0:T(8,128)(2,1)S(1)}, u32[]{:S(2)}, u32[]{:S(2)}) %collective-permute-start.28) | collective-permute-done | bytes 344096 | tf_op jit(solution)/shard_map/ppermute | solution.py:31
  261.1 4.5 %collective-permute-done.32 = bf16[96,896]{1,0:T(8,128)(2,1)S(1)} collective-permute-done((bf16[96,896]{1,0:T(8,128)(2,1)S(1)}, bf16[96,896]{1,0:T(8,128)(2,1)S(1)}, u32[]{:S(2)}, u32[]{:S(2)}) %collective-permute-start.32) | collective-permute-done | bytes 172064 | tf_op jit(solution)/shard_map/ppermute | solution.py:31
  280.2 3.2 %shard_map.338 = (f32[768,768]{1,0:T(8,128)}, f32[768,768]{1,0:T(8,128)}) custom-call(s32[2]{0:T(128)S(1)} %pad_add_fusion.1.place_ref, bf16[4,2,96,768]{3,2,1,0:T(8,128)(2,1)S(1)} %shard_map.337.own_ref, bf16[4,2,96,768]{3,2,1,0:T(8,128)(2,1)S(1)} %collective-permute-done.50.other_ref), custom_call_target="tpu_custom_call" | custom-call | tf_op jit(solution)/shard_map/pallas_call | solution.py:245
  (337 shorter events, 153.0 us)
Async XLA Ops:
  6.6 14.0 %collective-permute-start.1 = (bf16[96,768]{1,0:T(8,128)(2,1)S(1)}, bf16[96,768]{1,0:T(8,128)(2,1)S(1)}, u32[]{:S(2)}, u32[]{:S(2)}) collective-permute-start(bf16[96,768]{1,0:T(8,128)(2,1)S(1)} %bitcast.157), channel_id=1, source_target_pairs={{0,2},{1,3},{2,0},{3,1},{4,6},{5,7},{6,4},{7,5},{8,10},{9,11},{10,... | collective-permute-start | bytes 442376 | tf_op jit(solution)/shard_map/ppermute | solution.py:31
  22.4 21.9 %collective-permute-start.3 = (bf16[3,96,768]{2,1,0:T(8,128)(2,1)S(1)}, bf16[3,96,768]{2,1,0:T(8,128)(2,1)S(1)}, u32[]{:S(2)}, u32[]{:S(2)}) collective-permute-start(bf16[3,96,768]{2,1,0:T(8,128)(2,1)S(1)} %shard_map.306), channel_id=1, source_target_pairs={{0,8},{4,12},{8,0},{12,4},{16,24},{20,28},{24,16},{28,20},{1,9},{5... | collective-permute-start | bytes 1327112 | tf_op jit(solution)/shard_map/ppermute | solution.py:31
  23.9 20.4 %collective-permute-start.4 = (bf16[3,96,768]{2,1,0:T(8,128)(2,1)S(1)}, bf16[3,96,768]{2,1,0:T(8,128)(2,1)S(1)}, u32[]{:S(2)}, u32[]{:S(2)}) collective-permute-start(bf16[3,96,768]{2,1,0:T(8,128)(2,1)S(1)} %shard_map.306), channel_id=1, source_target_pairs={{0,16},{4,20},{8,24},{12,28},{16,0},{20,4},{24,8},{28,12},{1,17},{... | collective-permute-start | bytes 1327112 | tf_op jit(solution)/shard_map/ppermute | solution.py:31
  25.4 18.9 %collective-permute-start.5 = (bf16[3,96,768]{2,1,0:T(8,128)(2,1)S(1)}, bf16[3,96,768]{2,1,0:T(8,128)(2,1)S(1)}, u32[]{:S(2)}, u32[]{:S(2)}) collective-permute-start(bf16[3,96,768]{2,1,0:T(8,128)(2,1)S(1)} %shard_map.306), channel_id=1, source_target_pairs={{0,24},{4,28},{8,16},{12,20},{16,8},{20,12},{24,0},{28,4},{1,25},{... | collective-permute-start | bytes 1327112 | tf_op jit(solution)/shard_map/ppermute | solution.py:31
  30.1 14.2 %collective-permute-start.7 = (bf16[112,768]{1,0:T(8,128)(2,1)S(1)}, bf16[112,768]{1,0:T(8,128)(2,1)S(1)}, u32[]{:S(2)}, u32[]{:S(2)}) collective-permute-start(bf16[112,768]{1,0:T(8,128)(2,1)S(1)} %shard_map.307), channel_id=1, source_target_pairs={{0,2},{1,3},{2,0},{3,1},{4,6},{5,7},{6,4},{7,5},{8,10},{9,11},{10,... | collective-permute-start | bytes 516104 | tf_op jit(solution)/shard_map/ppermute | solution.py:31
  47.7 43.2 %collective-permute-start.9 = (bf16[4,4,2,3,16,768]{5,4,3,2,1,0:T(8,128)(2,1)}, bf16[4,4,2,3,16,768]{5,4,3,2,1,0:T(8,128)(2,1)}, u32[]{:S(2)}, u32[]{:S(2)}) collective-permute-start(bf16[4,4,2,3,16,768]{5,4,3,2,1,0:T(8,128)(2,1)} %shard_map.308.own), channel_id=1, source_target_pairs={{0,4},{4,0},{8,12},{12,8},{16,20},{20,16},{24,28},{28,24},{1,5},{5... | collective-permute-start | bytes 7077896 | tf_op jit(solution)/shard_map/ppermute | solution.py:31
  52.4 38.5 %collective-permute-start.10 = (bf16[256,768]{1,0:T(8,128)(2,1)}, bf16[256,768]{1,0:T(8,128)(2,1)}, u32[]{:S(2)}, u32[]{:S(2)}) collective-permute-start(bf16[256,768]{1,0:T(8,128)(2,1)} %shard_map.309), channel_id=1, source_target_pairs={{0,1},{1,0},{2,3},{3,2},{4,5},{5,4},{6,7},{7,6},{8,9},{9,8},{10,11... | collective-permute-start | bytes 1179656 | tf_op jit(solution)/shard_map/ppermute | solution.py:31
  62.0 13.7 %collective-permute-start.15 = (bf16[3,96,768]{2,1,0:T(8,128)(2,1)S(1)}, bf16[3,96,768]{2,1,0:T(8,128)(2,1)S(1)}, u32[]{:S(2)}, u32[]{:S(2)}) collective-permute-start(bf16[3,96,768]{2,1,0:T(8,128)(2,1)S(1)} %shard_map.312.refs_1_), channel_id=1, source_target_pairs={{0,16},{4,20},{8,24},{12,28},{16,0},{20,4},{24,8},{28,12},{1,17},{... | collective-permute-start | bytes 1327112 | tf_op jit(solution)/shard_map/ppermute | solution.py:31
  80.4 15.4 %collective-permute-start.11 = (bf16[96,768]{1,0:T(8,128)(2,1)S(1)}, bf16[96,768]{1,0:T(8,128)(2,1)S(1)}, u32[]{:S(2)}, u32[]{:S(2)}) collective-permute-start(bf16[96,768]{1,0:T(8,128)(2,1)S(1)} %shard_map.311), channel_id=1, source_target_pairs={{0,1},{1,0},{2,3},{3,2},{4,5},{5,4},{6,7},{7,6},{8,9},{9,8},{10,11... | collective-permute-start | bytes 442376 | tf_op jit(solution)/shard_map/ppermute | solution.py:31
  81.2 14.7 %collective-permute-start.12 = (bf16[96,768]{1,0:T(8,128)(2,1)S(1)}, bf16[96,768]{1,0:T(8,128)(2,1)S(1)}, u32[]{:S(2)}, u32[]{:S(2)}) collective-permute-start(bf16[96,768]{1,0:T(8,128)(2,1)S(1)} %shard_map.311), channel_id=1, source_target_pairs={{0,2},{1,3},{2,0},{3,1},{4,6},{5,7},{6,4},{7,5},{8,10},{9,11},{10,... | collective-permute-start | bytes 442376 | tf_op jit(solution)/shard_map/ppermute | solution.py:31
  90.9 37.2 %collective-permute-start.18 = (bf16[1536,768]{1,0:T(8,128)(2,1)}, bf16[1536,768]{1,0:T(8,128)(2,1)}, u32[]{:S(2)}, u32[]{:S(2)}) collective-permute-start(bf16[1536,768]{1,0:T(8,128)(2,1)} %bitcast.18.w_ref.w_own_ref), channel_id=1, source_target_pairs={{0,4},{4,0},{8,12},{12,8},{16,20},{20,16},{24,28},{28,24},{1,5},{5... | collective-permute-start | bytes 7077896 | tf_op jit(solution)/shard_map/ppermute | solution.py:31
  97.1 12.6 %collective-permute-start.19 = (bf16[3,96,768]{2,1,0:T(8,128)(2,1)S(1)}, bf16[3,96,768]{2,1,0:T(8,128)(2,1)S(1)}, u32[]{:S(2)}, u32[]{:S(2)}) collective-permute-start(bf16[3,96,768]{2,1,0:T(8,128)(2,1)S(1)} %shard_map.313._.refs_1_), channel_id=1, source_target_pairs={{0,8},{4,12},{8,0},{12,4},{16,24},{20,28},{24,16},{28,20},{1,9},{5... | collective-permute-start | bytes 1327112 | tf_op jit(solution)/shard_map/ppermute | solution.py:31
  142.4 19.5 %collective-permute-start.24 = (bf16[1536,768]{1,0:T(8,128)(2,1)}, bf16[1536,768]{1,0:T(8,128)(2,1)}, u32[]{:S(2)}, u32[]{:S(2)}) collective-permute-start(bf16[1536,768]{1,0:T(8,128)(2,1)} %get-tuple-element.80), channel_id=1, source_target_pairs={{0,4},{4,0},{8,12},{12,8},{16,20},{20,16},{24,28},{28,24},{1,5},{5... | collective-permute-start | bytes 7077896 | tf_op jit(solution)/shard_map/ppermute | solution.py:31
  146.1 20.5 %collective-permute-start.38 = (bf16[1536,768]{1,0:T(8,128)(2,1)}, bf16[1536,768]{1,0:T(8,128)(2,1)}, u32[]{:S(2)}, u32[]{:S(2)}) collective-permute-start(bf16[1536,768]{1,0:T(8,128)(2,1)} %get-tuple-element.100), channel_id=1, source_target_pairs={{0,4},{4,0},{8,12},{12,8},{16,20},{20,16},{24,28},{28,24},{1,5},{5... | collective-permute-start | bytes 7077896 | tf_op jit(solution)/shard_map/ppermute | solution.py:31
  165.0 28.4 %collective-permute-start.41 = (bf16[2,4,96,768]{3,2,1,0:T(8,128)(2,1)S(1)}, bf16[2,4,96,768]{3,2,1,0:T(8,128)(2,1)S(1)}, u32[]{:S(2)}, u32[]{:S(2)}) collective-permute-start(bf16[2,4,96,768]{3,2,1,0:T(8,128)(2,1)S(1)} %bitcast.168), channel_id=1, source_target_pairs={{0,16},{4,20},{8,24},{12,28},{16,0},{20,4},{24,8},{28,12},{1,17},{... | collective-permute-start | bytes 3538952 | tf_op jit(solution)/shard_map/ppermute | solution.py:31
  169.2 28.6 %collective-permute-start.39 = (bf16[2,4,96,768]{3,2,1,0:T(8,128)(2,1)S(1)}, bf16[2,4,96,768]{3,2,1,0:T(8,128)(2,1)S(1)}, u32[]{:S(2)}, u32[]{:S(2)}) collective-permute-start(bf16[2,4,96,768]{3,2,1,0:T(8,128)(2,1)S(1)} %slice_bitcast_fusion), channel_id=1, source_target_pairs={{0,8},{4,12},{8,0},{12,4},{16,24},{20,28},{24,16},{28,20},{1,9},{5... | collective-permute-start | bytes 3538952 | tf_op jit(solution)/shard_map/ppermute | solution.py:31
  185.6 29.2 %collective-permute-start.26 = (bf16[4,4,96,896]{3,2,1,0:T(8,128)(2,1)S(1)}, bf16[4,4,96,896]{3,2,1,0:T(8,128)(2,1)S(1)}, u32[]{:S(2)}, u32[]{:S(2)}) collective-permute-start(bf16[4,4,96,896]{3,2,1,0:T(8,128)(2,1)S(1)} %get-tuple-element.93.refs_1_), channel_id=1, source_target_pairs={{0,4},{4,0},{8,12},{12,8},{16,20},{20,16},{24,28},{28,24},{1,5},{5... | collective-permute-start | bytes 8257544 | tf_op jit(solution)/shard_map/ppermute | solution.py:31
  194.5 15.5 %collective-permute-start.42 = (bf16[4,96,768]{2,1,0:T(8,128)(2,1)S(1)}, bf16[4,96,768]{2,1,0:T(8,128)(2,1)S(1)}, u32[]{:S(2)}, u32[]{:S(2)}) collective-permute-start(bf16[4,96,768]{2,1,0:T(8,128)(2,1)S(1)} %shard_map.334), channel_id=1, source_target_pairs={{0,8},{4,12},{8,0},{12,4},{16,24},{20,28},{24,16},{28,20},{1,9},{5... | collective-permute-start | bytes 1769480 | tf_op jit(solution)/shard_map/ppermute | solution.py:31
  198.9 14.2 %collective-permute-start.40 = (bf16[4,96,768]{2,1,0:T(8,128)(2,1)S(1)}, bf16[4,96,768]{2,1,0:T(8,128)(2,1)S(1)}, u32[]{:S(2)}, u32[]{:S(2)}) collective-permute-start(bf16[4,96,768]{2,1,0:T(8,128)(2,1)S(1)} %shard_map.333), channel_id=1, source_target_pairs={{0,16},{4,20},{8,24},{12,28},{16,0},{20,4},{24,8},{28,12},{1,17},{... | collective-permute-start | bytes 1769480 | tf_op jit(solution)/shard_map/ppermute | solution.py:31
  215.7 24.6 %collective-permute-start.27 = (bf16[2,2,96,896]{3,2,1,0:T(8,128)(2,1)S(1)}, bf16[2,2,96,896]{3,2,1,0:T(8,128)(2,1)S(1)}, u32[]{:S(2)}, u32[]{:S(2)}) collective-permute-start(bf16[2,2,96,896]{3,2,1,0:T(8,128)(2,1)S(1)} %slice_bitcast_fusion.4), channel_id=1, source_target_pairs={{0,8},{4,12},{8,0},{12,4},{16,24},{20,28},{24,16},{28,20},{1,9},{5... | collective-permute-start | bytes 2064392 | tf_op jit(solution)/shard_map/ppermute | solution.py:31
  217.2 23.1 %collective-permute-start.30 = (bf16[2,2,96,896]{3,2,1,0:T(8,128)(2,1)S(1)}, bf16[2,2,96,896]{3,2,1,0:T(8,128)(2,1)S(1)}, u32[]{:S(2)}, u32[]{:S(2)}) collective-permute-start(bf16[2,2,96,896]{3,2,1,0:T(8,128)(2,1)S(1)} %slice_bitcast_fusion.2), channel_id=1, source_target_pairs={{0,16},{4,20},{8,24},{12,28},{16,0},{20,4},{24,8},{28,12},{1,17},{... | collective-permute-start | bytes 2064392 | tf_op jit(solution)/shard_map/ppermute | solution.py:31
  217.8 19.8 %collective-permute-start.44 = (bf16[2,96,768]{2,1,0:T(8,128)(2,1)S(1)}, bf16[2,96,768]{2,1,0:T(8,128)(2,1)S(1)}, u32[]{:S(2)}, u32[]{:S(2)}) collective-permute-start(bf16[2,96,768]{2,1,0:T(8,128)(2,1)S(1)} %pad_maximum_fusion.1), channel_id=1, source_target_pairs={{0,2},{1,3},{2,0},{3,1},{4,6},{5,7},{6,4},{7,5},{8,10},{9,11},{10,... | collective-permute-start | bytes 884744 | tf_op jit(solution)/shard_map/ppermute | solution.py:31
  217.9 19.7 %collective-permute-start.43 = (bf16[2,96,768]{2,1,0:T(8,128)(2,1)S(1)}, bf16[2,96,768]{2,1,0:T(8,128)(2,1)S(1)}, u32[]{:S(2)}, u32[]{:S(2)}) collective-permute-start(bf16[2,96,768]{2,1,0:T(8,128)(2,1)S(1)} %pad_maximum_fusion), channel_id=1, source_target_pairs={{0,1},{1,0},{2,3},{3,2},{4,5},{5,4},{6,7},{7,6},{8,9},{9,8},{10,11... | collective-permute-start | bytes 884744 | tf_op jit(solution)/shard_map/ppermute | solution.py:31
  261.0 19.1 %collective-permute-start.50 = (bf16[4,2,96,768]{3,2,1,0:T(8,128)(2,1)S(1)}, bf16[4,2,96,768]{3,2,1,0:T(8,128)(2,1)S(1)}, u32[]{:S(2)}, u32[]{:S(2)}) collective-permute-start(bf16[4,2,96,768]{3,2,1,0:T(8,128)(2,1)S(1)} %shard_map.337.own_ref), channel_id=1, source_target_pairs={{0,4},{4,0},{8,12},{12,8},{16,20},{20,16},{24,28},{28,24},{1,5},{5... | collective-permute-start | bytes 3538952 | tf_op jit(solution)/shard_map/ppermute | solution.py:31
  (90 other events, 712.4 us)
where the time goes:
time: 293 us; the launch traced here: 292 us
  waiting for transfers between devices  96.1 us (33%)
  Pallas kernels  85.8 us (29%)
  starting transfers between devices  58.5 us (20%)
  local copies, waits for them, and re-layouts  29.5 us (10%)
  other arithmetic  17.6 us (6%)
    ppermute x51, waiting for transfers between devices, swap(): return lax.ppermute(v, axis, [(i, i ^ bit) for i in range(count)])  96.1 us
    ppermute x51, starting transfers between devices, swap(): return lax.ppermute(v, axis, [(i, i ^ bit) for i in range(count)])  58.5 us
    pallas_call x20, Pallas kernels, pack(): pl.pallas_call(functools.partial(pack_kernel, moves, len(arrays)), in_spe...  27.9 us
    pallas_call x8, Pallas kernels, whole_call(): pl.pallas_call(kernel, in_specs=[vmem] * len(args), out_specs=[vmem] * le...  25.3 us
    unnamed x137, local copies, waits for them, and re-layouts  13.9 us
    pallas_call x1, Pallas kernels, attend_back(): pl.pallas_call(functools.partial(attend_back_kernel, half_rows=rows), gri...  8.93 us
    pallas_call x1, Pallas kernels, attend(): pl.pallas_call(functools.partial(attend_kernel, half_rows=rows), grid=(pa...  8.22 us
    convert_element_type x10, other arithmetic, add(): return (a.astype(F32) + b.astype(F32)).astype(BF16)  7.6 us
  transfers between devices with their start and end apart: 51, of which 25 were waited for; matrix products, arithmetic and copies ran while one was open for 11% of the time, Pallas kernels for 23%

commit v1 on v0

v1 whole, which is shorter than its diff:
```python
import functools

import jax
import jax.numpy as jnp
from jax import lax
from jax.experimental import pallas as pl
from jax.experimental.pallas import tpu as pltpu
from jax.sharding import PartitionSpec as P

HD = 64
LANES = 128
PLANE = 8
CORE, XBIT, YBIT = 1, 2, 4
BF16, F32 = jnp.bfloat16, jnp.float32
MIB = 1024 * 1024
FREE = pl.CostEstimate(flops=1, bytes_accessed=1, transcendentals=0)


def dot_nn(a, b):
    return lax.dot_general(a, b, (((1,), (0,)), ((), ())), preferred_element_type=F32)


def dot_nt(a, b):
    return lax.dot_general(a, b, (((1,), (1,)), ((), ())), preferred_element_type=F32)


def dot_tn(a, b):
    return lax.dot_general(a, b, (((0,), (0,)), ((), ())), preferred_element_type=F32)


def swap(v, axis, bit):
    count = lax.axis_size(axis)
    return lax.ppermute(v, axis, [(i, i ^ bit) for i in range(count)])


def pack_kernel(moves, place_ref, *refs):
    out_ref, sem = refs[-2], refs[-1]
    core, chip = place_ref[0], place_ref[1]
    copies = [
        pltpu.make_async_copy(refs[which].at[source(core, chip)], out_ref.at[target], sem.at[k])
        for k, (which, source, target) in enumerate(moves)
    ]
    for copy in copies:
        copy.start()
    for copy in copies:
        copy.wait()


def pack(where, shape, moves, arrays, earlier=(), far=0):
    vmem, space = pl.BlockSpec(memory_space=pltpu.VMEM), pl.BlockSpec(memory_space=pl.ANY)
    return pl.pallas_call(
        functools.partial(pack_kernel, moves),
        in_specs=[pl.BlockSpec(memory_space=pltpu.SMEM)]
        + [pl.BlockSpec(memory_space=pltpu.HBM)] * far
        + [space] * (len(arrays) - far + len(earlier)),
        out_specs=vmem,
        out_shape=jax.ShapeDtypeStruct(shape, BF16),
        scratch_shapes=[pltpu.SemaphoreType.DMA((len(moves),))],
        compiler_params=pltpu.CompilerParams(vmem_limit_bytes=6 * MIB),
        cost_estimate=FREE,
    )(where, *arrays, *earlier)


def nothing_kernel(*refs):
    del refs


def after(v, *earlier):
    space = pl.BlockSpec(memory_space=pl.ANY)
    return pl.pallas_call(
        nothing_kernel,
        in_specs=[space] * (1 + len(earlier)),
        out_specs=space,
        out_shape=jax.ShapeDtypeStruct(v.shape, v.dtype),
        input_output_aliases={0: 0},
    )(v, *earlier)


def fold_kernel(plan, place_ref, *refs):
    del place_ref
    outs = refs[len(refs) - sum(len(picks) for picks in plan) :]
    spot = 0
    for k, picks in enumerate(plan):
        for pick in picks:
            total = refs[2 * k][pick].astype(F32) + refs[2 * k + 1][pick].astype(F32)
            outs[spot][...] = total.astype(BF16)
            spot += 1


def fold(where, groups, earlier=()):
    vmem, space = pl.BlockSpec(memory_space=pltpu.VMEM), pl.BlockSpec(memory_space=pl.ANY)
    arrays = [v for a, b, _ in groups for v in (a, b)]
    outs = [
        jax.ShapeDtypeStruct(jax.eval_shape(lambda v, p=pick: v[p], a).shape, BF16)
        for a, _, picks in groups
        for pick in picks
    ]
    return pl.pallas_call(
        functools.partial(fold_kernel, [picks for _, _, picks in groups]),
        in_specs=[pl.BlockSpec(memory_space=pltpu.SMEM)]
        + [vmem] * len(arrays)
        + [space] * len(earlier),
        out_specs=[vmem] * len(outs),
        out_shape=outs,
        compiler_params=pltpu.CompilerParams(vmem_limit_bytes=14 * MIB),
        cost_estimate=FREE,
    )(where, *arrays, *earlier)


def sum_kernel(first_ref, a_ref, b_ref, c_ref, *refs):
    total = first_ref[...].astype(F32) + a_ref[...].astype(F32)
    total = total + b_ref[...].astype(F32) + c_ref[...].astype(F32)
    refs[-1][...] = total.astype(refs[-1].dtype)


def at(*index):
    return lambda core, chip: index


def stacked(where, arrays, rows, earlier=()):
    top = pl.ds(0, rows)
    moves = [(i, at(top), (i,)) for i in range(len(arrays))]
    return pack(where, (len(arrays), rows) + arrays[0].shape[1:], moves, arrays, earlier)


def from_shards(v):
    return [swap(v, "tensor", k) for k in range(1, lax.axis_size("tensor"))]


def halves_from_chips(where, v, between=(), sent=False):
    v_x, v_y = swap(v, "dp", XBIT), swap(v, "dp", YBIT)
    half = v.shape[1] // 2
    low, high = (slice(None), pl.ds(0, half)), (slice(None), pl.ds(half, half))
    shape = (v.shape[0], half) + v.shape[2:]
    on_y = pack(where, shape, [(0, at(*low), ())], [v_x], between)
    on_x = pack(where, shape, [(0, at(*high), ())], [v_y], between)
    got = [v, v_x, v_y, swap(on_y, "dp", YBIT), swap(on_x, "dp", XBIT)]
    return (got, [on_y, on_x]) if sent else got


def from_chips(v):
    return [v] + [swap(v, "dp", bits) for bits in (XBIT, YBIT, XBIT | YBIT)]


def shards_reduce(pieces, got, earlier=()):
    more = lax.axis_size("dp") > PLANE
    vmem, space = pl.BlockSpec(memory_space=pltpu.VMEM), pl.BlockSpec(memory_space=pl.ANY)
    total = pl.pallas_call(
        sum_kernel,
        in_specs=[vmem] * len(pieces) + [space] * len(earlier),
        out_specs=vmem,
        out_shape=jax.ShapeDtypeStruct(pieces[0].shape, F32 if more else BF16),
        compiler_params=pltpu.CompilerParams(vmem_limit_bytes=6 * MIB),
        cost_estimate=FREE,
    )(pieces[0], *got, *earlier)
    step = PLANE
    while step < lax.axis_size("dp"):
        total = total + swap(total, "dp", step)
        step *= 2
    return total.astype(BF16)


def send_pieces(pieces):
    return [swap(pieces[k], "tensor", k) for k in range(1, len(pieces))]


def relative_lanes(v, where_me, bits, block):
    width = v.shape[-1]
    spot = lax.broadcasted_iota(jnp.int32, v.shape, 1) // block
    for b in range(bits):
        shift = block << b
        right, left = pltpu.roll(v, shift, 1), pltpu.roll(v, width - shift, 1)
        flipped = jnp.where(((spot >> b) & 1) == 1, right, left)
        v = jnp.where(((where_me >> b) & 1) == 1, flipped, v)
    return v


def bias_kernel(place_ref, *refs):
    sources, (bq_ref, bv_ref, bh_ref) = refs[:4], refs[4:]
    core, chip = place_ref[0], place_ref[1]
    rows = sources[0].shape[0] - 16
    width = bq_ref.shape[1]
    group = width // 4
    hidden, heads = [], []
    for ref in sources:
        tail = ref[rows : rows + 16].astype(F32)
        hidden.append(tail[0:1] + tail[1:2])
        heads.append(tail[2:3] + tail[3:4])
    hidden = jnp.concatenate(hidden + hidden, axis=0)
    hidden = relative_lanes(hidden, core * 4 + chip, 3, hidden.shape[1] // PLANE)
    half = hidden.shape[1] // 2
    for s in range(4):
        bh_ref[0:1, s * half : (s + 1) * half] = hidden[s : s + 1, :half]
        bh_ref[1:2, s * half : (s + 1) * half] = hidden[s : s + 1, half:]
    for k, out in enumerate((bq_ref, bv_ref)):
        row = jnp.concatenate([h[:, k * group : (k + 1) * group] for h in heads], axis=1)
        row = jnp.broadcast_to(row, (8, width))
        out[...] = relative_lanes(row, chip, 2, HD // 4)[0:1]


def biases(where, sources, width, hidden):
    vmem = pl.BlockSpec(memory_space=pltpu.VMEM)
    return pl.pallas_call(
        bias_kernel,
        in_specs=[pl.BlockSpec(memory_space=pltpu.SMEM)] + [vmem] * 4,
        out_specs=[vmem] * 3,
        out_shape=[
            jax.ShapeDtypeStruct((1, width), F32),
            jax.ShapeDtypeStruct((1, width), F32),
            jax.ShapeDtypeStruct((2, 2 * hidden), F32),
        ],
        compiler_params=pltpu.CompilerParams(vmem_limit_bytes=4 * MIB),
        cost_estimate=FREE,
    )(where, *sources)


def qkv_kernel(place_ref, own, other, x_ref, xo_ref, bq_ref, bv_ref, *refs):
    outs, scratch, sem, out_sem = refs[:7], refs[7:14], refs[14], refs[15]
    (q_ref, k_ref, v_ref), weights = scratch[:3], scratch[3:]
    core = place_ref[0]
    rows, width = x_ref.shape

    def copies(src, group):
        return [
            pltpu.make_async_copy(
                src.at[j, :, m], weights[2 * group + m].at[:, :, j], sem.at[group, m, j]
            )
            for m in range(2)
            for j in range(4)
        ]

    for group in (0, 1):

        @pl.when(core == group)
        def _():
            for copy in copies(own, group):
                copy.start()

        @pl.when(core != group)
        def _():
            for copy in copies(other, group):
                copy.start()

    def landed(group):
        @pl.when(core == group)
        def _():
            for copy in copies(own, group):
                copy.wait()

        @pl.when(core != group)
        def _():
            for copy in copies(other, group):
                copy.wait()

    leaving = [pltpu.make_async_copy(scratch[k], outs[k], out_sem.at[k]) for k in range(7)]
    landed(0)
    leaving[3].start()
    leaving[4].start()
    x, xo = x_ref[...], xo_ref[...]
    q_ref[...] = (dot_nt(x, weights[0][...].reshape(width, width)) + bq_ref[...]).astype(BF16)
    leaving[0].start()
    w = weights[1][...].reshape(width, width)
    k_ref[:rows] = dot_nt(x, w).astype(BF16)
    k_ref[rows:] = dot_nt(xo, w).astype(BF16)
    leaving[1].start()
    landed(1)
    leaving[5].start()
    leaving[6].start()
    w = weights[2][...].reshape(width, width)
    v_ref[:rows] = (dot_nt(x, w) + bv_ref[...]).astype(BF16)
    v_ref[rows:] = (dot_nt(xo, w) + bv_ref[...]).astype(BF16)
    leaving[2].start()
    for copy in leaving:
        copy.wait()


def project(where, own, other, x, xo, bq, bv):
    rows, width = x.shape
    _, shards, _, heads, part, _ = own.shape
    vmem, hbm = pl.BlockSpec(memory_space=pltpu.VMEM), pl.BlockSpec(memory_space=pltpu.HBM)
    space = pl.BlockSpec(memory_space=pl.ANY)
    shapes = [(rows, width), (2 * rows, width), (2 * rows, width)]
    shapes += [(shards, heads, 4, part, width)] * 4
    return pl.pallas_call(
        qkv_kernel,
        in_specs=[pl.BlockSpec(memory_space=pltpu.SMEM), space, space] + [vmem] * 4,
        out_specs=[hbm] * 7,
        out_shape=[jax.ShapeDtypeStruct(shape, BF16) for shape in shapes],
        scratch_shapes=[pltpu.VMEM(shape, BF16) for shape in shapes]
        + [pltpu.SemaphoreType.DMA((2, 2, 4)), pltpu.SemaphoreType.DMA((7,))],
        compiler_params=pltpu.CompilerParams(vmem_limit_bytes=18 * MIB),
        cost_estimate=FREE,
    )(where, own, other, x, xo, bq, bv)


def att_out_kernel(place_ref, own_ref, other_ref, gq_ref, gk_ref, gv_ref, go_ref, *sums):
    core, chip = place_ref[0], place_ref[1]
    head_cols, width = go_ref.shape
    heads, part = head_cols // HD, HD // 4
    extras = []
    for group in (0, 1):
        blocks = []
        for c in range(4):
            block = jnp.where(core == group, own_ref[c ^ chip], other_ref[c ^ chip])
            extras.append(block[:, width:])
            blocks.append(block)
        for m in range(2):
            pieces = [
                blocks[c][(m * heads + h) * part : (m * heads + h + 1) * part]
                for h in range(heads)
                for c in range(4)
            ]
            whole = jnp.concatenate(pieces, axis=0)
            (gq_ref, gk_ref, gv_ref, go_ref)[2 * group + m][...] = whole[:, :width].astype(F32)
            if m == 0:
                sums[group][...] = whole[:, width:].astype(F32).T[0]
    extras = jnp.concatenate(extras, axis=0).astype(F32).T
    for k in range(1, 8):
        sums[1 + k][...] = extras[k]


def att_outputs(where, own, other, head_cols, width):
    vmem = pl.BlockSpec(memory_space=pltpu.VMEM)
    weight = jax.ShapeDtypeStruct((head_cols, width), F32)
    vector = jax.ShapeDtypeStruct((width,), F32)
    few = jax.ShapeDtypeStruct((head_cols,), F32)
    return pl.pallas_call(
        att_out_kernel,
        in_specs=[pl.BlockSpec(memory_space=pltpu.SMEM), vmem, vmem],
        out_specs=[vmem] * 13,
        out_shape=[weight] * 4 + [few] * 2 + [vector] * 7,
        compiler_params=pltpu.CompilerParams(vmem_limit_bytes=14 * MIB),
    )(where, own, other)


def ffn_out_kernel(place_ref, own_ref, other_ref, back_ref, hid_ref):
    core, chip = place_ref[0], place_ref[1]
    rows = own_ref.shape[2]
    blocks = []
    for group in (0, 1):
        for c in range(4):
            block = jnp.where(core == group, own_ref[c ^ chip], other_ref[c ^ chip])
            spot = (group * 4 + c) * rows
            back_ref[spot : spot + rows] = block[0].astype(F32)
            blocks.append(block[1])
    hid_ref[...] = jnp.concatenate(blocks, axis=0).astype(F32).T


def ffn_outputs(where, own, other, hidden, width):
    vmem = pl.BlockSpec(memory_space=pltpu.VMEM)
    return pl.pallas_call(
        ffn_out_kernel,
        in_specs=[pl.BlockSpec(memory_space=pltpu.SMEM), vmem, vmem],
        out_specs=[vmem] * 2,
        out_shape=[
            jax.ShapeDtypeStruct((hidden, width), F32),
            jax.ShapeDtypeStruct((width, hidden), F32),
        ],
        compiler_params=pltpu.CompilerParams(vmem_limit_bytes=20 * MIB),
    )(where, own, other)


def live_keys(place_ref, keys, half_rows):
    spot = lax.broadcasted_iota(jnp.int32, (keys, 1), 0)
    first = place_ref[1]
    spot = jnp.where(spot < half_rows, spot + first, spot - first)
    return spot < place_ref[0]


def attend_kernel(place_ref, q_ref, k_ref, v_ref, *refs, half_rows):
    out_ref, lse_ref = refs[-2:]
    rows, keys = q_ref.shape[0], k_ref.shape[0]
    q = q_ref[...] * jnp.asarray(0.125, BF16)
    k = k_ref[...]
    v_turned = v_ref[...].T
    live = live_keys(place_ref, keys, half_rows)
    lane = lax.broadcasted_iota(jnp.int32, (rows, LANES), 1)
    outs, sums = [], []
    for h in range(LANES // HD):
        qh = jnp.where((lane // HD) == h, q, jnp.zeros_like(q))
        s = jnp.where(live, dot_nt(k, qh), -1e30)
        top = jnp.max(s, axis=0, keepdims=True)
        e = jnp.exp(s - top)
        total = jnp.sum(e, axis=0, keepdims=True)
        p = (e * (1.0 / total)).astype(BF16)
        outs.append(dot_nn(v_turned, p)[h * HD : (h + 1) * HD])
        sums.append(top + jnp.log(total))
    out_ref[...] = jnp.concatenate(outs, axis=0).T.astype(BF16)
    lse_ref[...] = jnp.concatenate(sums + [jnp.zeros((6, rows), F32)], axis=0)


def attend_back_kernel(
    place_ref, q_ref, k_ref, v_ref, lse_ref, do_ref, _, dq_ref, dk_ref, dv_ref, *, half_rows
):
    rows, keys = q_ref.shape[0], k_ref.shape[0]
    k, v, do = k_ref[...], v_ref[...], do_ref[...]
    q = q_ref[...] * jnp.asarray(0.125, BF16)
    k_turned = k.T
    live = live_keys(place_ref, keys, half_rows)
    lane = lax.broadcasted_iota(jnp.int32, (rows, LANES), 1)
    dqs, dks, dvs = [], [], []
    for h in range(LANES // HD):
        mine = (lane // HD) == h
        qh = jnp.where(mine, q, jnp.zeros_like(q))
        doh = jnp.where(mine, do, jnp.zeros_like(do))
        s = jnp.where(live, dot_nt(k, qh), -1e30)
        p = jnp.exp(s - lse_ref[h : h + 1, :])
        dp = dot_nt(v, doh)
        inner = jnp.sum(p * dp, axis=0, keepdims=True)
        ds = (p * (dp - inner)).astype(BF16)
        dqs.append(dot_nn(k_turned, ds)[h * HD : (h + 1) * HD])
        dks.append(dot_nn(ds, qh))
        dvs.append(dot_nn(p.astype(BF16), doh))
    dq_ref[...] = (jnp.concatenate(dqs, axis=0).T * 0.125).astype(BF16)
    dk_ref[...] = (dks[0] + dks[1]).astype(BF16)
    dv_ref[...] = (dvs[0] + dvs[1]).astype(BF16)


def attend(place, q, k, v, first, pairs, earlier):
    rows, width = q.shape[0], pairs * LANES
    keys = k.shape[0]
    q_spec = pl.BlockSpec((rows, LANES), lambda i: (0, i + first))
    k_spec = pl.BlockSpec((keys, LANES), lambda i: (0, i + first))
    out_spec = pl.BlockSpec((rows, LANES), lambda i: (0, i))
    lse_spec = pl.BlockSpec((8, rows), lambda i: (i, 0))
    return pl.pallas_call(
        functools.partial(attend_kernel, half_rows=rows),
        grid=(pairs,),
        in_specs=[
            pl.BlockSpec(memory_space=pltpu.SMEM),
            q_spec,
            k_spec,
            k_spec,
        ]
        + [pl.BlockSpec(memory_space=pl.ANY)] * len(earlier),
        out_specs=[out_spec, lse_spec],
        out_shape=[
            jax.ShapeDtypeStruct((rows, width), BF16),
            jax.ShapeDtypeStruct((8 * pairs, rows), F32),
        ],
        compiler_params=pltpu.CompilerParams(vmem_limit_bytes=10 * MIB),
        cost_estimate=FREE,
    )(place, q, k, v, *earlier)


def attend_back(place, q, k, v, lse, do, earlier):
    rows, width = q.shape
    keys = k.shape[0]
    q_spec = pl.BlockSpec((rows, LANES), lambda i: (0, i))
    k_spec = pl.BlockSpec((keys, LANES), lambda i: (0, i))
    lse_spec = pl.BlockSpec((8, rows), lambda i: (i, 0))
    return pl.pallas_call(
        functools.partial(attend_back_kernel, half_rows=rows),
        grid=(width // LANES,),
        in_specs=[
            pl.BlockSpec(memory_space=pltpu.SMEM),
            q_spec,
            k_spec,
            k_spec,
            lse_spec,
            q_spec,
            pl.BlockSpec(memory_space=pl.ANY),
        ],
        out_specs=[q_spec, k_spec, k_spec],
        out_shape=[
            jax.ShapeDtypeStruct((rows, width), BF16),
            jax.ShapeDtypeStruct((keys, width), BF16),
            jax.ShapeDtypeStruct((keys, width), BF16),
        ],
        compiler_params=pltpu.CompilerParams(vmem_limit_bytes=10 * MIB),
        cost_estimate=FREE,
    )(place, q, k, v, lse, do, earlier)


def weights_kernel(
    place_ref,
    dq_ref,
    dk_ref,
    dv_ref,
    context_ref,
    context_two_ref,
    ga_ref,
    x_ref,
    xo_ref,
    one_ref,
    two_ref,
    hid_ref,
    _,
    keep_ref,
    send_ref,
):
    rows, width = dq_ref.shape
    shards = keep_ref.shape[1]
    group = width // shards
    heads = group // HD
    part = HD // 4
    core, chip = place_ref[0], place_ref[1]
    span = 2 * group
    lane = lax.broadcasted_iota(jnp.int32, (part, LANES), 1)
    spots = lax.broadcasted_iota(jnp.int32, (8, LANES), 0)
    spots = (spots == lax.broadcasted_iota(jnp.int32, (8, LANES), 1)).astype(BF16)
    att_rows = keep_ref.shape[2]
    half = 4 * att_rows
    whole = jnp.concatenate([jnp.zeros((2, width), F32), one_ref[...], two_ref[...]], axis=0)
    whole = relative_lanes(whole, core * 4 + chip, 3, att_rows)
    line = lax.broadcasted_iota(jnp.int32, (8, half), 0)
    extra = []
    for g in range(2):
        extra.append([])
        for s in range(shards):
            mine = hid_ref[g : g + 1, s * half : (s + 1) * half]
            mine = jnp.where(line == 1, mine, whole[:, g * half : (g + 1) * half])
            extra[g].append(dot_tn(mine.astype(BF16), spots))

    def put(which, m, left_ref, rights, with_sum):
        ones = jnp.ones((rows, LANES), BF16)
        for first in range(0, width, span):
            out, sums = None, None
            for k, right in enumerate(rights):
                if isinstance(left_ref, tuple):
                    left = left_ref[first // span][...]
                else:
                    left = left_ref[k * rows : (k + 1) * rows, first : first + span]
                more = dot_tn(left, right[...])
                out = more if out is None else out + more
                if with_sum:
                    more = dot_tn(left, ones)
                    sums = more if sums is None else sums + more

            def store(dst, base):
                for at in range(0, span, part):
                    row = first + at
                    shard, rest = row // group, row % group
                    head, j = rest // HD, (rest % HD) // part
                    spot = (m * heads + head) * part
                    dst[j, shard, spot : spot + part, :width] = out[at : at + part].astype(BF16)
                    tail = extra[base][shard][j * att_rows + spot : j * att_rows + spot + part]
                    if with_sum:
                        tail = jnp.where(lane == 0, sums[at : at + part], tail)
                    dst[j, shard, spot : spot + part, width:] = tail.astype(BF16)

            @pl.when(core == which)
            def _():
                store(keep_ref, 0)

            @pl.when(core != which)
            def _():
                store(send_ref, 1)

    put(0, 0, dq_ref, [x_ref], True)
    put(0, 1, dk_ref, [x_ref, xo_ref], False)
    put(1, 0, dv_ref, [x_ref, xo_ref], True)
    put(1, 1, (context_ref, context_two_ref), [ga_ref], False)


def attention_weight_grads(where, dq, dk, dv, contexts, ga, x, xo, sums, shards, earlier):
    width = dq.shape[1]
    full = jax.ShapeDtypeStruct((4, shards, width // (2 * shards), width + LANES), BF16)
    vmem = pl.BlockSpec(memory_space=pltpu.VMEM)
    return pl.pallas_call(
        weights_kernel,
        in_specs=[pl.BlockSpec(memory_space=pltpu.SMEM)] + [vmem] * 11 + [pl.BlockSpec(memory_space=pl.ANY)],
        out_specs=[vmem, vmem],
        out_shape=[full, full],
        compiler_params=pltpu.CompilerParams(vmem_limit_bytes=22 * MIB),
        cost_estimate=FREE,
    )(where, dq, dk, dv, *contexts, ga, x, xo, *sums, earlier)


def whole_call(kernel, outs, args, flops, earlier=()):
    vmem, space = pl.BlockSpec(memory_space=pltpu.VMEM), pl.BlockSpec(memory_space=pl.ANY)
    if earlier:
        inner, count = kernel, len(args)
        kernel = lambda *refs: inner(*refs[:count], *refs[count + len(earlier) :])
    return pl.pallas_call(
        kernel,
        in_specs=[vmem] * len(args) + [space] * len(earlier),
        out_specs=[vmem] * len(outs),
        out_shape=[jax.ShapeDtypeStruct(shape, dtype) for shape, dtype in outs],
        compiler_params=pltpu.CompilerParams(vmem_limit_bytes=22 * MIB),
        cost_estimate=FREE,
    )(*args, *earlier)


def normalize(z):
    center = z - jnp.mean(z, axis=-1, keepdims=True)
    spread = jnp.mean(center * center, axis=-1, keepdims=True)
    scale = lax.rsqrt(spread + 1e-05)
    return center * scale, scale


def norm_back(grad, zhat, scale, gain):
    e = grad * gain
    inner = jnp.mean(e * zhat, axis=-1, keepdims=True)
    return (e - jnp.mean(e, axis=-1, keepdims=True) - zhat * inner) * scale


def column_sums(v):
    return jnp.sum(v, axis=0, keepdims=True)


def mid_kernel(
    context_ref,
    context_two_ref,
    wo_ref,
    x_ref,
    b_ref,
    gain_ref,
    shift_ref,
    mid_ref,
    zhat_ref,
    scale_ref,
):
    half = context_ref.shape[1]
    z = dot_nn(context_ref[...], wo_ref[:half]) + dot_nn(context_two_ref[...], wo_ref[half:])
    z = z + b_ref[...] + x_ref[...].astype(F32)
    zhat, scale = normalize(z)
    mid_ref[...] = (zhat * gain_ref[...] + shift_ref[...]).astype(BF16)
    zhat_ref[...] = zhat
    scale_ref[...] = jnp.broadcast_to(scale, scale_ref.shape)


def hidden_kernel(mid_ref, w_ref, b_ref, act_ref, slope_ref):
    block = 512
    for first in range(0, w_ref.shape[0], block):
        cols = slice(first, first + block)
        act, slope = gelu_pair(dot_nt(mid_ref[...], w_ref[cols]) + b_ref[:, cols])
        act_ref[:, cols] = act.astype(BF16)
        slope_ref[:, cols] = slope.astype(BF16)


def branch_kernel(
    act_own_ref,
    act_other_ref,
    w_own_ref,
    w_other_ref,
    mid_ref,
    b_ref,
    gain_ref,
    shift_ref,
    cotangent_ref,
    out_ref,
    grad_ref,
    low_ref,
    sums_ref,
):
    z = dot_nn(act_own_ref[...], w_own_ref[...]) + dot_nn(act_other_ref[...], w_other_ref[...])
    zhat, scale = normalize(z + b_ref[...] + mid_ref[...].astype(F32))
    out_ref[...] = (zhat * gain_ref[...] + shift_ref[...]).astype(BF16)
    c = cotangent_ref[...].astype(F32)
    grad = norm_back(c, zhat, scale, gain_ref[...])
    low = grad.astype(BF16)
    grad_ref[...] = grad
    low_ref[...] = low
    sums_ref[...] = jnp.concatenate(
        [column_sums(low.astype(F32)), column_sums(c * zhat), column_sums(c)], axis=0
    )


def pair_grads_kernel(left_own_ref, left_other_ref, right_ref, keep_ref, send_ref):
    send_ref[...] = dot_tn(left_other_ref[...], right_ref[...]).astype(BF16)
    keep_ref[...] = dot_tn(left_own_ref[...], right_ref[...]).astype(BF16)


def input_kernel(
    dq_ref, dk_ref, dv_ref, wq_ref, wk_ref, wv_ref, first_ref, own_ref, other_ref
):
    rows = dq_ref.shape[0]
    total = dot_nn(dk_ref[rows:], wk_ref[...]) + dot_nn(dv_ref[rows:], wv_ref[...])
    other_ref[...] = total.astype(BF16)
    total = dot_nn(dk_ref[:rows], wk_ref[...]) + dot_nn(dv_ref[:rows], wv_ref[...])
    own_ref[...] = total + dot_nn(dq_ref[...], wq_ref[...]) + first_ref[...]


def pre_kernel(
    low_ref, w_own_ref, w_other_ref, slope_own_ref, slope_other_ref, own_ref, other_ref, sums_ref
):
    for k, (w, slope, out) in enumerate(
        ((w_own_ref, slope_own_ref, own_ref), (w_other_ref, slope_other_ref, other_ref))
    ):
        grad = (dot_nt(low_ref[...], w[...]) * slope[...].astype(F32)).astype(BF16)
        out[...] = grad
        sums_ref[k : k + 1] = column_sums(grad.astype(F32))


def first_kernel(
    pre_own_ref,
    pre_other_ref,
    w_own_ref,
    w_other_ref,
    grad_ref,
    zhat_ref,
    scale_ref,
    gain_ref,
    wo_ref,
    first_ref,
    low_ref,
    context_ref,
    sums_ref,
):
    grad = dot_nn(pre_own_ref[...], w_own_ref[...]) + dot_nn(pre_other_ref[...], w_other_ref[...])
    grad = grad + grad_ref[...]
    zhat = zhat_ref[...]
    first = norm_back(grad, zhat, scale_ref[:, :1], gain_ref[...])
    low = first.astype(BF16)
    first_ref[...] = first
    low_ref[...] = low
    context_ref[...] = dot_nt(low, wo_ref[...]).astype(BF16)
    sums_ref[...] = jnp.concatenate(
        [column_sums(low.astype(F32)), column_sums(grad * zhat), column_sums(grad)], axis=0
    )


def gelu_pair(v):
    cdf = 0.5 * (1.0 + lax.erf(v * (0.5**0.5)))
    density = jnp.exp(-0.5 * v * v) * 0.3989422804014327
    return v * cdf, cdf + v * density


def local(
    inputs,
    cotangent,
    lengths,
    w_query,
    w_key,
    w_value,
    b_query,
    b_value,
    w_output,
    b_output,
    gain_one,
    shift_one,
    w_hidden,
    b_hidden,
    w_back,
    b_back,
    gain_two,
    shift_two,
):
    rows, width = inputs.shape
    shards = lax.axis_size("tensor")
    head_cols = w_query.shape[1]
    hidden = w_hidden.shape[1]
    heads = head_cols // HD
    part = HD // 4
    ffn_rows = hidden // PLANE
    per_slot = shards // lengths.shape[0]
    assert per_slot == 2 and shards == 4 and lax.axis_size("dp") % PLANE == 0
    dp = lax.axis_index("dp")
    core = dp & 1
    chip = (((dp >> 2) & 1) << 1) | ((dp >> 1) & 1)
    me = core * 4 + chip
    t = lax.axis_index("tensor")

    where = jnp.stack([core, chip]).astype(jnp.int32)
    att_rows = 2 * heads * part
    far = pl.ds(1, shards - 1)

    by_head = (heads, 4, part, width)
    pair = [
        jnp.where(core == 0, w_query, w_value).T.reshape(by_head),
        jnp.where(core == 0, w_key.T, w_output).reshape(by_head),
    ]
    hid_near = lax.dynamic_slice_in_dim(w_hidden, core * (hidden // 2), hidden // 2, 1)
    hid_near = hid_near.T.reshape(4, ffn_rows, width)
    back_near = w_back.reshape(PLANE, ffn_rows, width)
    bias = jnp.pad(jnp.concatenate([b_query, b_value]), (0, width - 2 * head_cols))
    bias = jnp.stack([b_hidden, b_hidden, bias, bias])
    bias_high = lax.reduce_precision(bias, 8, 7)
    bias_rows = jnp.where(jnp.arange(4)[:, None] % 2 == 0, bias_high, bias - bias_high)
    bias_rows = jnp.pad(bias_rows.astype(BF16), ((0, 12), (0, 0)))

    def near_heads(j):
        return lambda core, chip: (slice(None), chip ^ j)

    def near_hid(j):
        return lambda core, chip: (chip ^ j,)

    def near_back(j):
        return lambda core, chip: (core * 4 + (chip ^ j),)

    att_send = pack(
        where, (2, heads, part, width), [(0, near_heads(0), (0,)), (1, near_heads(0), (1,))], pair, (), 2
    )
    att_z = from_shards(att_send.reshape(att_rows, width))
    packed = pack(
        where,
        (ffn_rows + 16, width),
        [(0, near_hid(0), (pl.ds(0, ffn_rows),)), (1, at(), (pl.ds(ffn_rows, 16),))],
        [hid_near, bias_rows],
        (),
        1,
    )
    back_send = pack(where, (ffn_rows, width), [(0, near_back(0), ())], [back_near], (), 1)
    rows_send = pack(where, inputs.shape, [(0, at(), ())], [inputs], (), 1)
    att_stack = stacked(where, att_z, att_rows, (packed, back_send, rows_send))
    hid_z = from_shards(after(packed, att_stack))
    rows_other = swap(after(rows_send, *hid_z), "tensor", 1)

    hid_stack = stacked(where, hid_z, ffn_rows)
    att_far = halves_from_chips(where, att_stack, hid_z[:1])
    shape = (4, shards, 2, heads, part, width)
    moves = [(m, near_heads(j), (j, 0, m)) for j in range(4) for m in range(2)]
    moves += [(2 + j, at(), (j, far)) for j in range(3)]
    moves += [(5 + m, at(), (3, far, m)) for m in range(2)]
    att_far = [v.reshape(shards - 1, -1, heads, part, width) for v in att_far[:3]] + [
        v.reshape(shards - 1, heads, part, width) for v in att_far[3:]
    ]
    att_own = pack(where, shape, moves, pair + att_far, (rows_other,), 2)
    att_swap = swap(att_own, "dp", CORE)

    def ffn_half(near, near_index, far_slices, earlier):
        halves = [pl.ds(0, ffn_rows // 2), pl.ds(ffn_rows // 2, ffn_rows // 2)]
        moves = [(0, near_index(j), (0, j)) for j in range(4)]
        moves += [(1 + j, at(), (far, j)) for j in range(3)]
        moves += [(4 + k, at(), (far, 3, halves[k])) for k in range(2)]
        own = pack(where, (shards, 4, ffn_rows, width), moves, [near] + far_slices, earlier, 1)
        own = own.reshape(-1, width)
        return own, swap(own, "dp", CORE)

    bq, bv, bh = biases(where, [packed] + hid_z, width, hidden)

    queries, key_rows, values, wq, wk, wv, wo = project(
        where, att_own, att_swap, inputs, rows_other, bq, bv
    )
    wq, wk, wv, wo = (w.reshape(shards * head_cols, width) for w in (wq, wk, wv, wo))
    place = jnp.stack([lengths[t // per_slot], (t % per_slot) * rows]).astype(jnp.int32)
    back_z = from_shards(after(back_send, rows_other, att_swap))
    hid_far, hid_sent = halves_from_chips(where, after(hid_stack, *att_far[3:]), [queries], True)
    pairs = width // LANES // 2
    context_one, logsum_one = attend(place, queries, key_rows, values, 0, pairs, hid_sent)
    back_stack = stacked(where, back_z, ffn_rows, [context_one])
    hid_own, hid_swap = ffn_half(hid_near, near_hid, hid_far, [back_stack])
    context_two, logsum_two = attend(place, queries, key_rows, values, pairs, pairs, [hid_own])
    logsum = jnp.concatenate([logsum_one, logsum_two], axis=0)
    contexts = (context_one, context_two)
    full, low = ((rows, width), F32), ((rows, width), BF16)
    half_low = ((rows, 2 * hidden), BF16)
    three = ((3, width), F32)
    mid, zhat_one, scale_one = whole_call(
        mid_kernel,
        [low, full, ((rows, LANES), F32)],
        (*contexts, wo, inputs, b_output[None], gain_one[None], shift_one[None]),
        2 * 10**8,
    )
    act_own, slope_own = whole_call(
        hidden_kernel, [half_low, half_low], (mid, hid_own, bh[:1]), 10**9
    )
    back_far = halves_from_chips(where, back_stack, [act_own])
    back_own, back_swap = ffn_half(back_near, near_back, back_far, ())
    act_swap, slope_swap = whole_call(
        hidden_kernel, [half_low, half_low], (mid, hid_swap, bh[1:]), 10**9
    )
    outputs, grad_second, grad_branch, sums_two = whole_call(
        branch_kernel,
        [low, full, low, three],
        (
            act_own,
            act_swap,
            back_own,
            back_swap,
            mid,
            b_back[None],
            gain_two[None],
            shift_two[None],
            cotangent,
        ),
        3 * 10**9,
    )

    two = shards // 2
    every = slice(None)
    low_half, high_half = pl.ds(0, two), pl.ds(two, shards - two)
    each = [(k,) for k in range(shards)]

    def first_step(keep, got, picks, earlier):
        a_keep, a_send, b_keep, b_send = fold(where, [(keep, got, picks)], earlier)
        return a_keep, b_keep, swap(a_send, "dp", XBIT), swap(b_send, "dp", YBIT), a_send

    def second_step(step, a_picks, b_picks, earlier):
        a_keep, b_keep, a_got, b_got, _ = step
        a_keep, a_send, b_keep, b_send = fold(
            where, [(a_keep, a_got, a_picks), (b_keep, b_got, b_picks)], earlier
        )
        return a_keep, b_keep, swap(a_send, "dp", YBIT), swap(b_send, "dp", XBIT), a_send

    def third_step(step, earlier):
        a_keep, b_keep, a_got, b_got, _ = step
        return fold(
            where, [(a_keep, a_got, each[:two]), (b_keep, b_got, each[: shards - two])], earlier
        )

    quarter = (shards, 2, 2, ffn_rows, width)
    ffn_picks = [
        (low_half, every, 0),
        (low_half, every, 1),
        (high_half, 0),
        (high_half, 1),
    ]
    ffn_again = [(every, 0), (every, 1)]
    pair_out = [((2 * hidden, width), BF16)] * 2
    back_keep, back_send = whole_call(
        pair_grads_kernel, pair_out, (act_own, act_swap, grad_branch), 10**9
    )
    back_got = swap(back_send, "dp", CORE)
    pre_own, pre_swap, grad_b_hidden = whole_call(
        pre_kernel,
        [half_low, half_low, ((2, 2 * hidden), F32)],
        (grad_branch, back_own, back_swap, slope_own, slope_swap),
        10**9,
    )
    back_step = first_step(back_keep.reshape(quarter), back_got.reshape(quarter), ffn_picks, ())
    hid_keep, hid_send = whole_call(
        pair_grads_kernel, pair_out, (pre_own, pre_swap, mid), 3 * 10**8, (back_step[4],)
    )
    hid_got = swap(hid_send, "dp", CORE)
    grad_first, grad_attn, grad_context, sums_one = whole_call(
        first_kernel,
        [full, low, low, three],
        (
            pre_own,
            pre_swap,
            hid_own,
            hid_swap,
            grad_second,
            zhat_one,
            scale_one,
            gain_one[None],
            wo,
        ),
        3 * 10**8,
        (hid_send,),
    )
    hid_step = first_step(
        hid_keep.reshape(quarter), hid_got.reshape(quarter), ffn_picks, (grad_first,)
    )
    grad_queries, grad_keys, grad_values = attend_back(
        place, queries, key_rows, values, logsum, grad_context, hid_step[4]
    )
    total, returned_send = whole_call(
        input_kernel,
        [full, low],
        (grad_queries, grad_keys, grad_values, wq, wk, wv, grad_first),
        3 * 10**8,
    )
    returned = swap(returned_send, "tensor", 1)
    back_step = second_step(back_step, ffn_again, ffn_again, (returned_send,))

    att_keep, att_send = attention_weight_grads(
        where,
        grad_queries,
        grad_keys,
        grad_values,
        contexts,
        grad_attn,
        inputs,
        rows_other,
        (sums_one, sums_two, grad_b_hidden),
        shards,
        back_step[4],
    )
    wide = att_keep.shape[-1]

    back_pieces = third_step(back_step, (att_keep, returned))
    back_got = send_pieces(back_pieces)
    hid_step = second_step(hid_step, ffn_again, ffn_again, (back_pieces[0],))
    att_got = swap(after(att_send, hid_step[4]), "dp", CORE)
    att_shape = (2, 2) + att_keep.shape[1:]
    att_picks = [
        (every, 0, low_half),
        (every, 1, low_half),
        (0, every, high_half),
        (1, every, high_half),
    ]
    att_step = first_step(att_keep.reshape(att_shape), att_got.reshape(att_shape), att_picks, ())
    hid_pieces = third_step(hid_step, ())
    back_sum = shards_reduce(back_pieces, back_got)
    hid_got = send_pieces(hid_pieces)
    att_step = second_step(att_step, [(0,), (1,)], [(0,), (1,)], (back_sum,))
    hid_sum = shards_reduce(hid_pieces, hid_got)
    att_pieces = third_step(att_step, (hid_sum,))
    att_got = send_pieces(att_pieces)
    input_grad = (total + returned.astype(F32)).astype(BF16)
    top = pl.ds(0, ffn_rows)
    ffn_sum = pack(
        where,
        (2, ffn_rows, width),
        [(0, at(top), (0,)), (1, at(top), (1,))],
        [back_sum, hid_sum],
        att_got[:1],
    )
    halves = [pl.ds(0, ffn_rows // 2), pl.ds(ffn_rows // 2, ffn_rows // 2)]
    moves = [(j, at(), (j,)) for j in range(3)]
    moves += [(3 + k, at(), (3, slice(None), halves[k])) for k in range(2)]
    att_sum = shards_reduce(att_pieces, att_got)
    ffn_far = halves_from_chips(where, ffn_sum, [att_sum])
    ffn_out = pack(where, (4, 2, ffn_rows, width), moves, ffn_far)
    back_out, hid_out = ffn_outputs(where, ffn_out, swap(ffn_out, "dp", CORE), hidden, width)
    att_out = stacked(where, from_chips(att_sum), att_rows, (back_out,))
    gq, gk, gv, go, sum_q, sum_v, sum_hid, *vectors = att_outputs(
        where, att_out, swap(att_out, "dp", CORE), head_cols, width
    )
    return (
        outputs,
        input_grad,
        gq.T,
        gk.T,
        gv.T,
        sum_q,
        sum_v,
        go,
        vectors[0],
        vectors[1],
        vectors[2],
        hid_out,
        sum_hid,
        back_out,
        vectors[3],
        vectors[4],
        vectors[5],
    )


def solution(mesh):
    rows = P(("dp", "tensor"), None)
    columns, depth, vector = P(None, "tensor"), P("tensor", None), P("tensor")
    return jax.shard_map(
        local,
        mesh=mesh,
        in_specs=(
            rows,
            rows,
            P("dp"),
            columns,
            columns,
            columns,
            vector,
            vector,
            depth,
            P(),
            P(),
            P(),
            columns,
            vector,
            depth,
            P(),
            P(),
            P(),
        ),
        out_specs=(
            rows,
            rows,
            columns,
            columns,
            columns,
            vector,
            vector,
            depth,
            P(),
            P(),
            P(),
            columns,
            vector,
            depth,
            P(),
            P(),
            P(),
        ),
        check_vma=False,
    )
```

time: 293 us -> 266 us (0.908)
  other arithmetic: 17.6 us -> 4.04 us
  local copies, waits for them, and re-layouts: 29.5 us -> 17 us
  starting transfers between devices: 58.5 us -> 63.9 us
  Pallas kernels: 85.8 us -> 82.4 us
    convert_element_type x13 -> x2, other arithmetic: 8.78 us -> 0.9 us  [the longest x1 0.82 us: local(): input_grad = (total + returned.astype(F32)).astype(BF16)]
    ppermute x51 -> x59, starting transfers between devices: 58.5 us -> 63.9 us  [swap(): return lax.ppermute(v, axis, [(i, i ^ bit) for i in range(count)])]
    pallas_call x28 -> x48, Pallas kernels: 53.2 us -> 49.3 us  [the longest x21 25.8 us: pack(): pl.pallas_call(functools.partial(pack_kernel, moves), in_specs=[pl.BlockS...]
    another operation x8 -> x2, local copies, waits for them, and re-layouts: 3.91 us -> 0.01 us  [local(): bias = jnp.stack([b_hidden, b_hidden, bias, bias])]
    select_n x8 -> x0, other arithmetic: 3.44 us -> none  [relative(): v = jnp.where(on == 1, jnp.flip(v, axis + b), v)]
    rev x3 -> x0, local copies, waits for them, and re-layouts: 3.41 us -> none  [relative(): v = jnp.where(on == 1, jnp.flip(v, axis + b), v)]
    unnamed x137 -> x121, local copies, waits for them, and re-layouts: 13.9 us -> 16 us
    pallas_call x1 -> x2, Pallas kernels: 8.22 us -> 8.74 us  [attend(): pl.pallas_call(functools.partial(attend_kernel, half_rows=rows), grid=(pa...]
  transfers between devices with their start and end apart: 51 -> 59, of which waited for: 25 -> 30; matrix products, arithmetic and copies ran while one was open for 11% -> 1% of each run, Pallas kernels for 23% -> 24%
where the time goes in v1:
time: 266 us; the launch traced here: 265 us
  waiting for transfers between devices  96 us (36%)
  Pallas kernels  82.4 us (31%)
  starting transfers between devices  63.9 us (24%)
  local copies, waits for them, and re-layouts  17 us (6%)
  other arithmetic  4.04 us (2%)
    ppermute x59, waiting for transfers between devices, swap(): return lax.ppermute(v, axis, [(i, i ^ bit) for i in range(count)])  96 us
    ppermute x59, starting transfers between devices, swap(): return lax.ppermute(v, axis, [(i, i ^ bit) for i in range(count)])  63.9 us
    pallas_call x21, Pallas kernels, pack(): pl.pallas_call(functools.partial(pack_kernel, moves), in_specs=[pl.BlockS...  25.8 us
    unnamed x121, local copies, waits for them, and re-layouts  16 us
    pallas_call x9, Pallas kernels, whole_call(): pl.pallas_call(kernel, in_specs=[vmem] * len(args) + [space] * len(earlie...  14.5 us
    pallas_call x1, Pallas kernels, attend_back(): pl.pallas_call(functools.partial(attend_back_kernel, half_rows=rows), gri...  9.13 us
    pallas_call x2, Pallas kernels, attend(): pl.pallas_call(functools.partial(attend_kernel, half_rows=rows), grid=(pa...  8.74 us
    pallas_call x9, Pallas kernels, fold(): pl.pallas_call(functools.partial(fold_kernel, [picks for _, _, picks in g...  8.01 us
  transfers between devices with their start and end apart: 59, of which 30 were waited for; matrix products, arithmetic and copies ran while one was open for 1% of the time, Pallas kernels for 24%

profile of v1, /device:TPU:0, one launch (start us, length us, event | category | flops | bytes accessed | tf_op | source)
XLA Modules:
  0.0 265.3 jit_solution(7842835961873221085)
XLA Ops:
  5.1 5.0 %collective-permute-start.2 = (bf16[96,768]{1,0:T(8,128)(2,1)}, bf16[96,768]{1,0:T(8,128)(2,1)S(1)}, u32[]{:S(2)}, u32[]{:S(2)}) collective-permute-start(bf16[96,768]{1,0:T(8,128)(2,1)} %bitcast.8), channel_id=1, source_target_pairs={{0,3},{1,2},{2,1},{3,0},{4,7},{5,6},{6,5},{7,4},{8,11},{9,10},{10,... | collective-permute-start | bytes 442376 | tf_op jit(solution)/shard_map/ppermute | solution.py:33
  15.1 7.9 %collective-permute-done.1.refs_1_ = bf16[96,768]{1,0:T(8,128)(2,1)} collective-permute-done((bf16[96,768]{1,0:T(8,128)(2,1)}, bf16[96,768]{1,0:T(8,128)(2,1)}, u32[]{:S(2)}, u32[]{:S(2)}) %collective-permute-start.1) | collective-permute-done | bytes 147488 | tf_op jit(solution)/shard_map/ppermute | solution.py:33
  32.7 4.9 %collective-permute-done.9.refs_3_.refs_2_ = bf16[112,768]{1,0:T(8,128)(2,1)S(1)} collective-permute-done((bf16[112,768]{1,0:T(8,128)(2,1)}, bf16[112,768]{1,0:T(8,128)(2,1)S(1)}, u32[]{:S(2)}, u32[]{:S(2)}) %collective-permute-start.9) | collective-permute-done | bytes 172064 | tf_op jit(solution)/shard_map/ppermute | solution.py:33
  37.7 6.4 %collective-permute-done.8.refs_2_.refs_1_ = bf16[112,768]{1,0:T(8,128)(2,1)S(1)} collective-permute-done((bf16[112,768]{1,0:T(8,128)(2,1)}, bf16[112,768]{1,0:T(8,128)(2,1)S(1)}, u32[]{:S(2)}, u32[]{:S(2)}) %collective-permute-start.8) | collective-permute-done | bytes 172064 | tf_op jit(solution)/shard_map/ppermute | solution.py:33
  50.6 4.8 %collective-permute-done.10.refs_7_.xo_ref.refs_1_ = bf16[256,768]{1,0:T(8,128)(2,1)S(1)} collective-permute-done((bf16[256,768]{1,0:T(8,128)(2,1)}, bf16[256,768]{1,0:T(8,128)(2,1)S(1)}, u32[]{:S(2)}, u32[]{:S(2)}) %collective-permute-start.10) | collective-permute-done | bytes 393248 | tf_op jit(solution)/shard_map/ppermute | solution.py:33
  75.5 4.6 %shard_map.316 = (bf16[256,768]{1,0:T(8,128)(2,1)S(1)}, bf16[512,768]{1,0:T(8,128)(2,1)S(1)}, bf16[512,768]{1,0:T(8,128)(2,1)S(1)}, bf16[4,3,4,16,768]{4,3,2,1,0...) custom-call(s32[2]{0:T(128)S(1)} %pad_add_fusion.1.place_ref, ...), custom_call_target="tpu_custom_call" | custom-call | flops 1 | bytes 1 | tf_op jit(solution)/shard_map/pallas_call | solution.py:284
  85.2 4.4 %shard_map.321 = (bf16[256,384]{1,0:T(8,128)(2,1)S(1)}, f32[24,256]{1,0:T(8,128)S(1)}) custom-call(s32[2]{0:T(128)S(1)} %pad_add_fusion.place_ref, bf16[256,768]{1,0:T(8,128)(2,1)S(1)} %get-tuple-element.113.refs_1_.q_ref, bf16[512,768]{1,0:T(8,128)(2,1)S(1)} %get-tuple-element.114.k_ref, bf16[512,768]{1,0:T(8,128)(2,1)S(1)} %get-tuple-element.115.v_ref, ...), custom_call_target="tpu_custom_call" | custom-call | flops 1 | bytes 1 | tf_op jit(solution)/shard_map/pallas_call | solution.py:426
  96.1 4.4 %shard_map.325 = (bf16[256,384]{1,0:T(8,128)(2,1)S(1)}, f32[24,256]{1,0:T(8,128)S(1)}) custom-call(s32[2]{0:T(128)S(1)} %pad_add_fusion.place_ref, bf16[256,768]{1,0:T(8,128)(2,1)S(1)} %get-tuple-element.113.refs_1_.q_ref, bf16[512,768]{1,0:T(8,128)(2,1)S(1)} %get-tuple-element.114.k_ref, bf16[512,768]{1,0:T(8,128)(2,1)S(1)} %get-tuple-element.115.v_ref, ...), custom_call_target="tpu_custom_call" | custom-call | flops 1 | bytes 1 | tf_op jit(solution)/shard_map/pallas_call | solution.py:426
  107.3 4.2 %collective-permute-done.22.refs_4_ = bf16[3,48,768]{2,1,0:T(8,128)(2,1)S(1)} collective-permute-done((bf16[3,48,768]{2,1,0:T(8,128)(2,1)S(1)}, bf16[3,48,768]{2,1,0:T(8,128)(2,1)S(1)}, u32[]{:S(2)}, u32[]{:S(2)}) %collective-permute-start.22) | collective-permute-done | bytes 221216 | tf_op jit(solution)/shard_map/ppermute | solution.py:33
  116.0 3.2 %collective-permute-done.24.w_other_ref = bf16[1536,768]{1,0:T(8,128)(2,1)S(1)} collective-permute-done((bf16[1536,768]{1,0:T(8,128)(2,1)S(1)}, bf16[1536,768]{1,0:T(8,128)(2,1)S(1)}, u32[]{:S(2)}, u32[]{:S(2)}) %collective-permute-start.24) | collective-permute-done | bytes 2359328 | tf_op jit(solution)/shard_map/ppermute | solution.py:33
  124.9 2.8 %collective-permute-done.25 = bf16[1536,768]{1,0:T(8,128)(2,1)S(1)} collective-permute-done((bf16[1536,768]{1,0:T(8,128)(2,1)S(1)}, bf16[1536,768]{1,0:T(8,128)(2,1)S(1)}, u32[]{:S(2)}, u32[]{:S(2)}) %collective-permute-start.25) | collective-permute-done | bytes 2359328 | tf_op jit(solution)/shard_map/ppermute | solution.py:33
  138.3 9.1 %shard_map.339 = (bf16[256,768]{1,0:T(8,128)(2,1)S(1)}, bf16[512,768]{1,0:T(8,128)(2,1)S(1)}, bf16[512,768]{1,0:T(8,128)(2,1)S(1)}) custom-call(s32[2]{0:T(128)S(1)} %pad_add_fusion.place_ref, bf16[256,768]{1,0:T(8,128)(2,1)S(1)} %get-tuple-element.113.refs_1_.q_ref, bf16[512,768]{1,0:T(8,128)(2,1)S(1)} %get-tuple-element.114.k_ref, ...), custom_call_target="tpu_custom_call" | custom-call | flops 1 | bytes 1 | tf_op jit(solution)/shard_map/pallas_call | solution.py:452
  153.3 5.4 %shard_map.342 = (bf16[4,4,96,896]{3,2,1,0:T(8,128)(2,1)S(1)}, bf16[4,4,96,896]{3,2,1,0:T(8,128)(2,1)S(1)}) custom-call(s32[2]{0:T(128)S(1)} %pad_add_fusion.1.place_ref, bf16[256,768]{1,0:T(8,128)(2,1)S(1)} %get-tuple-element.142.dq_ref, bf16[512,768]{1,0:T(8,128)(2,1)S(1)} %get-tuple-element.143.dk_ref, bf16[512,768]{1,0:T(8,128)(2,1)S(1)} %get-tuple-element.144.dv_ref, ...), custom_call_target="tpu_custom_call" | custom-call | flops 1 | bytes 1 | tf_op jit(solution)/shard_map/pallas_call | solution.py:560
  160.3 6.0 %collective-permute-done.33.refs_3_ = bf16[2,96,768]{2,1,0:T(8,128)(2,1)S(1)} collective-permute-done((bf16[2,96,768]{2,1,0:T(8,128)(2,1)S(1)}, bf16[2,96,768]{2,1,0:T(8,128)(2,1)S(1)}, u32[]{:S(2)}, u32[]{:S(2)}) %collective-permute-start.33) | collective-permute-done | bytes 294944 | tf_op jit(solution)/shard_map/ppermute | solution.py:33
  169.4 5.3 %collective-permute-done.34 = bf16[4,4,96,896]{3,2,1,0:T(8,128)(2,1)S(1)} collective-permute-done((bf16[4,4,96,896]{3,2,1,0:T(8,128)(2,1)}, bf16[4,4,96,896]{3,2,1,0:T(8,128)(2,1)S(1)}, u32[]{:S(2)}, u32[]{:S(2)}) %collective-permute-start.34) | collective-permute-done | bytes 2752544 | tf_op jit(solution)/shard_map/ppermute | solution.py:33
  181.7 2.9 %collective-permute-done.37.a_ref = bf16[96,768]{1,0:T(8,128)(2,1)S(1)} collective-permute-done((bf16[96,768]{1,0:T(8,128)(2,1)S(1)}, bf16[96,768]{1,0:T(8,128)(2,1)S(1)}, u32[]{:S(2)}, u32[]{:S(2)}) %collective-permute-start.37) | collective-permute-done | bytes 147488 | tf_op jit(solution)/shard_map/ppermute | solution.py:33
  185.9 6.2 %collective-permute-done.38.b_ref = bf16[96,768]{1,0:T(8,128)(2,1)S(1)} collective-permute-done((bf16[96,768]{1,0:T(8,128)(2,1)S(1)}, bf16[96,768]{1,0:T(8,128)(2,1)S(1)}, u32[]{:S(2)}, u32[]{:S(2)}) %collective-permute-start.38) | collective-permute-done | bytes 147488 | tf_op jit(solution)/shard_map/ppermute | solution.py:33
  197.9 2.8 %collective-permute-done.43.refs_3_ = bf16[2,96,768]{2,1,0:T(8,128)(2,1)S(1)} collective-permute-done((bf16[2,96,768]{2,1,0:T(8,128)(2,1)S(1)}, bf16[2,96,768]{2,1,0:T(8,128)(2,1)S(1)}, u32[]{:S(2)}, u32[]{:S(2)}) %collective-permute-start.43) | collective-permute-done | bytes 294944 | tf_op jit(solution)/shard_map/ppermute | solution.py:33
  207.2 3.4 %collective-permute-done.44.a_ref = bf16[96,768]{1,0:T(8,128)(2,1)S(1)} collective-permute-done((bf16[96,768]{1,0:T(8,128)(2,1)S(1)}, bf16[96,768]{1,0:T(8,128)(2,1)S(1)}, u32[]{:S(2)}, u32[]{:S(2)}) %collective-permute-start.44) | collective-permute-done | bytes 147488 | tf_op jit(solution)/shard_map/ppermute | solution.py:33
  210.6 4.6 %collective-permute-done.45.b_ref = bf16[96,768]{1,0:T(8,128)(2,1)S(1)} collective-permute-done((bf16[96,768]{1,0:T(8,128)(2,1)S(1)}, bf16[96,768]{1,0:T(8,128)(2,1)S(1)}, u32[]{:S(2)}, u32[]{:S(2)}) %collective-permute-start.45) | collective-permute-done | bytes 147488 | tf_op jit(solution)/shard_map/ppermute | solution.py:33
  218.4 3.4 %collective-permute-done.47.a_ref.refs_2_ = bf16[96,896]{1,0:T(8,128)(2,1)S(1)} collective-permute-done((bf16[96,896]{1,0:T(8,128)(2,1)S(1)}, bf16[96,896]{1,0:T(8,128)(2,1)S(1)}, u32[]{:S(2)}, u32[]{:S(2)}) %collective-permute-start.47) | collective-permute-done | bytes 172064 | tf_op jit(solution)/shard_map/ppermute | solution.py:33
  229.1 8.7 %collective-permute-done.48.b_ref = bf16[96,896]{1,0:T(8,128)(2,1)S(1)} collective-permute-done((bf16[96,896]{1,0:T(8,128)(2,1)S(1)}, bf16[96,896]{1,0:T(8,128)(2,1)S(1)}, u32[]{:S(2)}, u32[]{:S(2)}) %collective-permute-start.48) | collective-permute-done | bytes 172064 | tf_op jit(solution)/shard_map/ppermute | solution.py:33
  249.7 3.2 %shard_map.357 = (f32[768,768]{1,0:T(8,128)}, f32[768,768]{1,0:T(8,128)}) custom-call(s32[2]{0:T(128)S(1)} %pad_add_fusion.1.place_ref, bf16[4,2,96,768]{3,2,1,0:T(8,128)(2,1)S(1)} %shard_map.356.own_ref, bf16[4,2,96,768]{3,2,1,0:T(8,128)(2,1)S(1)} %collective-permute-done.57.other_ref), custom_call_target="tpu_custom_call" | custom-call | tf_op jit(solution)/shard_map/pallas_call | solution.py:351
  254.4 3.2 %collective-permute-done.51.refs_2_ = bf16[96,896]{1,0:T(8,128)(2,1)S(1)} collective-permute-done((bf16[96,896]{1,0:T(8,128)(2,1)S(1)}, bf16[96,896]{1,0:T(8,128)(2,1)S(1)}, u32[]{:S(2)}, u32[]{:S(2)}) %collective-permute-start.51) | collective-permute-done | bytes 172064 | tf_op jit(solution)/shard_map/ppermute | solution.py:33
  (292 shorter events, 146.4 us)
Async XLA Ops:
  24.6 20.9 %collective-permute-start.4 = (bf16[3,96,768]{2,1,0:T(8,128)(2,1)S(1)}, bf16[3,96,768]{2,1,0:T(8,128)(2,1)S(1)}, u32[]{:S(2)}, u32[]{:S(2)}) collective-permute-start(bf16[3,96,768]{2,1,0:T(8,128)(2,1)S(1)} %shard_map.309.refs_1_), channel_id=1, source_target_pairs={{0,16},{4,20},{8,24},{12,28},{16,0},{20,4},{24,8},{28,12},{1,17},{... | collective-permute-start | bytes 1327112 | tf_op jit(solution)/shard_map/ppermute | solution.py:33
  26.2 21.5 %collective-permute-start.3 = (bf16[3,96,768]{2,1,0:T(8,128)(2,1)S(1)}, bf16[3,96,768]{2,1,0:T(8,128)(2,1)}, u32[]{:S(2)}, u32[]{:S(2)}) collective-permute-start(bf16[3,96,768]{2,1,0:T(8,128)(2,1)S(1)} %shard_map.309.refs_1_), channel_id=1, source_target_pairs={{0,8},{4,12},{8,0},{12,4},{16,24},{20,28},{24,16},{28,20},{1,9},{5... | collective-permute-start | bytes 1327112 | tf_op jit(solution)/shard_map/ppermute | solution.py:33
  64.4 15.7 %collective-permute-start.12 = (bf16[3,96,768]{2,1,0:T(8,128)(2,1)}, bf16[3,96,768]{2,1,0:T(8,128)(2,1)}, u32[]{:S(2)}, u32[]{:S(2)}) collective-permute-start(bf16[3,96,768]{2,1,0:T(8,128)(2,1)} %shard_map.318.refs_1_), channel_id=1, source_target_pairs={{0,8},{4,12},{8,0},{12,4},{16,24},{20,28},{24,16},{28,20},{1,9},{5... | collective-permute-start | bytes 1327112 | tf_op jit(solution)/shard_map/ppermute | solution.py:33
  65.9 16.6 %collective-permute-start.13 = (bf16[3,96,768]{2,1,0:T(8,128)(2,1)}, bf16[3,96,768]{2,1,0:T(8,128)(2,1)}, u32[]{:S(2)}, u32[]{:S(2)}) collective-permute-start(bf16[3,96,768]{2,1,0:T(8,128)(2,1)} %shard_map.318.refs_1_), channel_id=1, source_target_pairs={{0,16},{4,20},{8,24},{12,28},{16,0},{20,4},{24,8},{28,12},{1,17},{... | collective-permute-start | bytes 1327112 | tf_op jit(solution)/shard_map/ppermute | solution.py:33
  67.1 22.5 %collective-permute-start.18 = (bf16[96,768]{1,0:T(8,128)(2,1)}, bf16[96,768]{1,0:T(8,128)(2,1)}, u32[]{:S(2)}, u32[]{:S(2)}) collective-permute-start(bf16[96,768]{1,0:T(8,128)(2,1)} %shard_map.322), channel_id=1, source_target_pairs={{0,3},{1,2},{2,1},{3,0},{4,7},{5,6},{6,5},{7,4},{8,11},{9,10},{10,... | collective-permute-start | bytes 442376 | tf_op jit(solution)/shard_map/ppermute | solution.py:33
  69.3 20.3 %collective-permute-start.17 = (bf16[96,768]{1,0:T(8,128)(2,1)}, bf16[96,768]{1,0:T(8,128)(2,1)}, u32[]{:S(2)}, u32[]{:S(2)}) collective-permute-start(bf16[96,768]{1,0:T(8,128)(2,1)} %shard_map.322), channel_id=1, source_target_pairs={{0,2},{1,3},{2,0},{3,1},{4,6},{5,7},{6,4},{7,5},{8,10},{9,11},{10,... | collective-permute-start | bytes 442376 | tf_op jit(solution)/shard_map/ppermute | solution.py:33
  70.5 19.1 %collective-permute-start.16 = (bf16[96,768]{1,0:T(8,128)(2,1)}, bf16[96,768]{1,0:T(8,128)(2,1)}, u32[]{:S(2)}, u32[]{:S(2)}) collective-permute-start(bf16[96,768]{1,0:T(8,128)(2,1)} %shard_map.322), channel_id=1, source_target_pairs={{0,1},{1,0},{2,3},{3,2},{4,5},{5,4},{6,7},{7,6},{8,9},{9,8},{10,11... | collective-permute-start | bytes 442376 | tf_op jit(solution)/shard_map/ppermute | solution.py:33
  91.2 14.6 %collective-permute-start.21 = (bf16[3,96,768]{2,1,0:T(8,128)(2,1)S(1)}, bf16[3,96,768]{2,1,0:T(8,128)(2,1)S(1)}, u32[]{:S(2)}, u32[]{:S(2)}) collective-permute-start(bf16[3,96,768]{2,1,0:T(8,128)(2,1)S(1)} %shard_map.323.refs_6_.refs_1_), channel_id=1, source_target_pairs={{0,16},{4,20},{8,24},{12,28},{16,0},{20,4},{24,8},{28,12},{1,17},{... | collective-permute-start | bytes 1327112 | tf_op jit(solution)/shard_map/ppermute | solution.py:33
  130.5 19.8 %collective-permute-start.29 = (bf16[2,2,96,768]{3,2,1,0:T(8,128)(2,1)S(1)}, bf16[2,2,96,768]{3,2,1,0:T(8,128)(2,1)S(1)}, u32[]{:S(2)}, u32[]{:S(2)}) collective-permute-start(bf16[2,2,96,768]{3,2,1,0:T(8,128)(2,1)S(1)} %get-tuple-element.156), channel_id=1, source_target_pairs={{0,16},{4,20},{8,24},{12,28},{16,0},{20,4},{24,8},{28,12},{1,17},{... | collective-permute-start | bytes 1769480 | tf_op jit(solution)/shard_map/ppermute | solution.py:33
  132.0 18.3 %collective-permute-start.28 = (bf16[2,2,96,768]{3,2,1,0:T(8,128)(2,1)S(1)}, bf16[2,2,96,768]{3,2,1,0:T(8,128)(2,1)S(1)}, u32[]{:S(2)}, u32[]{:S(2)}) collective-permute-start(bf16[2,2,96,768]{3,2,1,0:T(8,128)(2,1)S(1)} %get-tuple-element.136.refs_3_), channel_id=1, source_target_pairs={{0,8},{4,12},{8,0},{12,4},{16,24},{20,28},{24,16},{28,20},{1,9},{5... | collective-permute-start | bytes 1769480 | tf_op jit(solution)/shard_map/ppermute | solution.py:33
  136.2 30.8 %collective-permute-start.31 = (bf16[2,2,96,768]{3,2,1,0:T(8,128)(2,1)S(1)}, bf16[2,2,96,768]{3,2,1,0:T(8,128)(2,1)S(1)}, u32[]{:S(2)}, u32[]{:S(2)}) collective-permute-start(bf16[2,2,96,768]{3,2,1,0:T(8,128)(2,1)S(1)} %get-tuple-element.162), channel_id=1, source_target_pairs={{0,16},{4,20},{8,24},{12,28},{16,0},{20,4},{24,8},{28,12},{1,17},{... | collective-permute-start | bytes 1769480 | tf_op jit(solution)/shard_map/ppermute | solution.py:33
  137.6 29.5 %collective-permute-start.30 = (bf16[2,2,96,768]{3,2,1,0:T(8,128)(2,1)S(1)}, bf16[2,2,96,768]{3,2,1,0:T(8,128)(2,1)S(1)}, u32[]{:S(2)}, u32[]{:S(2)}) collective-permute-start(bf16[2,2,96,768]{3,2,1,0:T(8,128)(2,1)S(1)} %get-tuple-element.141._), channel_id=1, source_target_pairs={{0,8},{4,12},{8,0},{12,4},{16,24},{20,28},{24,16},{28,20},{1,9},{5... | collective-permute-start | bytes 1769480 | tf_op jit(solution)/shard_map/ppermute | solution.py:33
  149.1 17.2 %collective-permute-start.27 = (bf16[256,768]{1,0:T(8,128)(2,1)S(1)}, bf16[256,768]{1,0:T(8,128)(2,1)S(1)}, u32[]{:S(2)}, u32[]{:S(2)}) collective-permute-start(bf16[256,768]{1,0:T(8,128)(2,1)S(1)} %get-tuple-element.149.refs_4_), channel_id=1, source_target_pairs={{0,1},{1,0},{2,3},{3,2},{4,5},{5,4},{6,7},{7,6},{8,9},{9,8},{10,11... | collective-permute-start | bytes 1179656 | tf_op jit(solution)/shard_map/ppermute | solution.py:33
  151.1 15.1 %collective-permute-start.33 = (bf16[2,96,768]{2,1,0:T(8,128)(2,1)S(1)}, bf16[2,96,768]{2,1,0:T(8,128)(2,1)S(1)}, u32[]{:S(2)}, u32[]{:S(2)}) collective-permute-start(bf16[2,96,768]{2,1,0:T(8,128)(2,1)S(1)} %get-tuple-element.165), channel_id=1, source_target_pairs={{0,8},{4,12},{8,0},{12,4},{16,24},{20,28},{24,16},{28,20},{1,9},{5... | collective-permute-start | bytes 884744 | tf_op jit(solution)/shard_map/ppermute | solution.py:33
  152.5 13.8 %collective-permute-start.32 = (bf16[2,96,768]{2,1,0:T(8,128)(2,1)S(1)}, bf16[2,96,768]{2,1,0:T(8,128)(2,1)S(1)}, u32[]{:S(2)}, u32[]{:S(2)}) collective-permute-start(bf16[2,96,768]{2,1,0:T(8,128)(2,1)S(1)} %get-tuple-element.157._), channel_id=1, source_target_pairs={{0,16},{4,20},{8,24},{12,28},{16,0},{20,4},{24,8},{28,12},{1,17},{... | collective-permute-start | bytes 884744 | tf_op jit(solution)/shard_map/ppermute | solution.py:33
  176.0 18.4 %collective-permute-start.35 = (bf16[2,2,96,896]{3,2,1,0:T(8,128)(2,1)S(1)}, bf16[2,2,96,896]{3,2,1,0:T(8,128)(2,1)S(1)}, u32[]{:S(2)}, u32[]{:S(2)}) collective-permute-start(bf16[2,2,96,896]{3,2,1,0:T(8,128)(2,1)S(1)} %get-tuple-element.169), channel_id=1, source_target_pairs={{0,8},{4,12},{8,0},{12,4},{16,24},{20,28},{24,16},{28,20},{1,9},{5... | collective-permute-start | bytes 2064392 | tf_op jit(solution)/shard_map/ppermute | solution.py:33
  176.6 18.3 %collective-permute-start.36 = (bf16[2,2,96,896]{3,2,1,0:T(8,128)(2,1)S(1)}, bf16[2,2,96,896]{3,2,1,0:T(8,128)(2,1)S(1)}, u32[]{:S(2)}, u32[]{:S(2)}) collective-permute-start(bf16[2,2,96,896]{3,2,1,0:T(8,128)(2,1)S(1)} %get-tuple-element.171), channel_id=1, source_target_pairs={{0,16},{4,20},{8,24},{12,28},{16,0},{20,4},{24,8},{28,12},{1,17},{... | collective-permute-start | bytes 2064392 | tf_op jit(solution)/shard_map/ppermute | solution.py:33
  178.4 13.7 %collective-permute-start.38 = (bf16[96,768]{1,0:T(8,128)(2,1)S(1)}, bf16[96,768]{1,0:T(8,128)(2,1)S(1)}, u32[]{:S(2)}, u32[]{:S(2)}) collective-permute-start(bf16[96,768]{1,0:T(8,128)(2,1)S(1)} %copy-done.47), channel_id=1, source_target_pairs={{0,2},{1,3},{2,0},{3,1},{4,6},{5,7},{6,4},{7,5},{8,10},{9,11},{10,... | collective-permute-start | bytes 442376 | tf_op jit(solution)/shard_map/ppermute | solution.py:33
  180.1 13.3 %collective-permute-start.39 = (bf16[96,768]{1,0:T(8,128)(2,1)S(1)}, bf16[96,768]{1,0:T(8,128)(2,1)S(1)}, u32[]{:S(2)}, u32[]{:S(2)}) collective-permute-start(bf16[96,768]{1,0:T(8,128)(2,1)S(1)} %copy-done.45), channel_id=1, source_target_pairs={{0,3},{1,2},{2,1},{3,0},{4,7},{5,6},{6,5},{7,4},{8,11},{9,10},{10,... | collective-permute-start | bytes 442376 | tf_op jit(solution)/shard_map/ppermute | solution.py:33
  184.6 16.1 %collective-permute-start.43 = (bf16[2,96,768]{2,1,0:T(8,128)(2,1)S(1)}, bf16[2,96,768]{2,1,0:T(8,128)(2,1)S(1)}, u32[]{:S(2)}, u32[]{:S(2)}) collective-permute-start(bf16[2,96,768]{2,1,0:T(8,128)(2,1)S(1)} %copy-done.43), channel_id=1, source_target_pairs={{0,8},{4,12},{8,0},{12,4},{16,24},{20,28},{24,16},{28,20},{1,9},{5... | collective-permute-start | bytes 884744 | tf_op jit(solution)/shard_map/ppermute | solution.py:33
  195.8 19.5 %collective-permute-start.40 = (bf16[2,96,896]{2,1,0:T(8,128)(2,1)S(1)}, bf16[2,96,896]{2,1,0:T(8,128)(2,1)S(1)}, u32[]{:S(2)}, u32[]{:S(2)}) collective-permute-start(bf16[2,96,896]{2,1,0:T(8,128)(2,1)S(1)} %get-tuple-element.176), channel_id=1, source_target_pairs={{0,16},{4,20},{8,24},{12,28},{16,0},{20,4},{24,8},{28,12},{1,17},{... | collective-permute-start | bytes 1032200 | tf_op jit(solution)/shard_map/ppermute | solution.py:33
  196.6 18.8 %collective-permute-start.41 = (bf16[2,96,896]{2,1,0:T(8,128)(2,1)S(1)}, bf16[2,96,896]{2,1,0:T(8,128)(2,1)S(1)}, u32[]{:S(2)}, u32[]{:S(2)}) collective-permute-start(bf16[2,96,896]{2,1,0:T(8,128)(2,1)S(1)} %get-tuple-element.178), channel_id=1, source_target_pairs={{0,8},{4,12},{8,0},{12,4},{16,24},{20,28},{24,16},{28,20},{1,9},{5... | collective-permute-start | bytes 1032200 | tf_op jit(solution)/shard_map/ppermute | solution.py:33
  222.7 15.1 %collective-permute-start.54 = (bf16[2,96,768]{2,1,0:T(8,128)(2,1)S(1)}, bf16[2,96,768]{2,1,0:T(8,128)(2,1)S(1)}, u32[]{:S(2)}, u32[]{:S(2)}) collective-permute-start(bf16[2,96,768]{2,1,0:T(8,128)(2,1)S(1)} %shard_map.353.refs_0_), channel_id=1, source_target_pairs={{0,16},{4,20},{8,24},{12,28},{16,0},{20,4},{24,8},{28,12},{1,17},{... | collective-permute-start | bytes 884744 | tf_op jit(solution)/shard_map/ppermute | solution.py:33
  223.4 15.9 %collective-permute-start.53 = (bf16[2,96,768]{2,1,0:T(8,128)(2,1)S(1)}, bf16[2,96,768]{2,1,0:T(8,128)(2,1)S(1)}, u32[]{:S(2)}, u32[]{:S(2)}) collective-permute-start(bf16[2,96,768]{2,1,0:T(8,128)(2,1)S(1)} %shard_map.353.refs_0_), channel_id=1, source_target_pairs={{0,8},{4,12},{8,0},{12,4},{16,24},{20,28},{24,16},{28,20},{1,9},{5... | collective-permute-start | bytes 884744 | tf_op jit(solution)/shard_map/ppermute | solution.py:33
  (95 other events, 707.1 us)

commit v2 on v1

--- a/solution.py
+++ b/solution.py
@@ -33,32 +33,44 @@
     return lax.ppermute(v, axis, [(i, i ^ bit) for i in range(count)])
 
 
-def pack_kernel(moves, place_ref, *refs):
-    out_ref, sem = refs[-2], refs[-1]
+def pack_kernel(plan, far, place_ref, *refs):
+    outs, sem = refs[len(refs) - len(plan) - 1 : -1], refs[-1]
     core, chip = place_ref[0], place_ref[1]
-    copies = [
-        pltpu.make_async_copy(refs[which].at[source(core, chip)], out_ref.at[target], sem.at[k])
-        for k, (which, source, target) in enumerate(moves)
-    ]
+    copies = []
+    for out_ref, moves in zip(outs, plan):
+        for which, source, target in moves:
+            if which < far:
+                src, dst = refs[which].at[source(core, chip)], out_ref.at[target]
+                copies.append(pltpu.make_async_copy(src, dst, sem.at[len(copies)]))
     for copy in copies:
         copy.start()
+    for out_ref, moves in zip(outs, plan):
+        for which, source, target in moves:
+            if which >= far:
+                out_ref[target or ...] = refs[which][source(core, chip) or ...]
     for copy in copies:
         copy.wait()
 
 
-def pack(where, shape, moves, arrays, earlier=(), far=0):
+def packs(where, shapes, plan, arrays, earlier=(), far=0):
     vmem, space = pl.BlockSpec(memory_space=pltpu.VMEM), pl.BlockSpec(memory_space=pl.ANY)
+    count = sum(which < far for moves in plan for which, _, _ in moves)
     return pl.pallas_call(
-        functools.partial(pack_kernel, moves),
+        functools.partial(pack_kernel, plan, far),
         in_specs=[pl.BlockSpec(memory_space=pltpu.SMEM)]
         + [pl.BlockSpec(memory_space=pltpu.HBM)] * far
-        + [space] * (len(arrays) - far + len(earlier)),
-        out_specs=vmem,
-        out_shape=jax.ShapeDtypeStruct(shape, BF16),
-        scratch_shapes=[pltpu.SemaphoreType.DMA((len(moves),))],
-        compiler_params=pltpu.CompilerParams(vmem_limit_bytes=6 * MIB),
+        + [vmem] * (len(arrays) - far)
+        + [space] * len(earlier),
+        out_specs=[vmem] * len(shapes),
+        out_shape=[jax.ShapeDtypeStruct(shape, BF16) for shape in shapes],
+        scratch_shapes=[pltpu.SemaphoreType.DMA((max(count, 1),))],
+        compiler_params=pltpu.CompilerParams(vmem_limit_bytes=10 * MIB),
         cost_estimate=FREE,
     )(where, *arrays, *earlier)
+
+
+def pack(where, shape, moves, arrays, earlier=(), far=0):
+    return packs(where, [shape], [moves], arrays, earlier, far)[0]
 
 
 def nothing_kernel(*refs):
@@ -76,27 +88,35 @@
     )(v, *earlier)
 
 
-def fold_kernel(plan, place_ref, *refs):
+def fold_kernel(plan, beside, place_ref, *refs):
     del place_ref
-    outs = refs[len(refs) - sum(len(picks) for picks in plan) :]
+    count = sum(len(picks) for picks in plan)
+    outs = refs[len(refs) - count :]
+    others = refs[2 * len(plan) : 2 * len(plan) + beside]
     spot = 0
     for k, picks in enumerate(plan):
         for pick in picks:
             total = refs[2 * k][pick].astype(F32) + refs[2 * k + 1][pick].astype(F32)
-            outs[spot][...] = total.astype(BF16)
+            if beside:
+                outs[spot][0] = others[spot][...]
+                outs[spot][1] = total.astype(BF16)
+            else:
+                outs[spot][...] = total.astype(BF16)
             spot += 1
 
 
-def fold(where, groups, earlier=()):
+def fold(where, groups, earlier=(), beside=()):
     vmem, space = pl.BlockSpec(memory_space=pltpu.VMEM), pl.BlockSpec(memory_space=pl.ANY)
-    arrays = [v for a, b, _ in groups for v in (a, b)]
+    arrays = [v for a, b, _ in groups for v in (a, b)] + list(beside)
     outs = [
-        jax.ShapeDtypeStruct(jax.eval_shape(lambda v, p=pick: v[p], a).shape, BF16)
+        jax.ShapeDtypeStruct(
+            ((2,) if beside else ()) + jax.eval_shape(lambda v, p=pick: v[p], a).shape, BF16
+        )
         for a, _, picks in groups
         for pick in picks
     ]
     return pl.pallas_call(
-        functools.partial(fold_kernel, [picks for _, _, picks in groups]),
+        functools.partial(fold_kernel, [picks for _, _, picks in groups], len(beside)),
         in_specs=[pl.BlockSpec(memory_space=pltpu.SMEM)]
         + [vmem] * len(arrays)
         + [space] * len(earlier),
@@ -127,13 +147,13 @@
     return [swap(v, "tensor", k) for k in range(1, lax.axis_size("tensor"))]
 
 
-def halves_from_chips(where, v, between=(), sent=False):
-    v_x, v_y = swap(v, "dp", XBIT), swap(v, "dp", YBIT)
+def halves_from_chips(where, v, between=(), sent=False, first=None):
+    v_x, v_y = first or (swap(v, "dp", XBIT), swap(v, "dp", YBIT))
     half = v.shape[1] // 2
     low, high = (slice(None), pl.ds(0, half)), (slice(None), pl.ds(half, half))
     shape = (v.shape[0], half) + v.shape[2:]
-    on_y = pack(where, shape, [(0, at(*low), ())], [v_x], between)
-    on_x = pack(where, shape, [(0, at(*high), ())], [v_y], between)
+    plan = [[(0, at(*low), ())], [(1, at(*high), ())]]
+    on_y, on_x = packs(where, [shape, shape], plan, [v_x, v_y], between)
     got = [v, v_x, v_y, swap(on_y, "dp", YBIT), swap(on_x, "dp", XBIT)]
     return (got, [on_y, on_x]) if sent else got
 
@@ -176,13 +196,15 @@
 
 
 def bias_kernel(place_ref, *refs):
-    sources, (bq_ref, bv_ref, bh_ref) = refs[:4], refs[4:]
+    sources, (stack_ref, bq_ref, bv_ref, bh_ref) = refs[:4], refs[-4:]
     core, chip = place_ref[0], place_ref[1]
     rows = sources[0].shape[0] - 16
     width = bq_ref.shape[1]
     group = width // 4
     hidden, heads = [], []
-    for ref in sources:
+    for k, ref in enumerate(sources):
+        if k > 0:
+            stack_ref[k - 1] = ref[:rows]
         tail = ref[rows : rows + 16].astype(F32)
         hidden.append(tail[0:1] + tail[1:2])
         heads.append(tail[2:3] + tail[3:4])
@@ -198,20 +220,24 @@
         out[...] = relative_lanes(row, chip, 2, HD // 4)[0:1]
 
 
-def biases(where, sources, width, hidden):
+def stack_and_biases(where, sources, width, hidden, earlier):
     vmem = pl.BlockSpec(memory_space=pltpu.VMEM)
+    rows = sources[0].shape[0] - 16
     return pl.pallas_call(
         bias_kernel,
-        in_specs=[pl.BlockSpec(memory_space=pltpu.SMEM)] + [vmem] * 4,
-        out_specs=[vmem] * 3,
+        in_specs=[pl.BlockSpec(memory_space=pltpu.SMEM)]
+        + [vmem] * 4
+        + [pl.BlockSpec(memory_space=pl.ANY)] * len(earlier),
+        out_specs=[vmem] * 4,
         out_shape=[
+            jax.ShapeDtypeStruct((len(sources) - 1, rows, width), BF16),
             jax.ShapeDtypeStruct((1, width), F32),
             jax.ShapeDtypeStruct((1, width), F32),
             jax.ShapeDtypeStruct((2, 2 * hidden), F32),
         ],
-        compiler_params=pltpu.CompilerParams(vmem_limit_bytes=4 * MIB),
+        compiler_params=pltpu.CompilerParams(vmem_limit_bytes=6 * MIB),
         cost_estimate=FREE,
-    )(where, *sources)
+    )(where, *sources, *earlier)
 
 
 def qkv_kernel(place_ref, own, other, x_ref, xo_ref, bq_ref, bv_ref, *refs):
@@ -485,10 +511,9 @@
     one_ref,
     two_ref,
     hid_ref,
-    _,
-    keep_ref,
-    send_ref,
+    *refs,
 ):
+    keep_ref, send_ref = refs[-2:]
     rows, width = dq_ref.shape
     shards = keep_ref.shape[1]
     group = width // shards
@@ -559,12 +584,12 @@
     vmem = pl.BlockSpec(memory_space=pltpu.VMEM)
     return pl.pallas_call(
         weights_kernel,
-        in_specs=[pl.BlockSpec(memory_space=pltpu.SMEM)] + [vmem] * 11 + [pl.BlockSpec(memory_space=pl.ANY)],
+        in_specs=[pl.BlockSpec(memory_space=pltpu.SMEM)] + [vmem] * 11 + [pl.BlockSpec(memory_space=pl.ANY)] * len(earlier),
         out_specs=[vmem, vmem],
         out_shape=[full, full],
         compiler_params=pltpu.CompilerParams(vmem_limit_bytes=22 * MIB),
         cost_estimate=FREE,
-    )(where, dq, dk, dv, *contexts, ga, x, xo, *sums, earlier)
+    )(where, dq, dk, dv, *contexts, ga, x, xo, *sums, *earlier)
 
 
 def whole_call(kernel, outs, args, flops, earlier=()):
@@ -779,26 +804,30 @@
     def near_back(j):
         return lambda core, chip: (core * 4 + (chip ^ j),)
 
+    ffn_send = pack(
+        where,
+        (2 * ffn_rows + 16, width),
+        [
+            (0, near_hid(0), (pl.ds(0, ffn_rows),)),
+            (1, near_back(0), (pl.ds(ffn_rows, ffn_rows),)),
+            (2, at(), (pl.ds(2 * ffn_rows, 16),)),
+        ],
+        [hid_near, back_near, bias_rows],
+        (),
+        2,
+    )
+    ffn_z = from_shards(ffn_send)
     att_send = pack(
         where, (2, heads, part, width), [(0, near_heads(0), (0,)), (1, near_heads(0), (1,))], pair, (), 2
     )
-    att_z = from_shards(att_send.reshape(att_rows, width))
-    packed = pack(
-        where,
-        (ffn_rows + 16, width),
-        [(0, near_hid(0), (pl.ds(0, ffn_rows),)), (1, at(), (pl.ds(ffn_rows, 16),))],
-        [hid_near, bias_rows],
-        (),
-        1,
-    )
-    back_send = pack(where, (ffn_rows, width), [(0, near_back(0), ())], [back_near], (), 1)
     rows_send = pack(where, inputs.shape, [(0, at(), ())], [inputs], (), 1)
-    att_stack = stacked(where, att_z, att_rows, (packed, back_send, rows_send))
-    hid_z = from_shards(after(packed, att_stack))
-    rows_other = swap(after(rows_send, *hid_z), "tensor", 1)
-
-    hid_stack = stacked(where, hid_z, ffn_rows)
-    att_far = halves_from_chips(where, att_stack, hid_z[:1])
+    ffn_stack, bq, bv, bh = stack_and_biases(where, [ffn_send] + ffn_z, width, hidden, ())
+    ffn_xy = swap(ffn_stack, "dp", XBIT), swap(ffn_stack, "dp", YBIT)
+    att_z = from_shards(after(att_send.reshape(att_rows, width), *ffn_z))
+    rows_other = swap(after(rows_send, *att_z), "tensor", 1)
+    att_stack = stacked(where, att_z, att_rows, ())
+
+    att_far = halves_from_chips(where, att_stack, list(ffn_xy))
     shape = (4, shards, 2, heads, part, width)
     moves = [(m, near_heads(j), (j, 0, m)) for j in range(4) for m in range(2)]
     moves += [(2 + j, at(), (j, far)) for j in range(3)]
@@ -809,31 +838,36 @@
     att_own = pack(where, shape, moves, pair + att_far, (rows_other,), 2)
     att_swap = swap(att_own, "dp", CORE)
 
-    def ffn_half(near, near_index, far_slices, earlier):
-        halves = [pl.ds(0, ffn_rows // 2), pl.ds(ffn_rows // 2, ffn_rows // 2)]
+    def ffn_half(near, near_index, first, diagonal, earlier):
+        mine = pl.ds(first, ffn_rows)
         moves = [(0, near_index(j), (0, j)) for j in range(4)]
-        moves += [(1 + j, at(), (far, j)) for j in range(3)]
-        moves += [(4 + k, at(), (far, 3, halves[k])) for k in range(2)]
-        own = pack(where, (shards, 4, ffn_rows, width), moves, [near] + far_slices, earlier, 1)
+        moves += [(1 + j, at(every, mine), (far, j)) for j in range(3)]
+        moves += [(4, at(), (far, 3))]
+        own = pack(
+            where,
+            (shards, 4, ffn_rows, width),
+            moves,
+            [near] + ffn_far[:3] + [diagonal],
+            earlier,
+            1,
+        )
         own = own.reshape(-1, width)
         return own, swap(own, "dp", CORE)
 
-    bq, bv, bh = biases(where, [packed] + hid_z, width, hidden)
-
+    every = slice(None)
+    ffn_far, ffn_sent = halves_from_chips(where, ffn_stack, [], True, ffn_xy)
     queries, key_rows, values, wq, wk, wv, wo = project(
         where, att_own, att_swap, inputs, rows_other, bq, bv
     )
     wq, wk, wv, wo = (w.reshape(shards * head_cols, width) for w in (wq, wk, wv, wo))
     place = jnp.stack([lengths[t // per_slot], (t % per_slot) * rows]).astype(jnp.int32)
-    back_z = from_shards(after(back_send, rows_other, att_swap))
-    hid_far, hid_sent = halves_from_chips(where, after(hid_stack, *att_far[3:]), [queries], True)
     pairs = width // LANES // 2
-    context_one, logsum_one = attend(place, queries, key_rows, values, 0, pairs, hid_sent)
-    back_stack = stacked(where, back_z, ffn_rows, [context_one])
-    hid_own, hid_swap = ffn_half(hid_near, near_hid, hid_far, [back_stack])
-    context_two, logsum_two = attend(place, queries, key_rows, values, pairs, pairs, [hid_own])
+    context_one, logsum_one = attend(place, queries, key_rows, values, 0, pairs, [])
+    context_two, logsum_two = attend(place, queries, key_rows, values, pairs, pairs, [context_one])
     logsum = jnp.concatenate([logsum_one, logsum_two], axis=0)
     contexts = (context_one, context_two)
+    hid_own, hid_swap = ffn_half(hid_near, near_hid, 0, ffn_far[3], [context_one])
+    back_own, back_swap = ffn_half(back_near, near_back, ffn_rows, ffn_far[4], [context_one])
     full, low = ((rows, width), F32), ((rows, width), BF16)
     half_low = ((rows, 2 * hidden), BF16)
     three = ((3, width), F32)
@@ -846,8 +880,6 @@
     act_own, slope_own = whole_call(
         hidden_kernel, [half_low, half_low], (mid, hid_own, bh[:1]), 10**9
     )
-    back_far = halves_from_chips(where, back_stack, [act_own])
-    back_own, back_swap = ffn_half(back_near, near_back, back_far, ())
     act_swap, slope_swap = whole_call(
         hidden_kernel, [half_low, half_low], (mid, hid_swap, bh[1:]), 10**9
     )
@@ -869,7 +901,6 @@
     )
 
     two = shards // 2
-    every = slice(None)
     low_half, high_half = pl.ds(0, two), pl.ds(two, shards - two)
     each = [(k,) for k in range(shards)]
 
@@ -884,11 +915,10 @@
         )
         return a_keep, b_keep, swap(a_send, "dp", YBIT), swap(b_send, "dp", XBIT), a_send
 
-    def third_step(step, earlier):
+    def third_step(step, earlier, beside=()):
         a_keep, b_keep, a_got, b_got, _ = step
-        return fold(
-            where, [(a_keep, a_got, each[:two]), (b_keep, b_got, each[: shards - two])], earlier
-        )
+        groups = [(a_keep, a_got, each[:two]), (b_keep, b_got, each[: shards - two])]
+        return fold(where, groups, earlier, beside)
 
     quarter = (shards, 2, 2, ffn_rows, width)
     ffn_picks = [
@@ -944,8 +974,7 @@
         3 * 10**8,
     )
     returned = swap(returned_send, "tensor", 1)
-    back_step = second_step(back_step, ffn_again, ffn_again, (returned_send,))
-
+    back_step = second_step(back_step, ffn_again, ffn_again, (grad_queries,))
     att_keep, att_send = attention_weight_grads(
         where,
         grad_queries,
@@ -957,14 +986,14 @@
         rows_other,
         (sums_one, sums_two, grad_b_hidden),
         shards,
-        back_step[4],
+        (back_step[4],),
     )
     wide = att_keep.shape[-1]
 
     back_pieces = third_step(back_step, (att_keep, returned))
     back_got = send_pieces(back_pieces)
     hid_step = second_step(hid_step, ffn_again, ffn_again, (back_pieces[0],))
-    att_got = swap(after(att_send, hid_step[4]), "dp", CORE)
+    att_got = swap(att_send, "dp", CORE)
     att_shape = (2, 2) + att_keep.shape[1:]
     att_picks = [
         (every, 0, low_half),
@@ -972,31 +1001,34 @@
         (0, every, high_half),
         (1, every, high_half),
     ]
-    att_step = first_step(att_keep.reshape(att_shape), att_got.reshape(att_shape), att_picks, ())
+    att_step = first_step(
+        att_keep.reshape(att_shape), att_got.reshape(att_shape), att_picks, ()
+    )
     hid_pieces = third_step(hid_step, ())
-    back_sum = shards_reduce(back_pieces, back_got)
+    back_sum = shards_reduce(back_pieces, back_got, ())
     hid_got = send_pieces(hid_pieces)
     att_step = second_step(att_step, [(0,), (1,)], [(0,), (1,)], (back_sum,))
     hid_sum = shards_reduce(hid_pieces, hid_got)
     att_pieces = third_step(att_step, (hid_sum,))
     att_got = send_pieces(att_pieces)
-    input_grad = (total + returned.astype(F32)).astype(BF16)
     top = pl.ds(0, ffn_rows)
     ffn_sum = pack(
         where,
         (2, ffn_rows, width),
         [(0, at(top), (0,)), (1, at(top), (1,))],
         [back_sum, hid_sum],
-        att_got[:1],
-    )
+        (),
+    )
+    att_sum = shards_reduce(att_pieces, att_got)
+    input_grad = (total + returned.astype(F32)).astype(BF16)
+    att_far = from_chips(att_sum)
+    ffn_far = halves_from_chips(where, ffn_sum, [att_sum])
     halves = [pl.ds(0, ffn_rows // 2), pl.ds(ffn_rows // 2, ffn_rows // 2)]
     moves = [(j, at(), (j,)) for j in range(3)]
     moves += [(3 + k, at(), (3, slice(None), halves[k])) for k in range(2)]
-    att_sum = shards_reduce(att_pieces, att_got)
-    ffn_far = halves_from_chips(where, ffn_sum, [att_sum])
-    ffn_out = pack(where, (4, 2, ffn_rows, width), moves, ffn_far)
+    ffn_out = pack(where, (4, 2, ffn_rows, width), moves, ffn_far, ())
     back_out, hid_out = ffn_outputs(where, ffn_out, swap(ffn_out, "dp", CORE), hidden, width)
-    att_out = stacked(where, from_chips(att_sum), att_rows, (back_out,))
+    att_out = stacked(where, att_far, att_rows, (back_out,))
     gq, gk, gv, go, sum_q, sum_v, sum_hid, *vectors = att_outputs(
         where, att_out, swap(att_out, "dp", CORE), head_cols, width
     )

time: 266 us -> 251 us (0.944)
  waiting for transfers between devices: 96 us -> 113 us
  starting transfers between devices: 63.9 us -> 50 us
  local copies, waits for them, and re-layouts: 17 us -> 6.17 us
  Pallas kernels: 82.4 us -> 75.4 us
    ppermute x59 -> x52, waiting for transfers between devices: 96 us -> 113 us  [swap(): return lax.ppermute(v, axis, [(i, i ^ bit) for i in range(count)])]
    ppermute x59 -> x52, starting transfers between devices: 63.9 us -> 50 us  [swap(): return lax.ppermute(v, axis, [(i, i ^ bit) for i in range(count)])]
    unnamed x121 -> x48, local copies, waits for them, and re-layouts: 16 us -> 4.43 us
    pallas_call x22 -> x14, Pallas kernels: 26.5 us -> 18.1 us  [the longest x13 16.4 us: packs(): pl.pallas_call(functools.partial(pack_kernel, plan, far), in_specs=[pl.Bl...]
  transfers between devices with their start and end apart: 59 -> 52, of which waited for: 30 -> 28; matrix products, arithmetic and copies ran while one was open for 1% -> 2% of each run, Pallas kernels for 24% -> 21%
where the time goes in v2:
time: 251 us; the launch traced here: 250 us
  waiting for transfers between devices  113 us (45%)
  Pallas kernels  75.4 us (30%)
  starting transfers between devices  50 us (20%)
  local copies, waits for them, and re-layouts  6.17 us (2%)
  other arithmetic  4.47 us (2%)
    ppermute x52, waiting for transfers between devices, swap(): return lax.ppermute(v, axis, [(i, i ^ bit) for i in range(count)])  113 us
    ppermute x52, starting transfers between devices, swap(): return lax.ppermute(v, axis, [(i, i ^ bit) for i in range(count)])  50 us
    pallas_call x13, Pallas kernels, packs(): pl.pallas_call(functools.partial(pack_kernel, plan, far), in_specs=[pl.Bl...  16.4 us
    pallas_call x9, Pallas kernels, whole_call(): pl.pallas_call(kernel, in_specs=[vmem] * len(args) + [space] * len(earlie...  14.5 us
    pallas_call x1, Pallas kernels, attend_back(): pl.pallas_call(functools.partial(attend_back_kernel, half_rows=rows), gri...  9.15 us
    pallas_call x2, Pallas kernels, attend(): pl.pallas_call(functools.partial(attend_kernel, half_rows=rows), grid=(pa...  8.94 us
    pallas_call x9, Pallas kernels, fold(): pl.pallas_call(functools.partial(fold_kernel, [picks for _, _, picks in g...  7.89 us
    pallas_call x1, Pallas kernels, project(): pl.pallas_call(qkv_kernel, in_specs=[pl.BlockSpec(memory_space=pltpu.SMEM...  5.85 us
  transfers between devices with their start and end apart: 52, of which 28 were waited for; matrix products, arithmetic and copies ran while one was open for 2% of the time, Pallas kernels for 21%

profile of v2, /device:TPU:0, one launch (start us, length us, event | category | flops | bytes accessed | tf_op | source)
XLA Modules:
  0.0 250.3 jit_solution(9594565662381499803)
XLA Ops:
  5.0 5.1 %collective-permute-start.2 = (bf16[208,768]{1,0:T(8,128)(2,1)S(1)}, bf16[208,768]{1,0:T(8,128)(2,1)S(1)}, u32[]{:S(2)}, u32[]{:S(2)}) collective-permute-start(bf16[208,768]{1,0:T(8,128)(2,1)S(1)} %shard_map.306.refs_0_), channel_id=1, source_target_pairs={{0,3},{1,2},{2,1},{3,0},{4,7},{5,6},{6,5},{7,4},{8,11},{9,10},{10,... | collective-permute-start | bytes 958472 | tf_op jit(solution)/shard_map/ppermute | solution.py:33
  10.7 7.9 %collective-permute-done.2.refs_3_ = bf16[208,768]{1,0:T(8,128)(2,1)S(1)} collective-permute-done((bf16[208,768]{1,0:T(8,128)(2,1)S(1)}, bf16[208,768]{1,0:T(8,128)(2,1)S(1)}, u32[]{:S(2)}, u32[]{:S(2)}) %collective-permute-start.2) | collective-permute-done | bytes 319520 | tf_op jit(solution)/shard_map/ppermute | solution.py:33
  18.6 18.7 %collective-permute-done.1.refs_2_ = bf16[208,768]{1,0:T(8,128)(2,1)S(1)} collective-permute-done((bf16[208,768]{1,0:T(8,128)(2,1)S(1)}, bf16[208,768]{1,0:T(8,128)(2,1)S(1)}, u32[]{:S(2)}, u32[]{:S(2)}) %collective-permute-start.1) | collective-permute-done | bytes 319520 | tf_op jit(solution)/shard_map/ppermute | solution.py:33
  49.8 4.4 %collective-permute-done.5.refs_2_.refs_3_ = bf16[96,768]{1,0:T(8,128)(2,1)S(1)} collective-permute-done((bf16[96,768]{1,0:T(8,128)(2,1)}, bf16[96,768]{1,0:T(8,128)(2,1)S(1)}, u32[]{:S(2)}, u32[]{:S(2)}) %collective-permute-start.5) | collective-permute-done | bytes 147488 | tf_op jit(solution)/shard_map/ppermute | solution.py:33
  54.2 5.1 %collective-permute-done.4.refs_1_.refs_2_ = bf16[96,768]{1,0:T(8,128)(2,1)S(1)} collective-permute-done((bf16[96,768]{1,0:T(8,128)(2,1)}, bf16[96,768]{1,0:T(8,128)(2,1)S(1)}, u32[]{:S(2)}, u32[]{:S(2)}) %collective-permute-start.4) | collective-permute-done | bytes 147488 | tf_op jit(solution)/shard_map/ppermute | solution.py:33
  63.3 8.9 %collective-permute-done.7.refs_1_ = bf16[3,96,768]{2,1,0:T(8,128)(2,1)} collective-permute-done((bf16[3,96,768]{2,1,0:T(8,128)(2,1)}, bf16[3,96,768]{2,1,0:T(8,128)(2,1)}, u32[]{:S(2)}, u32[]{:S(2)}) %collective-permute-start.7) | collective-permute-done | bytes 442400 | tf_op jit(solution)/shard_map/ppermute | solution.py:33
  75.8 3.9 %collective-permute-done.10 = bf16[3,48,768]{2,1,0:T(8,128)(2,1)S(1)} collective-permute-done((bf16[3,48,768]{2,1,0:T(8,128)(2,1)S(1)}, bf16[3,48,768]{2,1,0:T(8,128)(2,1)S(1)}, u32[]{:S(2)}, u32[]{:S(2)}) %collective-permute-start.10) | collective-permute-done | bytes 221216 | tf_op jit(solution)/shard_map/ppermute | solution.py:33
  81.2 3.2 %shard_map.313.own = bf16[4,4,2,3,16,768]{5,4,3,2,1,0:T(8,128)(2,1)} custom-call(s32[2]{0:T(128)S(1)} %pad_add_fusion.1.place_ref, bf16[3,4,16,768]{3,2,1,0:T(8,128)(2,1)S(1)} %bitcast.49, bf16[3,4,16,768]{3,2,1,0:T(8,128)(2,1)S(1)} %bitcast.51, bf16[3,2,3,16,768]{4,3,2,1,0:T(8,128)(2,1)} %bitcast.12.refs_2_, bf16[3,2,3,16,768]{4,3,2,1,0:T(8,128)(2,1)} %bitcast.13.refs_3_, ...), custom_call_target="tpu_custom_call" | custom-call | flops 1 | bytes 1 | tf_op jit(solution)/shard_map/pallas_call | solution.py:58
  89.3 5.8 %shard_map.314 = (bf16[256,768]{1,0:T(8,128)(2,1)S(1)}, bf16[512,768]{1,0:T(8,128)(2,1)S(1)}, bf16[512,768]{1,0:T(8,128)(2,1)S(1)}, bf16[4,3,4,16,768]{4,3,2,1,0...) custom-call(s32[2]{0:T(128)S(1)} %pad_add_fusion.1.place_ref, ...), custom_call_target="tpu_custom_call" | custom-call | flops 1 | bytes 1 | tf_op jit(solution)/shard_map/pallas_call | solution.py:310
  95.2 4.4 %shard_map.315 = (bf16[256,384]{1,0:T(8,128)(2,1)S(1)}, f32[24,256]{1,0:T(8,128)S(1)}) custom-call(s32[2]{0:T(128)S(1)} %pad_add_fusion.place_ref, bf16[256,768]{1,0:T(8,128)(2,1)S(1)} %get-tuple-element.123.q_ref, bf16[512,768]{1,0:T(8,128)(2,1)S(1)} %get-tuple-element.124.k_ref, bf16[512,768]{1,0:T(8,128)(2,1)S(1)} %get-tuple-element.125.v_ref), custom_call_target="tpu_custom_call" | custom-call | flops 1 | bytes 1 | tf_op jit(solution)/shard_map/pallas_call | solution.py:452
  105.0 4.6 %shard_map.316 = (bf16[256,384]{1,0:T(8,128)(2,1)S(1)}, f32[24,256]{1,0:T(8,128)S(1)}) custom-call(s32[2]{0:T(128)S(1)} %pad_add_fusion.place_ref, bf16[256,768]{1,0:T(8,128)(2,1)S(1)} %get-tuple-element.123.q_ref, bf16[512,768]{1,0:T(8,128)(2,1)S(1)} %get-tuple-element.124.k_ref, bf16[512,768]{1,0:T(8,128)(2,1)S(1)} %get-tuple-element.125.v_ref, ...), custom_call_target="tpu_custom_call" | custom-call | flops 1 | bytes 1 | tf_op jit(solution)/shard_map/pallas_call | solution.py:452
  118.7 2.8 %collective-permute-done.18 = bf16[1536,768]{1,0:T(8,128)(2,1)S(1)} collective-permute-done((bf16[1536,768]{1,0:T(8,128)(2,1)S(1)}, bf16[1536,768]{1,0:T(8,128)(2,1)S(1)}, u32[]{:S(2)}, u32[]{:S(2)}) %collective-permute-start.18) | collective-permute-done | bytes 2359328 | tf_op jit(solution)/shard_map/ppermute | solution.py:33
  130.0 9.1 %shard_map.330 = (bf16[256,768]{1,0:T(8,128)(2,1)S(1)}, bf16[512,768]{1,0:T(8,128)(2,1)S(1)}, bf16[512,768]{1,0:T(8,128)(2,1)S(1)}) custom-call(s32[2]{0:T(128)S(1)} %pad_add_fusion.place_ref, bf16[256,768]{1,0:T(8,128)(2,1)S(1)} %get-tuple-element.123.q_ref, bf16[512,768]{1,0:T(8,128)(2,1)S(1)} %get-tuple-element.124.k_ref, ...), custom_call_target="tpu_custom_call" | custom-call | flops 1 | bytes 1 | tf_op jit(solution)/shard_map/pallas_call | solution.py:478
  140.9 5.5 %shard_map.333 = (bf16[4,4,96,896]{3,2,1,0:T(8,128)(2,1)S(1)}, bf16[4,4,96,896]{3,2,1,0:T(8,128)(2,1)S(1)}) custom-call(s32[2]{0:T(128)S(1)} %pad_add_fusion.1.place_ref, bf16[256,768]{1,0:T(8,128)(2,1)S(1)} %get-tuple-element.154.dq_ref.refs_4_, bf16[512,768]{1,0:T(8,128)(2,1)S(1)} %get-tuple-element.155.dk_ref, ...), custom_call_target="tpu_custom_call" | custom-call | flops 1 | bytes 1 | tf_op jit(solution)/shard_map/pallas_call | solution.py:585
  158.4 4.3 %collective-permute-done.20.refs_5_ = bf16[256,768]{1,0:T(8,128)(2,1)S(1)} collective-permute-done((bf16[256,768]{1,0:T(8,128)(2,1)S(1)}, bf16[256,768]{1,0:T(8,128)(2,1)S(1)}, u32[]{:S(2)}, u32[]{:S(2)}) %collective-permute-start.20) | collective-permute-done | bytes 393248 | tf_op jit(solution)/shard_map/ppermute | solution.py:33
  163.8 6.8 %collective-permute-done.34.refs_3_ = bf16[2,2,96,768]{3,2,1,0:T(8,128)(2,1)S(1)} collective-permute-done((bf16[2,2,96,768]{3,2,1,0:T(8,128)(2,1)S(1)}, bf16[2,2,96,768]{3,2,1,0:T(8,128)(2,1)S(1)}, u32[]{:S(2)}, u32[]{:S(2)}) %collective-permute-start.34) | collective-permute-done | bytes 589856 | tf_op jit(solution)/shard_map/ppermute | solution.py:33
  173.4 5.2 %collective-permute-done.29.b_ref = bf16[96,768]{1,0:T(8,128)(2,1)S(1)} collective-permute-done((bf16[96,768]{1,0:T(8,128)(2,1)S(1)}, bf16[96,768]{1,0:T(8,128)(2,1)S(1)}, u32[]{:S(2)}, u32[]{:S(2)}) %collective-permute-start.29) | collective-permute-done | bytes 147488 | tf_op jit(solution)/shard_map/ppermute | solution.py:33
  180.1 5.5 %collective-permute-done.30.c_ref = bf16[96,768]{1,0:T(8,128)(2,1)S(1)} collective-permute-done((bf16[96,768]{1,0:T(8,128)(2,1)S(1)}, bf16[96,768]{1,0:T(8,128)(2,1)S(1)}, u32[]{:S(2)}, u32[]{:S(2)}) %collective-permute-start.30) | collective-permute-done | bytes 147488 | tf_op jit(solution)/shard_map/ppermute | solution.py:33
  188.5 3.1 %collective-permute-done.35.refs_1_ = bf16[2,96,768]{2,1,0:T(8,128)(2,1)S(1)} collective-permute-done((bf16[2,96,768]{2,1,0:T(8,128)(2,1)S(1)}, bf16[2,96,768]{2,1,0:T(8,128)(2,1)S(1)}, u32[]{:S(2)}, u32[]{:S(2)}) %collective-permute-start.35) | collective-permute-done | bytes 294944 | tf_op jit(solution)/shard_map/ppermute | solution.py:33
  199.4 6.1 %collective-permute-done.38.b_ref = bf16[96,768]{1,0:T(8,128)(2,1)S(1)} collective-permute-done((bf16[96,768]{1,0:T(8,128)(2,1)S(1)}, bf16[96,768]{1,0:T(8,128)(2,1)S(1)}, u32[]{:S(2)}, u32[]{:S(2)}) %collective-permute-start.38) | collective-permute-done | bytes 147488 | tf_op jit(solution)/shard_map/ppermute | solution.py:33
  216.1 8.8 %collective-permute-done.41.b_ref = bf16[96,896]{1,0:T(8,128)(2,1)S(1)} collective-permute-done((bf16[96,896]{1,0:T(8,128)(2,1)S(1)}, bf16[96,896]{1,0:T(8,128)(2,1)S(1)}, u32[]{:S(2)}, u32[]{:S(2)}) %collective-permute-start.41) | collective-permute-done | bytes 172064 | tf_op jit(solution)/shard_map/ppermute | solution.py:33
  227.7 3.1 %collective-permute-done.48.refs_3_ = bf16[2,48,768]{2,1,0:T(8,128)(2,1)S(1)} collective-permute-done((bf16[2,48,768]{2,1,0:T(8,128)(2,1)S(1)}, bf16[2,48,768]{2,1,0:T(8,128)(2,1)S(1)}, u32[]{:S(2)}, u32[]{:S(2)}) %collective-permute-start.48) | collective-permute-done | bytes 147488 | tf_op jit(solution)/shard_map/ppermute | solution.py:33
  235.7 3.2 %shard_map.346 = (f32[768,768]{1,0:T(8,128)}, f32[768,768]{1,0:T(8,128)}) custom-call(s32[2]{0:T(128)S(1)} %pad_add_fusion.1.place_ref, bf16[4,2,96,768]{3,2,1,0:T(8,128)(2,1)S(1)} %shard_map.345.own_ref, bf16[4,2,96,768]{3,2,1,0:T(8,128)(2,1)S(1)} %collective-permute-done.50.other_ref), custom_call_target="tpu_custom_call" | custom-call | tf_op jit(solution)/shard_map/pallas_call | solution.py:377
  240.4 3.2 %collective-permute-done.44.refs_2_ = bf16[96,896]{1,0:T(8,128)(2,1)S(1)} collective-permute-done((bf16[96,896]{1,0:T(8,128)(2,1)S(1)}, bf16[96,896]{1,0:T(8,128)(2,1)S(1)}, u32[]{:S(2)}, u32[]{:S(2)}) %collective-permute-start.44) | collective-permute-done | bytes 172064 | tf_op jit(solution)/shard_map/ppermute | solution.py:33
  (194 shorter events, 110.2 us)
Async XLA Ops:
  5.0 13.6 %collective-permute-start.2 = (bf16[208,768]{1,0:T(8,128)(2,1)S(1)}, bf16[208,768]{1,0:T(8,128)(2,1)S(1)}, u32[]{:S(2)}, u32[]{:S(2)}) collective-permute-start(bf16[208,768]{1,0:T(8,128)(2,1)S(1)} %shard_map.306.refs_0_), channel_id=1, source_target_pairs={{0,3},{1,2},{2,1},{3,0},{4,7},{5,6},{6,5},{7,4},{8,11},{9,10},{10,... | collective-permute-start | bytes 958472 | tf_op jit(solution)/shard_map/ppermute | solution.py:33
  10.1 27.2 %collective-permute-start.1 = (bf16[208,768]{1,0:T(8,128)(2,1)S(1)}, bf16[208,768]{1,0:T(8,128)(2,1)S(1)}, u32[]{:S(2)}, u32[]{:S(2)}) collective-permute-start(bf16[208,768]{1,0:T(8,128)(2,1)S(1)} %shard_map.306.refs_0_), channel_id=1, source_target_pairs={{0,2},{1,3},{2,0},{3,1},{4,6},{5,7},{6,4},{7,5},{8,10},{9,11},{10,... | collective-permute-start | bytes 958472 | tf_op jit(solution)/shard_map/ppermute | solution.py:33
  10.1 27.2 %collective-permute-start = (bf16[208,768]{1,0:T(8,128)(2,1)S(1)}, bf16[208,768]{1,0:T(8,128)(2,1)S(1)}, u32[]{:S(2)}, u32[]{:S(2)}) collective-permute-start(bf16[208,768]{1,0:T(8,128)(2,1)S(1)} %shard_map.306.refs_0_), channel_id=1, source_target_pairs={{0,1},{1,0},{2,3},{3,2},{4,5},{5,4},{6,7},{7,6},{8,9},{9,8},{10,11... | collective-permute-start | bytes 958472 | tf_op jit(solution)/shard_map/ppermute | solution.py:33
  39.0 33.5 %collective-permute-start.9 = (bf16[3,192,768]{2,1,0:T(8,128)(2,1)}, bf16[3,192,768]{2,1,0:T(8,128)(2,1)S(1)}, u32[]{:S(2)}, u32[]{:S(2)}) collective-permute-start(bf16[3,192,768]{2,1,0:T(8,128)(2,1)} %get-tuple-element.118.refs_1_), channel_id=1, source_target_pairs={{0,16},{4,20},{8,24},{12,28},{16,0},{20,4},{24,8},{28,12},{1,17},{... | collective-permute-start | bytes 2654216 | tf_op jit(solution)/shard_map/ppermute | solution.py:33
  40.6 31.9 %collective-permute-start.8 = (bf16[3,192,768]{2,1,0:T(8,128)(2,1)}, bf16[3,192,768]{2,1,0:T(8,128)(2,1)S(1)}, u32[]{:S(2)}, u32[]{:S(2)}) collective-permute-start(bf16[3,192,768]{2,1,0:T(8,128)(2,1)} %get-tuple-element.118.refs_1_), channel_id=1, source_target_pairs={{0,8},{4,12},{8,0},{12,4},{16,24},{20,28},{24,16},{28,20},{1,9},{5... | collective-permute-start | bytes 2654216 | tf_op jit(solution)/shard_map/ppermute | solution.py:33
  60.7 11.6 %collective-permute-start.7 = (bf16[3,96,768]{2,1,0:T(8,128)(2,1)}, bf16[3,96,768]{2,1,0:T(8,128)(2,1)}, u32[]{:S(2)}, u32[]{:S(2)}) collective-permute-start(bf16[3,96,768]{2,1,0:T(8,128)(2,1)} %shard_map.308), channel_id=1, source_target_pairs={{0,16},{4,20},{8,24},{12,28},{16,0},{20,4},{24,8},{28,12},{1,17},{... | collective-permute-start | bytes 1327112 | tf_op jit(solution)/shard_map/ppermute | solution.py:33
  63.3 12.5 %collective-permute-start.12 = (bf16[256,768]{1,0:T(8,128)(2,1)}, bf16[256,768]{1,0:T(8,128)(2,1)S(1)}, u32[]{:S(2)}, u32[]{:S(2)}) collective-permute-start(bf16[256,768]{1,0:T(8,128)(2,1)} %shard_map.312), channel_id=1, source_target_pairs={{0,1},{1,0},{2,3},{3,2},{4,5},{5,4},{6,7},{7,6},{8,9},{9,8},{10,11... | collective-permute-start | bytes 1179656 | tf_op jit(solution)/shard_map/ppermute | solution.py:33
  86.0 13.6 %collective-permute-start.14 = (bf16[3,96,768]{2,1,0:T(8,128)(2,1)}, bf16[3,96,768]{2,1,0:T(8,128)(2,1)}, u32[]{:S(2)}, u32[]{:S(2)}) collective-permute-start(bf16[3,96,768]{2,1,0:T(8,128)(2,1)} %get-tuple-element.130), channel_id=1, source_target_pairs={{0,16},{4,20},{8,24},{12,28},{16,0},{20,4},{24,8},{28,12},{1,17},{... | collective-permute-start | bytes 1327112 | tf_op jit(solution)/shard_map/ppermute | solution.py:33
  86.6 15.7 %collective-permute-start.16 = (bf16[3,96,768]{2,1,0:T(8,128)(2,1)}, bf16[3,96,768]{2,1,0:T(8,128)(2,1)}, u32[]{:S(2)}, u32[]{:S(2)}) collective-permute-start(bf16[3,96,768]{2,1,0:T(8,128)(2,1)} %get-tuple-element.134), channel_id=1, source_target_pairs={{0,8},{4,12},{8,0},{12,4},{16,24},{20,28},{24,16},{28,20},{1,9},{5... | collective-permute-start | bytes 1327112 | tf_op jit(solution)/shard_map/ppermute | solution.py:33
  124.2 15.6 %collective-permute-start.22 = (bf16[2,2,96,768]{3,2,1,0:T(8,128)(2,1)S(1)}, bf16[2,2,96,768]{3,2,1,0:T(8,128)(2,1)S(1)}, u32[]{:S(2)}, u32[]{:S(2)}) collective-permute-start(bf16[2,2,96,768]{3,2,1,0:T(8,128)(2,1)S(1)} %get-tuple-element.168), channel_id=1, source_target_pairs={{0,16},{4,20},{8,24},{12,28},{16,0},{20,4},{24,8},{28,12},{1,17},{... | collective-permute-start | bytes 1769480 | tf_op jit(solution)/shard_map/ppermute | solution.py:33
  124.8 15.3 %collective-permute-start.21 = (bf16[2,2,96,768]{3,2,1,0:T(8,128)(2,1)S(1)}, bf16[2,2,96,768]{3,2,1,0:T(8,128)(2,1)S(1)}, u32[]{:S(2)}, u32[]{:S(2)}) collective-permute-start(bf16[2,2,96,768]{3,2,1,0:T(8,128)(2,1)S(1)} %get-tuple-element.148.refs_3_), channel_id=1, source_target_pairs={{0,8},{4,12},{8,0},{12,4},{16,24},{20,28},{24,16},{28,20},{1,9},{5... | collective-permute-start | bytes 1769480 | tf_op jit(solution)/shard_map/ppermute | solution.py:33
  148.6 22.0 %collective-permute-start.34 = (bf16[2,2,96,768]{3,2,1,0:T(8,128)(2,1)S(1)}, bf16[2,2,96,768]{3,2,1,0:T(8,128)(2,1)S(1)}, u32[]{:S(2)}, u32[]{:S(2)}) collective-permute-start(bf16[2,2,96,768]{3,2,1,0:T(8,128)(2,1)S(1)} %get-tuple-element.189), channel_id=1, source_target_pairs={{0,16},{4,20},{8,24},{12,28},{16,0},{20,4},{24,8},{28,12},{1,17},{... | collective-permute-start | bytes 1769480 | tf_op jit(solution)/shard_map/ppermute | solution.py:33
  150.1 20.5 %collective-permute-start.33 = (bf16[2,2,96,768]{3,2,1,0:T(8,128)(2,1)S(1)}, bf16[2,2,96,768]{3,2,1,0:T(8,128)(2,1)S(1)}, u32[]{:S(2)}, u32[]{:S(2)}) collective-permute-start(bf16[2,2,96,768]{3,2,1,0:T(8,128)(2,1)S(1)} %get-tuple-element.153._), channel_id=1, source_target_pairs={{0,8},{4,12},{8,0},{12,4},{16,24},{20,28},{24,16},{28,20},{1,9},{5... | collective-permute-start | bytes 1769480 | tf_op jit(solution)/shard_map/ppermute | solution.py:33
  156.4 29.2 %collective-permute-start.24 = (bf16[2,2,96,896]{3,2,1,0:T(8,128)(2,1)S(1)}, bf16[2,2,96,896]{3,2,1,0:T(8,128)(2,1)S(1)}, u32[]{:S(2)}, u32[]{:S(2)}) collective-permute-start(bf16[2,2,96,896]{3,2,1,0:T(8,128)(2,1)S(1)} %get-tuple-element.173), channel_id=1, source_target_pairs={{0,8},{4,12},{8,0},{12,4},{16,24},{20,28},{24,16},{28,20},{1,9},{5... | collective-permute-start | bytes 2064392 | tf_op jit(solution)/shard_map/ppermute | solution.py:33
  157.9 27.7 %collective-permute-start.25 = (bf16[2,2,96,896]{3,2,1,0:T(8,128)(2,1)S(1)}, bf16[2,2,96,896]{3,2,1,0:T(8,128)(2,1)S(1)}, u32[]{:S(2)}, u32[]{:S(2)}) collective-permute-start(bf16[2,2,96,896]{3,2,1,0:T(8,128)(2,1)S(1)} %get-tuple-element.175), channel_id=1, source_target_pairs={{0,16},{4,20},{8,24},{12,28},{16,0},{20,4},{24,8},{28,12},{1,17},{... | collective-permute-start | bytes 2064392 | tf_op jit(solution)/shard_map/ppermute | solution.py:33
  171.4 20.2 %collective-permute-start.35 = (bf16[2,96,768]{2,1,0:T(8,128)(2,1)S(1)}, bf16[2,96,768]{2,1,0:T(8,128)(2,1)S(1)}, u32[]{:S(2)}, u32[]{:S(2)}) collective-permute-start(bf16[2,96,768]{2,1,0:T(8,128)(2,1)S(1)} %get-tuple-element.191), channel_id=1, source_target_pairs={{0,16},{4,20},{8,24},{12,28},{16,0},{20,4},{24,8},{28,12},{1,17},{... | collective-permute-start | bytes 884744 | tf_op jit(solution)/shard_map/ppermute | solution.py:33
  172.0 19.7 %collective-permute-start.36 = (bf16[2,96,768]{2,1,0:T(8,128)(2,1)S(1)}, bf16[2,96,768]{2,1,0:T(8,128)(2,1)S(1)}, u32[]{:S(2)}, u32[]{:S(2)}) collective-permute-start(bf16[2,96,768]{2,1,0:T(8,128)(2,1)S(1)} %get-tuple-element.193), channel_id=1, source_target_pairs={{0,8},{4,12},{8,0},{12,4},{16,24},{20,28},{24,16},{28,20},{1,9},{5... | collective-permute-start | bytes 884744 | tf_op jit(solution)/shard_map/ppermute | solution.py:33
  186.5 21.7 %collective-permute-start.31 = (bf16[2,96,896]{2,1,0:T(8,128)(2,1)S(1)}, bf16[2,96,896]{2,1,0:T(8,128)(2,1)S(1)}, u32[]{:S(2)}, u32[]{:S(2)}) collective-permute-start(bf16[2,96,896]{2,1,0:T(8,128)(2,1)S(1)} %get-tuple-element.184), channel_id=1, source_target_pairs={{0,16},{4,20},{8,24},{12,28},{16,0},{20,4},{24,8},{28,12},{1,17},{... | collective-permute-start | bytes 1032200 | tf_op jit(solution)/shard_map/ppermute | solution.py:33
  187.2 21.0 %collective-permute-start.32 = (bf16[2,96,896]{2,1,0:T(8,128)(2,1)S(1)}, bf16[2,96,896]{2,1,0:T(8,128)(2,1)S(1)}, u32[]{:S(2)}, u32[]{:S(2)}) collective-permute-start(bf16[2,96,896]{2,1,0:T(8,128)(2,1)S(1)} %get-tuple-element.186), channel_id=1, source_target_pairs={{0,8},{4,12},{8,0},{12,4},{16,24},{20,28},{24,16},{28,20},{1,9},{5... | collective-permute-start | bytes 1032200 | tf_op jit(solution)/shard_map/ppermute | solution.py:33
  192.4 13.1 %collective-permute-start.38 = (bf16[96,768]{1,0:T(8,128)(2,1)S(1)}, bf16[96,768]{1,0:T(8,128)(2,1)S(1)}, u32[]{:S(2)}, u32[]{:S(2)}) collective-permute-start(bf16[96,768]{1,0:T(8,128)(2,1)S(1)} %get-tuple-element.196), channel_id=1, source_target_pairs={{0,2},{1,3},{2,0},{3,1},{4,6},{5,7},{6,4},{7,5},{8,10},{9,11},{10,... | collective-permute-start | bytes 442376 | tf_op jit(solution)/shard_map/ppermute | solution.py:33
  206.2 18.8 %collective-permute-start.47 = (bf16[2,96,768]{2,1,0:T(8,128)(2,1)S(1)}, bf16[2,96,768]{2,1,0:T(8,128)(2,1)S(1)}, u32[]{:S(2)}, u32[]{:S(2)}) collective-permute-start(bf16[2,96,768]{2,1,0:T(8,128)(2,1)S(1)} %shard_map.343.refs_0_), channel_id=1, source_target_pairs={{0,16},{4,20},{8,24},{12,28},{16,0},{20,4},{24,8},{28,12},{1,17},{... | collective-permute-start | bytes 884744 | tf_op jit(solution)/shard_map/ppermute | solution.py:33
  206.8 18.2 %collective-permute-start.46 = (bf16[2,96,768]{2,1,0:T(8,128)(2,1)S(1)}, bf16[2,96,768]{2,1,0:T(8,128)(2,1)S(1)}, u32[]{:S(2)}, u32[]{:S(2)}) collective-permute-start(bf16[2,96,768]{2,1,0:T(8,128)(2,1)S(1)} %shard_map.343.refs_0_), channel_id=1, source_target_pairs={{0,8},{4,12},{8,0},{12,4},{16,24},{20,28},{24,16},{28,20},{1,9},{5... | collective-permute-start | bytes 884744 | tf_op jit(solution)/shard_map/ppermute | solution.py:33
  211.2 13.6 %collective-permute-start.41 = (bf16[96,896]{1,0:T(8,128)(2,1)S(1)}, bf16[96,896]{1,0:T(8,128)(2,1)S(1)}, u32[]{:S(2)}, u32[]{:S(2)}) collective-permute-start(bf16[96,896]{1,0:T(8,128)(2,1)S(1)} %get-tuple-element.200), channel_id=1, source_target_pairs={{0,2},{1,3},{2,0},{3,1},{4,6},{5,7},{6,4},{7,5},{8,10},{9,11},{10,... | collective-permute-start | bytes 516104 | tf_op jit(solution)/shard_map/ppermute | solution.py:33
  212.1 12.7 %collective-permute-start.42 = (bf16[96,896]{1,0:T(8,128)(2,1)S(1)}, bf16[96,896]{1,0:T(8,128)(2,1)S(1)}, u32[]{:S(2)}, u32[]{:S(2)}) collective-permute-start(bf16[96,896]{1,0:T(8,128)(2,1)S(1)} %get-tuple-element.201), channel_id=1, source_target_pairs={{0,3},{1,2},{2,1},{3,0},{4,7},{5,6},{6,5},{7,4},{8,11},{9,10},{10,... | collective-permute-start | bytes 516104 | tf_op jit(solution)/shard_map/ppermute | solution.py:33
  (52 other events, 348.8 us)

commit v3 on v2

--- a/solution.py
+++ b/solution.py
@@ -241,8 +241,7 @@
 
 
 def qkv_kernel(place_ref, own, other, x_ref, xo_ref, bq_ref, bv_ref, *refs):
-    outs, scratch, sem, out_sem = refs[:7], refs[7:14], refs[14], refs[15]
-    (q_ref, k_ref, v_ref), weights = scratch[:3], scratch[3:]
+    (q_ref, k_ref, v_ref), weights, sem = refs[:3], refs[3:7], refs[7]
     core = place_ref[0]
     rows, width = x_ref.shape
 
@@ -278,42 +277,31 @@
             for copy in copies(other, group):
                 copy.wait()
 
-    leaving = [pltpu.make_async_copy(scratch[k], outs[k], out_sem.at[k]) for k in range(7)]
     landed(0)
-    leaving[3].start()
-    leaving[4].start()
     x, xo = x_ref[...], xo_ref[...]
     q_ref[...] = (dot_nt(x, weights[0][...].reshape(width, width)) + bq_ref[...]).astype(BF16)
-    leaving[0].start()
     w = weights[1][...].reshape(width, width)
     k_ref[:rows] = dot_nt(x, w).astype(BF16)
     k_ref[rows:] = dot_nt(xo, w).astype(BF16)
-    leaving[1].start()
     landed(1)
-    leaving[5].start()
-    leaving[6].start()
     w = weights[2][...].reshape(width, width)
     v_ref[:rows] = (dot_nt(x, w) + bv_ref[...]).astype(BF16)
     v_ref[rows:] = (dot_nt(xo, w) + bv_ref[...]).astype(BF16)
-    leaving[2].start()
-    for copy in leaving:
-        copy.wait()
 
 
 def project(where, own, other, x, xo, bq, bv):
     rows, width = x.shape
     _, shards, _, heads, part, _ = own.shape
-    vmem, hbm = pl.BlockSpec(memory_space=pltpu.VMEM), pl.BlockSpec(memory_space=pltpu.HBM)
+    vmem = pl.BlockSpec(memory_space=pltpu.VMEM)
     space = pl.BlockSpec(memory_space=pl.ANY)
     shapes = [(rows, width), (2 * rows, width), (2 * rows, width)]
     shapes += [(shards, heads, 4, part, width)] * 4
     return pl.pallas_call(
         qkv_kernel,
         in_specs=[pl.BlockSpec(memory_space=pltpu.SMEM), space, space] + [vmem] * 4,
-        out_specs=[hbm] * 7,
+        out_specs=[vmem] * 7,
         out_shape=[jax.ShapeDtypeStruct(shape, BF16) for shape in shapes],
-        scratch_shapes=[pltpu.VMEM(shape, BF16) for shape in shapes]
-        + [pltpu.SemaphoreType.DMA((2, 2, 4)), pltpu.SemaphoreType.DMA((7,))],
+        scratch_shapes=[pltpu.SemaphoreType.DMA((2, 2, 4))],
         compiler_params=pltpu.CompilerParams(vmem_limit_bytes=18 * MIB),
         cost_estimate=FREE,
     )(where, own, other, x, xo, bq, bv)
@@ -382,7 +370,7 @@
             jax.ShapeDtypeStruct((hidden, width), F32),
             jax.ShapeDtypeStruct((width, hidden), F32),
         ],
-        compiler_params=pltpu.CompilerParams(vmem_limit_bytes=20 * MIB),
+        compiler_params=pltpu.CompilerParams(vmem_limit_bytes=58 * MIB),
     )(where, own, other)
 
 
@@ -697,6 +685,10 @@
     own_ref[...] = total + dot_nn(dq_ref[...], wq_ref[...]) + first_ref[...]
 
 
+def sum_rows_kernel(total_ref, more_ref, out_ref):
+    out_ref[...] = (total_ref[...] + more_ref[...].astype(F32)).astype(BF16)
+
+
 def pre_kernel(
     low_ref, w_own_ref, w_other_ref, slope_own_ref, slope_other_ref, own_ref, other_ref, sums_ref
 ):
@@ -818,7 +810,7 @@
     )
     ffn_z = from_shards(ffn_send)
     att_send = pack(
-        where, (2, heads, part, width), [(0, near_heads(0), (0,)), (1, near_heads(0), (1,))], pair, (), 2
+        where, (2, heads, part, width), [(0, near_heads(0), (0,)), (1, near_heads(0), (1,))], pair, (), 0
     )
     rows_send = pack(where, inputs.shape, [(0, at(), ())], [inputs], (), 1)
     ffn_stack, bq, bv, bh = stack_and_biases(where, [ffn_send] + ffn_z, width, hidden, ())
@@ -835,7 +827,7 @@
     att_far = [v.reshape(shards - 1, -1, heads, part, width) for v in att_far[:3]] + [
         v.reshape(shards - 1, heads, part, width) for v in att_far[3:]
     ]
-    att_own = pack(where, shape, moves, pair + att_far, (rows_other,), 2)
+    att_own = pack(where, shape, moves, pair + att_far, (rows_other,), 0)
     att_swap = swap(att_own, "dp", CORE)
 
     def ffn_half(near, near_index, first, diagonal, earlier):
@@ -990,6 +982,7 @@
     )
     wide = att_keep.shape[-1]
 
+    input_grad = whole_call(sum_rows_kernel, [low], (total, returned), 1)[0]
     back_pieces = third_step(back_step, (att_keep, returned))
     back_got = send_pieces(back_pieces)
     hid_step = second_step(hid_step, ffn_again, ffn_again, (back_pieces[0],))
@@ -1020,7 +1013,6 @@
         (),
     )
     att_sum = shards_reduce(att_pieces, att_got)
-    input_grad = (total + returned.astype(F32)).astype(BF16)
     att_far = from_chips(att_sum)
     ffn_far = halves_from_chips(where, ffn_sum, [att_sum])
     halves = [pl.ds(0, ffn_rows // 2), pl.ds(ffn_rows // 2, ffn_rows // 2)]

time: 251 us -> 250 us (level)
    unnamed x48 -> x56, local copies, waits for them, and re-layouts: 4.43 us -> 5.47 us
    pallas_call x9 -> x10, Pallas kernels: 14.5 us -> 15.2 us  [whole_call(): pl.pallas_call(kernel, in_specs=[vmem] * len(args) + [space] * len(earlie...]
  transfers between devices with their start and end apart: 52 -> 52, of which waited for: 28 -> 29; matrix products, arithmetic and copies ran while one was open for 2% -> 1% of each run, Pallas kernels for 21% -> 21%
where the time goes in v3:
time: 250 us; the launch traced here: 249 us
  waiting for transfers between devices  111 us (44%)
  Pallas kernels  75.2 us (30%)
  starting transfers between devices  50.9 us (20%)
  local copies, waits for them, and re-layouts  7.2 us (3%)
  other arithmetic  3.65 us (1%)
    ppermute x52, waiting for transfers between devices, swap(): return lax.ppermute(v, axis, [(i, i ^ bit) for i in range(count)])  111 us
    ppermute x52, starting transfers between devices, swap(): return lax.ppermute(v, axis, [(i, i ^ bit) for i in range(count)])  50.9 us
    pallas_call x13, Pallas kernels, packs(): pl.pallas_call(functools.partial(pack_kernel, plan, far), in_specs=[pl.Bl...  16.1 us
    pallas_call x10, Pallas kernels, whole_call(): pl.pallas_call(kernel, in_specs=[vmem] * len(args) + [space] * len(earlie...  15.2 us
    pallas_call x1, Pallas kernels, attend_back(): pl.pallas_call(functools.partial(attend_back_kernel, half_rows=rows), gri...  9.15 us
    pallas_call x2, Pallas kernels, attend(): pl.pallas_call(functools.partial(attend_kernel, half_rows=rows), grid=(pa...  8.93 us
    pallas_call x9, Pallas kernels, fold(): pl.pallas_call(functools.partial(fold_kernel, [picks for _, _, picks in g...  7.87 us
    unnamed x56, local copies, waits for them, and re-layouts  5.47 us
  transfers between devices with their start and end apart: 52, of which 29 were waited for; matrix products, arithmetic and copies ran while one was open for 1% of the time, Pallas kernels for 21%

profile of v3, /device:TPU:0, one launch (start us, length us, event | category | flops | bytes accessed | tf_op | source)
XLA Modules:
  0.0 249.2 jit_solution(14896067786999069209)
XLA Ops:
  5.0 5.1 %collective-permute-start.2 = (bf16[208,768]{1,0:T(8,128)(2,1)S(1)}, bf16[208,768]{1,0:T(8,128)(2,1)S(1)}, u32[]{:S(2)}, u32[]{:S(2)}) collective-permute-start(bf16[208,768]{1,0:T(8,128)(2,1)S(1)} %shard_map.306.refs_0_), channel_id=1, source_target_pairs={{0,3},{1,2},{2,1},{3,0},{4,7},{5,6},{6,5},{7,4},{8,11},{9,10},{10,... | collective-permute-start | bytes 958472 | tf_op jit(solution)/shard_map/ppermute | solution.py:33
  10.7 7.9 %collective-permute-done.2.refs_3_ = bf16[208,768]{1,0:T(8,128)(2,1)S(1)} collective-permute-done((bf16[208,768]{1,0:T(8,128)(2,1)S(1)}, bf16[208,768]{1,0:T(8,128)(2,1)S(1)}, u32[]{:S(2)}, u32[]{:S(2)}) %collective-permute-start.2) | collective-permute-done | bytes 319520 | tf_op jit(solution)/shard_map/ppermute | solution.py:33
  18.6 18.7 %collective-permute-done.1.refs_2_ = bf16[208,768]{1,0:T(8,128)(2,1)S(1)} collective-permute-done((bf16[208,768]{1,0:T(8,128)(2,1)S(1)}, bf16[208,768]{1,0:T(8,128)(2,1)S(1)}, u32[]{:S(2)}, u32[]{:S(2)}) %collective-permute-start.1) | collective-permute-done | bytes 319520 | tf_op jit(solution)/shard_map/ppermute | solution.py:33
  49.7 4.4 %collective-permute-done.5.refs_2_.refs_3_ = bf16[96,768]{1,0:T(8,128)(2,1)S(1)} collective-permute-done((bf16[96,768]{1,0:T(8,128)(2,1)}, bf16[96,768]{1,0:T(8,128)(2,1)S(1)}, u32[]{:S(2)}, u32[]{:S(2)}) %collective-permute-start.5) | collective-permute-done | bytes 147488 | tf_op jit(solution)/shard_map/ppermute | solution.py:33
  54.2 5.1 %collective-permute-done.4.refs_1_.refs_2_ = bf16[96,768]{1,0:T(8,128)(2,1)S(1)} collective-permute-done((bf16[96,768]{1,0:T(8,128)(2,1)}, bf16[96,768]{1,0:T(8,128)(2,1)S(1)}, u32[]{:S(2)}, u32[]{:S(2)}) %collective-permute-start.4) | collective-permute-done | bytes 147488 | tf_op jit(solution)/shard_map/ppermute | solution.py:33
  63.3 8.9 %collective-permute-done.7.refs_1_ = bf16[3,96,768]{2,1,0:T(8,128)(2,1)} collective-permute-done((bf16[3,96,768]{2,1,0:T(8,128)(2,1)}, bf16[3,96,768]{2,1,0:T(8,128)(2,1)}, u32[]{:S(2)}, u32[]{:S(2)}) %collective-permute-start.7) | collective-permute-done | bytes 442400 | tf_op jit(solution)/shard_map/ppermute | solution.py:33
  75.8 3.9 %collective-permute-done.10 = bf16[3,48,768]{2,1,0:T(8,128)(2,1)S(1)} collective-permute-done((bf16[3,48,768]{2,1,0:T(8,128)(2,1)S(1)}, bf16[3,48,768]{2,1,0:T(8,128)(2,1)S(1)}, u32[]{:S(2)}, u32[]{:S(2)}) %collective-permute-start.10) | collective-permute-done | bytes 221216 | tf_op jit(solution)/shard_map/ppermute | solution.py:33
  81.2 2.9 %shard_map.313.own = bf16[4,4,2,3,16,768]{5,4,3,2,1,0:T(8,128)(2,1)} custom-call(s32[2]{0:T(128)S(1)} %pad_add_fusion.1.place_ref, bf16[3,4,16,768]{3,2,1,0:T(8,128)(2,1)S(1)} %bitcast.49, bf16[3,4,16,768]{3,2,1,0:T(8,128)(2,1)S(1)} %bitcast.51, bf16[3,2,3,16,768]{4,3,2,1,0:T(8,128)(2,1)} %bitcast.12.refs_2_, bf16[3,2,3,16,768]{4,3,2,1,0:T(8,128)(2,1)} %bitcast.13.refs_3_, ...), custom_call_target="tpu_custom_call" | custom-call | flops 1 | bytes 1 | tf_op jit(solution)/shard_map/pallas_call | solution.py:58
  89.0 4.3 %shard_map.314 = (bf16[256,768]{1,0:T(8,128)(2,1)S(1)}, bf16[512,768]{1,0:T(8,128)(2,1)S(1)}, bf16[512,768]{1,0:T(8,128)(2,1)S(1)}, bf16[4,3,4,16,768]{4,3,2,1,0...) custom-call(s32[2]{0:T(128)S(1)} %pad_add_fusion.1.place_ref, ...), custom_call_target="tpu_custom_call" | custom-call | flops 1 | bytes 1 | tf_op jit(solution)/shard_map/pallas_call | solution.py:299
  93.3 4.4 %shard_map.315 = (bf16[256,384]{1,0:T(8,128)(2,1)S(1)}, f32[24,256]{1,0:T(8,128)S(1)}) custom-call(s32[2]{0:T(128)S(1)} %pad_add_fusion.place_ref, bf16[256,768]{1,0:T(8,128)(2,1)S(1)} %get-tuple-element.123.q_ref, bf16[512,768]{1,0:T(8,128)(2,1)S(1)} %get-tuple-element.124.k_ref, bf16[512,768]{1,0:T(8,128)(2,1)S(1)} %get-tuple-element.125.v_ref), custom_call_target="tpu_custom_call" | custom-call | flops 1 | bytes 1 | tf_op jit(solution)/shard_map/pallas_call | solution.py:440
  104.0 4.6 %shard_map.316 = (bf16[256,384]{1,0:T(8,128)(2,1)S(1)}, f32[24,256]{1,0:T(8,128)S(1)}) custom-call(s32[2]{0:T(128)S(1)} %pad_add_fusion.place_ref, bf16[256,768]{1,0:T(8,128)(2,1)S(1)} %get-tuple-element.123.q_ref, bf16[512,768]{1,0:T(8,128)(2,1)S(1)} %get-tuple-element.124.k_ref, bf16[512,768]{1,0:T(8,128)(2,1)S(1)} %get-tuple-element.125.v_ref, ...), custom_call_target="tpu_custom_call" | custom-call | flops 1 | bytes 1 | tf_op jit(solution)/shard_map/pallas_call | solution.py:440
  117.5 3.0 %collective-permute-done.18 = bf16[1536,768]{1,0:T(8,128)(2,1)S(1)} collective-permute-done((bf16[1536,768]{1,0:T(8,128)(2,1)S(1)}, bf16[1536,768]{1,0:T(8,128)(2,1)S(1)}, u32[]{:S(2)}, u32[]{:S(2)}) %collective-permute-start.18) | collective-permute-done | bytes 2359328 | tf_op jit(solution)/shard_map/ppermute | solution.py:33
  128.7 9.1 %shard_map.330 = (bf16[256,768]{1,0:T(8,128)(2,1)S(1)}, bf16[512,768]{1,0:T(8,128)(2,1)S(1)}, bf16[512,768]{1,0:T(8,128)(2,1)S(1)}) custom-call(s32[2]{0:T(128)S(1)} %pad_add_fusion.place_ref, bf16[256,768]{1,0:T(8,128)(2,1)S(1)} %get-tuple-element.123.q_ref, bf16[512,768]{1,0:T(8,128)(2,1)S(1)} %get-tuple-element.124.k_ref, ...), custom_call_target="tpu_custom_call" | custom-call | flops 1 | bytes 1 | tf_op jit(solution)/shard_map/pallas_call | solution.py:466
  139.8 5.5 %shard_map.334 = (bf16[4,4,96,896]{3,2,1,0:T(8,128)(2,1)S(1)}, bf16[4,4,96,896]{3,2,1,0:T(8,128)(2,1)S(1)}) custom-call(s32[2]{0:T(128)S(1)} %pad_add_fusion.1.place_ref, bf16[256,768]{1,0:T(8,128)(2,1)S(1)} %get-tuple-element.154.dq_ref.refs_4_, bf16[512,768]{1,0:T(8,128)(2,1)S(1)} %get-tuple-element.155.dk_ref, ...), custom_call_target="tpu_custom_call" | custom-call | flops 1 | bytes 1 | tf_op jit(solution)/shard_map/pallas_call | solution.py:573
  152.5 2.8 %collective-permute-done.27.refs_3_ = bf16[2,96,768]{2,1,0:T(8,128)(2,1)S(1)} collective-permute-done((bf16[2,96,768]{2,1,0:T(8,128)(2,1)S(1)}, bf16[2,96,768]{2,1,0:T(8,128)(2,1)S(1)}, u32[]{:S(2)}, u32[]{:S(2)}) %collective-permute-start.27) | collective-permute-done | bytes 294944 | tf_op jit(solution)/shard_map/ppermute | solution.py:33
  157.4 4.3 %collective-permute-done.20.more_ref.refs_5_ = bf16[256,768]{1,0:T(8,128)(2,1)S(1)} collective-permute-done((bf16[256,768]{1,0:T(8,128)(2,1)S(1)}, bf16[256,768]{1,0:T(8,128)(2,1)S(1)}, u32[]{:S(2)}, u32[]{:S(2)}) %collective-permute-start.20) | collective-permute-done | bytes 393248 | tf_op jit(solution)/shard_map/ppermute | solution.py:33
  162.7 6.0 %collective-permute-done.34.refs_3_ = bf16[2,2,96,768]{3,2,1,0:T(8,128)(2,1)S(1)} collective-permute-done((bf16[2,2,96,768]{3,2,1,0:T(8,128)(2,1)S(1)}, bf16[2,2,96,768]{3,2,1,0:T(8,128)(2,1)S(1)}, u32[]{:S(2)}, u32[]{:S(2)}) %collective-permute-start.34) | collective-permute-done | bytes 589856 | tf_op jit(solution)/shard_map/ppermute | solution.py:33
  172.4 4.2 %collective-permute-done.29.b_ref = bf16[96,768]{1,0:T(8,128)(2,1)S(1)} collective-permute-done((bf16[96,768]{1,0:T(8,128)(2,1)S(1)}, bf16[96,768]{1,0:T(8,128)(2,1)S(1)}, u32[]{:S(2)}, u32[]{:S(2)}) %collective-permute-start.29) | collective-permute-done | bytes 147488 | tf_op jit(solution)/shard_map/ppermute | solution.py:33
  178.2 5.4 %collective-permute-done.30.c_ref = bf16[96,768]{1,0:T(8,128)(2,1)S(1)} collective-permute-done((bf16[96,768]{1,0:T(8,128)(2,1)S(1)}, bf16[96,768]{1,0:T(8,128)(2,1)S(1)}, u32[]{:S(2)}, u32[]{:S(2)}) %collective-permute-start.30) | collective-permute-done | bytes 147488 | tf_op jit(solution)/shard_map/ppermute | solution.py:33
  190.5 2.8 %collective-permute-start.38 = (bf16[96,768]{1,0:T(8,128)(2,1)S(1)}, bf16[96,768]{1,0:T(8,128)(2,1)S(1)}, u32[]{:S(2)}, u32[]{:S(2)}) collective-permute-start(bf16[96,768]{1,0:T(8,128)(2,1)S(1)} %get-tuple-element.196), channel_id=1, source_target_pairs={{0,2},{1,3},{2,0},{3,1},{4,6},{5,7},{6,4},{7,5},{8,10},{9,11},{10,... | collective-permute-start | bytes 442376 | tf_op jit(solution)/shard_map/ppermute | solution.py:33
  197.6 6.0 %collective-permute-done.38.b_ref = bf16[96,768]{1,0:T(8,128)(2,1)S(1)} collective-permute-done((bf16[96,768]{1,0:T(8,128)(2,1)S(1)}, bf16[96,768]{1,0:T(8,128)(2,1)S(1)}, u32[]{:S(2)}, u32[]{:S(2)}) %collective-permute-start.38) | collective-permute-done | bytes 147488 | tf_op jit(solution)/shard_map/ppermute | solution.py:33
  215.0 8.8 %collective-permute-done.41.b_ref = bf16[96,896]{1,0:T(8,128)(2,1)S(1)} collective-permute-done((bf16[96,896]{1,0:T(8,128)(2,1)S(1)}, bf16[96,896]{1,0:T(8,128)(2,1)S(1)}, u32[]{:S(2)}, u32[]{:S(2)}) %collective-permute-start.41) | collective-permute-done | bytes 172064 | tf_op jit(solution)/shard_map/ppermute | solution.py:33
  225.8 3.9 %collective-permute-done.48.refs_3_ = bf16[2,48,768]{2,1,0:T(8,128)(2,1)S(1)} collective-permute-done((bf16[2,48,768]{2,1,0:T(8,128)(2,1)S(1)}, bf16[2,48,768]{2,1,0:T(8,128)(2,1)S(1)}, u32[]{:S(2)}, u32[]{:S(2)}) %collective-permute-start.48) | collective-permute-done | bytes 147488 | tf_op jit(solution)/shard_map/ppermute | solution.py:33
  235.6 4.2 %shard_map.347 = (f32[768,768]{1,0:T(8,128)}, f32[768,768]{1,0:T(8,128)}) custom-call(s32[2]{0:T(128)} %copy-done.18, bf16[4,2,96,768]{3,2,1,0:T(8,128)(2,1)} %copy-done.3, bf16[4,2,96,768]{3,2,1,0:T(8,128)(2,1)} %copy-done.20), custom_call_target="tpu_custom_call" | custom-call | tf_op jit(solution)/shard_map/pallas_call | solution.py:365
  (202 shorter events, 111.5 us)
Async XLA Ops:
  5.0 13.6 %collective-permute-start.2 = (bf16[208,768]{1,0:T(8,128)(2,1)S(1)}, bf16[208,768]{1,0:T(8,128)(2,1)S(1)}, u32[]{:S(2)}, u32[]{:S(2)}) collective-permute-start(bf16[208,768]{1,0:T(8,128)(2,1)S(1)} %shard_map.306.refs_0_), channel_id=1, source_target_pairs={{0,3},{1,2},{2,1},{3,0},{4,7},{5,6},{6,5},{7,4},{8,11},{9,10},{10,... | collective-permute-start | bytes 958472 | tf_op jit(solution)/shard_map/ppermute | solution.py:33
  10.1 27.2 %collective-permute-start.1 = (bf16[208,768]{1,0:T(8,128)(2,1)S(1)}, bf16[208,768]{1,0:T(8,128)(2,1)S(1)}, u32[]{:S(2)}, u32[]{:S(2)}) collective-permute-start(bf16[208,768]{1,0:T(8,128)(2,1)S(1)} %shard_map.306.refs_0_), channel_id=1, source_target_pairs={{0,2},{1,3},{2,0},{3,1},{4,6},{5,7},{6,4},{7,5},{8,10},{9,11},{10,... | collective-permute-start | bytes 958472 | tf_op jit(solution)/shard_map/ppermute | solution.py:33
  10.1 27.2 %collective-permute-start = (bf16[208,768]{1,0:T(8,128)(2,1)S(1)}, bf16[208,768]{1,0:T(8,128)(2,1)S(1)}, u32[]{:S(2)}, u32[]{:S(2)}) collective-permute-start(bf16[208,768]{1,0:T(8,128)(2,1)S(1)} %shard_map.306.refs_0_), channel_id=1, source_target_pairs={{0,1},{1,0},{2,3},{3,2},{4,5},{5,4},{6,7},{7,6},{8,9},{9,8},{10,11... | collective-permute-start | bytes 958472 | tf_op jit(solution)/shard_map/ppermute | solution.py:33
  39.0 33.4 %collective-permute-start.9 = (bf16[3,192,768]{2,1,0:T(8,128)(2,1)}, bf16[3,192,768]{2,1,0:T(8,128)(2,1)S(1)}, u32[]{:S(2)}, u32[]{:S(2)}) collective-permute-start(bf16[3,192,768]{2,1,0:T(8,128)(2,1)} %get-tuple-element.118.refs_1_), channel_id=1, source_target_pairs={{0,16},{4,20},{8,24},{12,28},{16,0},{20,4},{24,8},{28,12},{1,17},{... | collective-permute-start | bytes 2654216 | tf_op jit(solution)/shard_map/ppermute | solution.py:33
  40.6 31.8 %collective-permute-start.8 = (bf16[3,192,768]{2,1,0:T(8,128)(2,1)}, bf16[3,192,768]{2,1,0:T(8,128)(2,1)S(1)}, u32[]{:S(2)}, u32[]{:S(2)}) collective-permute-start(bf16[3,192,768]{2,1,0:T(8,128)(2,1)} %get-tuple-element.118.refs_1_), channel_id=1, source_target_pairs={{0,8},{4,12},{8,0},{12,4},{16,24},{20,28},{24,16},{28,20},{1,9},{5... | collective-permute-start | bytes 2654216 | tf_op jit(solution)/shard_map/ppermute | solution.py:33
  60.6 11.6 %collective-permute-start.7 = (bf16[3,96,768]{2,1,0:T(8,128)(2,1)}, bf16[3,96,768]{2,1,0:T(8,128)(2,1)}, u32[]{:S(2)}, u32[]{:S(2)}) collective-permute-start(bf16[3,96,768]{2,1,0:T(8,128)(2,1)} %shard_map.308), channel_id=1, source_target_pairs={{0,16},{4,20},{8,24},{12,28},{16,0},{20,4},{24,8},{28,12},{1,17},{... | collective-permute-start | bytes 1327112 | tf_op jit(solution)/shard_map/ppermute | solution.py:33
  63.3 12.5 %collective-permute-start.12 = (bf16[256,768]{1,0:T(8,128)(2,1)}, bf16[256,768]{1,0:T(8,128)(2,1)S(1)}, u32[]{:S(2)}, u32[]{:S(2)}) collective-permute-start(bf16[256,768]{1,0:T(8,128)(2,1)} %shard_map.312), channel_id=1, source_target_pairs={{0,1},{1,0},{2,3},{3,2},{4,5},{5,4},{6,7},{7,6},{8,9},{9,8},{10,11... | collective-permute-start | bytes 1179656 | tf_op jit(solution)/shard_map/ppermute | solution.py:33
  85.6 12.9 %collective-permute-start.14 = (bf16[3,96,768]{2,1,0:T(8,128)(2,1)}, bf16[3,96,768]{2,1,0:T(8,128)(2,1)}, u32[]{:S(2)}, u32[]{:S(2)}) collective-permute-start(bf16[3,96,768]{2,1,0:T(8,128)(2,1)} %get-tuple-element.130), channel_id=1, source_target_pairs={{0,16},{4,20},{8,24},{12,28},{16,0},{20,4},{24,8},{28,12},{1,17},{... | collective-permute-start | bytes 1327112 | tf_op jit(solution)/shard_map/ppermute | solution.py:33
  86.2 14.8 %collective-permute-start.16 = (bf16[3,96,768]{2,1,0:T(8,128)(2,1)}, bf16[3,96,768]{2,1,0:T(8,128)(2,1)}, u32[]{:S(2)}, u32[]{:S(2)}) collective-permute-start(bf16[3,96,768]{2,1,0:T(8,128)(2,1)} %get-tuple-element.134), channel_id=1, source_target_pairs={{0,8},{4,12},{8,0},{12,4},{16,24},{20,28},{24,16},{28,20},{1,9},{5... | collective-permute-start | bytes 1327112 | tf_op jit(solution)/shard_map/ppermute | solution.py:33
  123.2 15.6 %collective-permute-start.22 = (bf16[2,2,96,768]{3,2,1,0:T(8,128)(2,1)S(1)}, bf16[2,2,96,768]{3,2,1,0:T(8,128)(2,1)S(1)}, u32[]{:S(2)}, u32[]{:S(2)}) collective-permute-start(bf16[2,2,96,768]{3,2,1,0:T(8,128)(2,1)S(1)} %get-tuple-element.168), channel_id=1, source_target_pairs={{0,16},{4,20},{8,24},{12,28},{16,0},{20,4},{24,8},{28,12},{1,17},{... | collective-permute-start | bytes 1769480 | tf_op jit(solution)/shard_map/ppermute | solution.py:33
  123.7 15.3 %collective-permute-start.21 = (bf16[2,2,96,768]{3,2,1,0:T(8,128)(2,1)S(1)}, bf16[2,2,96,768]{3,2,1,0:T(8,128)(2,1)S(1)}, u32[]{:S(2)}, u32[]{:S(2)}) collective-permute-start(bf16[2,2,96,768]{3,2,1,0:T(8,128)(2,1)S(1)} %get-tuple-element.148.refs_3_), channel_id=1, source_target_pairs={{0,8},{4,12},{8,0},{12,4},{16,24},{20,28},{24,16},{28,20},{1,9},{5... | collective-permute-start | bytes 1769480 | tf_op jit(solution)/shard_map/ppermute | solution.py:33
  147.5 21.1 %collective-permute-start.34 = (bf16[2,2,96,768]{3,2,1,0:T(8,128)(2,1)S(1)}, bf16[2,2,96,768]{3,2,1,0:T(8,128)(2,1)S(1)}, u32[]{:S(2)}, u32[]{:S(2)}) collective-permute-start(bf16[2,2,96,768]{3,2,1,0:T(8,128)(2,1)S(1)} %get-tuple-element.189), channel_id=1, source_target_pairs={{0,16},{4,20},{8,24},{12,28},{16,0},{20,4},{24,8},{28,12},{1,17},{... | collective-permute-start | bytes 1769480 | tf_op jit(solution)/shard_map/ppermute | solution.py:33
  148.2 20.5 %collective-permute-start.33 = (bf16[2,2,96,768]{3,2,1,0:T(8,128)(2,1)S(1)}, bf16[2,2,96,768]{3,2,1,0:T(8,128)(2,1)S(1)}, u32[]{:S(2)}, u32[]{:S(2)}) collective-permute-start(bf16[2,2,96,768]{3,2,1,0:T(8,128)(2,1)S(1)} %get-tuple-element.153._), channel_id=1, source_target_pairs={{0,8},{4,12},{8,0},{12,4},{16,24},{20,28},{24,16},{28,20},{1,9},{5... | collective-permute-start | bytes 1769480 | tf_op jit(solution)/shard_map/ppermute | solution.py:33
  155.3 28.4 %collective-permute-start.24 = (bf16[2,2,96,896]{3,2,1,0:T(8,128)(2,1)S(1)}, bf16[2,2,96,896]{3,2,1,0:T(8,128)(2,1)S(1)}, u32[]{:S(2)}, u32[]{:S(2)}) collective-permute-start(bf16[2,2,96,896]{3,2,1,0:T(8,128)(2,1)S(1)} %get-tuple-element.173), channel_id=1, source_target_pairs={{0,8},{4,12},{8,0},{12,4},{16,24},{20,28},{24,16},{28,20},{1,9},{5... | collective-permute-start | bytes 2064392 | tf_op jit(solution)/shard_map/ppermute | solution.py:33
  156.0 27.7 %collective-permute-start.25 = (bf16[2,2,96,896]{3,2,1,0:T(8,128)(2,1)S(1)}, bf16[2,2,96,896]{3,2,1,0:T(8,128)(2,1)S(1)}, u32[]{:S(2)}, u32[]{:S(2)}) collective-permute-start(bf16[2,2,96,896]{3,2,1,0:T(8,128)(2,1)S(1)} %get-tuple-element.175), channel_id=1, source_target_pairs={{0,16},{4,20},{8,24},{12,28},{16,0},{20,4},{24,8},{28,12},{1,17},{... | collective-permute-start | bytes 2064392 | tf_op jit(solution)/shard_map/ppermute | solution.py:33
  169.4 20.2 %collective-permute-start.35 = (bf16[2,96,768]{2,1,0:T(8,128)(2,1)S(1)}, bf16[2,96,768]{2,1,0:T(8,128)(2,1)S(1)}, u32[]{:S(2)}, u32[]{:S(2)}) collective-permute-start(bf16[2,96,768]{2,1,0:T(8,128)(2,1)S(1)} %get-tuple-element.191), channel_id=1, source_target_pairs={{0,16},{4,20},{8,24},{12,28},{16,0},{20,4},{24,8},{28,12},{1,17},{... | collective-permute-start | bytes 884744 | tf_op jit(solution)/shard_map/ppermute | solution.py:33
  170.9 18.8 %collective-permute-start.36 = (bf16[2,96,768]{2,1,0:T(8,128)(2,1)S(1)}, bf16[2,96,768]{2,1,0:T(8,128)(2,1)S(1)}, u32[]{:S(2)}, u32[]{:S(2)}) collective-permute-start(bf16[2,96,768]{2,1,0:T(8,128)(2,1)S(1)} %get-tuple-element.193), channel_id=1, source_target_pairs={{0,8},{4,12},{8,0},{12,4},{16,24},{20,28},{24,16},{28,20},{1,9},{5... | collective-permute-start | bytes 884744 | tf_op jit(solution)/shard_map/ppermute | solution.py:33
  184.6 22.6 %collective-permute-start.31 = (bf16[2,96,896]{2,1,0:T(8,128)(2,1)S(1)}, bf16[2,96,896]{2,1,0:T(8,128)(2,1)S(1)}, u32[]{:S(2)}, u32[]{:S(2)}) collective-permute-start(bf16[2,96,896]{2,1,0:T(8,128)(2,1)S(1)} %get-tuple-element.184), channel_id=1, source_target_pairs={{0,16},{4,20},{8,24},{12,28},{16,0},{20,4},{24,8},{28,12},{1,17},{... | collective-permute-start | bytes 1032200 | tf_op jit(solution)/shard_map/ppermute | solution.py:33
  186.0 21.2 %collective-permute-start.32 = (bf16[2,96,896]{2,1,0:T(8,128)(2,1)S(1)}, bf16[2,96,896]{2,1,0:T(8,128)(2,1)S(1)}, u32[]{:S(2)}, u32[]{:S(2)}) collective-permute-start(bf16[2,96,896]{2,1,0:T(8,128)(2,1)S(1)} %get-tuple-element.186), channel_id=1, source_target_pairs={{0,8},{4,12},{8,0},{12,4},{16,24},{20,28},{24,16},{28,20},{1,9},{5... | collective-permute-start | bytes 1032200 | tf_op jit(solution)/shard_map/ppermute | solution.py:33
  190.5 13.1 %collective-permute-start.38 = (bf16[96,768]{1,0:T(8,128)(2,1)S(1)}, bf16[96,768]{1,0:T(8,128)(2,1)S(1)}, u32[]{:S(2)}, u32[]{:S(2)}) collective-permute-start(bf16[96,768]{1,0:T(8,128)(2,1)S(1)} %get-tuple-element.196), channel_id=1, source_target_pairs={{0,2},{1,3},{2,0},{3,1},{4,6},{5,7},{6,4},{7,5},{8,10},{9,11},{10,... | collective-permute-start | bytes 442376 | tf_op jit(solution)/shard_map/ppermute | solution.py:33
  204.3 19.7 %collective-permute-start.47 = (bf16[2,96,768]{2,1,0:T(8,128)(2,1)S(1)}, bf16[2,96,768]{2,1,0:T(8,128)(2,1)S(1)}, u32[]{:S(2)}, u32[]{:S(2)}) collective-permute-start(bf16[2,96,768]{2,1,0:T(8,128)(2,1)S(1)} %shard_map.344.refs_0_), channel_id=1, source_target_pairs={{0,16},{4,20},{8,24},{12,28},{16,0},{20,4},{24,8},{28,12},{1,17},{... | collective-permute-start | bytes 884744 | tf_op jit(solution)/shard_map/ppermute | solution.py:33
  205.8 18.2 %collective-permute-start.46 = (bf16[2,96,768]{2,1,0:T(8,128)(2,1)S(1)}, bf16[2,96,768]{2,1,0:T(8,128)(2,1)S(1)}, u32[]{:S(2)}, u32[]{:S(2)}) collective-permute-start(bf16[2,96,768]{2,1,0:T(8,128)(2,1)S(1)} %shard_map.344.refs_0_), channel_id=1, source_target_pairs={{0,8},{4,12},{8,0},{12,4},{16,24},{20,28},{24,16},{28,20},{1,9},{5... | collective-permute-start | bytes 884744 | tf_op jit(solution)/shard_map/ppermute | solution.py:33
  210.2 13.6 %collective-permute-start.41 = (bf16[96,896]{1,0:T(8,128)(2,1)S(1)}, bf16[96,896]{1,0:T(8,128)(2,1)S(1)}, u32[]{:S(2)}, u32[]{:S(2)}) collective-permute-start(bf16[96,896]{1,0:T(8,128)(2,1)S(1)} %get-tuple-element.200), channel_id=1, source_target_pairs={{0,2},{1,3},{2,0},{3,1},{4,6},{5,7},{6,4},{7,5},{8,10},{9,11},{10,... | collective-permute-start | bytes 516104 | tf_op jit(solution)/shard_map/ppermute | solution.py:33
  211.1 12.7 %collective-permute-start.42 = (bf16[96,896]{1,0:T(8,128)(2,1)S(1)}, bf16[96,896]{1,0:T(8,128)(2,1)S(1)}, u32[]{:S(2)}, u32[]{:S(2)}) collective-permute-start(bf16[96,896]{1,0:T(8,128)(2,1)S(1)} %get-tuple-element.201), channel_id=1, source_target_pairs={{0,3},{1,2},{2,1},{3,0},{4,7},{5,6},{6,5},{7,4},{8,11},{9,10},{10,... | collective-permute-start | bytes 516104 | tf_op jit(solution)/shard_map/ppermute | solution.py:33
  (56 other events, 593.1 us)

commit v4 on v3

--- a/solution.py
+++ b/solution.py
@@ -396,8 +396,8 @@
         top = jnp.max(s, axis=0, keepdims=True)
         e = jnp.exp(s - top)
         total = jnp.sum(e, axis=0, keepdims=True)
-        p = (e * (1.0 / total)).astype(BF16)
-        outs.append(dot_nn(v_turned, p)[h * HD : (h + 1) * HD])
+        out = dot_nn(v_turned, e.astype(BF16))[h * HD : (h + 1) * HD]
+        outs.append(out * (1.0 / total))
         sums.append(top + jnp.log(total))
     out_ref[...] = jnp.concatenate(outs, axis=0).T.astype(BF16)
     lse_ref[...] = jnp.concatenate(sums + [jnp.zeros((6, rows), F32)], axis=0)

time: 250 us -> 249 us (level)
  transfers between devices with their start and end apart: 52 -> 52, of which waited for: 29 -> 28; matrix products, arithmetic and copies ran while one was open for 1% -> 1% of each run, Pallas kernels for 21% -> 21%
where the time goes in v4:
time: 249 us
  waiting for transfers between devices  111 us (45%)
  Pallas kernels  74.3 us (30%)
  starting transfers between devices  50.9 us (20%)
  local copies, waits for them, and re-layouts  7.2 us (3%)
  other arithmetic  3.65 us (1%)
    ppermute x52, waiting for transfers between devices, swap(): return lax.ppermute(v, axis, [(i, i ^ bit) for i in range(count)])  111 us
    ppermute x52, starting transfers between devices, swap(): return lax.ppermute(v, axis, [(i, i ^ bit) for i in range(count)])  50.9 us
    pallas_call x13, Pallas kernels, packs(): pl.pallas_call(functools.partial(pack_kernel, plan, far), in_specs=[pl.Bl...  16.1 us
    pallas_call x10, Pallas kernels, whole_call(): pl.pallas_call(kernel, in_specs=[vmem] * len(args) + [space] * len(earlie...  15.2 us
    pallas_call x1, Pallas kernels, attend_back(): pl.pallas_call(functools.partial(attend_back_kernel, half_rows=rows), gri...  9.15 us
    pallas_call x2, Pallas kernels, attend(): pl.pallas_call(functools.partial(attend_kernel, half_rows=rows), grid=(pa...  8.06 us
    pallas_call x9, Pallas kernels, fold(): pl.pallas_call(functools.partial(fold_kernel, [picks for _, _, picks in g...  7.87 us
    pallas_call x1, Pallas kernels, attention_weight_grads(): pl.pallas_call(weights_kernel, in_specs=[pl.BlockSpec(memory_space=pltpu....  5.47 us
  transfers between devices with their start and end apart: 52, of which 28 were waited for; matrix products, arithmetic and copies ran while one was open for 1% of the time, Pallas kernels for 21%

profile of v4, /device:TPU:0, one launch (start us, length us, event | category | flops | bytes accessed | tf_op | source)
XLA Modules:
  0.0 248.8 jit_solution(17534941228989309923)
XLA Ops:
  5.0 5.1 %collective-permute-start.2 = (bf16[208,768]{1,0:T(8,128)(2,1)S(1)}, bf16[208,768]{1,0:T(8,128)(2,1)S(1)}, u32[]{:S(2)}, u32[]{:S(2)}) collective-permute-start(bf16[208,768]{1,0:T(8,128)(2,1)S(1)} %shard_map.306.refs_0_), channel_id=1, source_target_pairs={{0,3},{1,2},{2,1},{3,0},{4,7},{5,6},{6,5},{7,4},{8,11},{9,10},{10,... | collective-permute-start | bytes 958472 | tf_op jit(solution)/shard_map/ppermute | solution.py:33
  10.7 7.9 %collective-permute-done.2.refs_3_ = bf16[208,768]{1,0:T(8,128)(2,1)S(1)} collective-permute-done((bf16[208,768]{1,0:T(8,128)(2,1)S(1)}, bf16[208,768]{1,0:T(8,128)(2,1)S(1)}, u32[]{:S(2)}, u32[]{:S(2)}) %collective-permute-start.2) | collective-permute-done | bytes 319520 | tf_op jit(solution)/shard_map/ppermute | solution.py:33
  18.6 18.7 %collective-permute-done.1.refs_2_ = bf16[208,768]{1,0:T(8,128)(2,1)S(1)} collective-permute-done((bf16[208,768]{1,0:T(8,128)(2,1)S(1)}, bf16[208,768]{1,0:T(8,128)(2,1)S(1)}, u32[]{:S(2)}, u32[]{:S(2)}) %collective-permute-start.1) | collective-permute-done | bytes 319520 | tf_op jit(solution)/shard_map/ppermute | solution.py:33
  49.7 4.4 %collective-permute-done.5.refs_2_.refs_3_ = bf16[96,768]{1,0:T(8,128)(2,1)S(1)} collective-permute-done((bf16[96,768]{1,0:T(8,128)(2,1)}, bf16[96,768]{1,0:T(8,128)(2,1)S(1)}, u32[]{:S(2)}, u32[]{:S(2)}) %collective-permute-start.5) | collective-permute-done | bytes 147488 | tf_op jit(solution)/shard_map/ppermute | solution.py:33
  54.2 5.1 %collective-permute-done.4.refs_1_.refs_2_ = bf16[96,768]{1,0:T(8,128)(2,1)S(1)} collective-permute-done((bf16[96,768]{1,0:T(8,128)(2,1)}, bf16[96,768]{1,0:T(8,128)(2,1)S(1)}, u32[]{:S(2)}, u32[]{:S(2)}) %collective-permute-start.4) | collective-permute-done | bytes 147488 | tf_op jit(solution)/shard_map/ppermute | solution.py:33
  63.3 8.9 %collective-permute-done.7.refs_1_ = bf16[3,96,768]{2,1,0:T(8,128)(2,1)} collective-permute-done((bf16[3,96,768]{2,1,0:T(8,128)(2,1)}, bf16[3,96,768]{2,1,0:T(8,128)(2,1)}, u32[]{:S(2)}, u32[]{:S(2)}) %collective-permute-start.7) | collective-permute-done | bytes 442400 | tf_op jit(solution)/shard_map/ppermute | solution.py:33
  75.8 3.9 %collective-permute-done.10 = bf16[3,48,768]{2,1,0:T(8,128)(2,1)S(1)} collective-permute-done((bf16[3,48,768]{2,1,0:T(8,128)(2,1)S(1)}, bf16[3,48,768]{2,1,0:T(8,128)(2,1)S(1)}, u32[]{:S(2)}, u32[]{:S(2)}) %collective-permute-start.10) | collective-permute-done | bytes 221216 | tf_op jit(solution)/shard_map/ppermute | solution.py:33
  81.2 2.9 %shard_map.313.own = bf16[4,4,2,3,16,768]{5,4,3,2,1,0:T(8,128)(2,1)} custom-call(s32[2]{0:T(128)S(1)} %pad_add_fusion.1.place_ref, bf16[3,4,16,768]{3,2,1,0:T(8,128)(2,1)S(1)} %bitcast.49, bf16[3,4,16,768]{3,2,1,0:T(8,128)(2,1)S(1)} %bitcast.51, bf16[3,2,3,16,768]{4,3,2,1,0:T(8,128)(2,1)} %bitcast.12.refs_2_, bf16[3,2,3,16,768]{4,3,2,1,0:T(8,128)(2,1)} %bitcast.13.refs_3_, ...), custom_call_target="tpu_custom_call" | custom-call | flops 1 | bytes 1 | tf_op jit(solution)/shard_map/pallas_call | solution.py:58
  89.0 4.3 %shard_map.314 = (bf16[256,768]{1,0:T(8,128)(2,1)S(1)}, bf16[512,768]{1,0:T(8,128)(2,1)S(1)}, bf16[512,768]{1,0:T(8,128)(2,1)S(1)}, bf16[4,3,4,16,768]{4,3,2,1,0...) custom-call(s32[2]{0:T(128)S(1)} %pad_add_fusion.1.place_ref, ...), custom_call_target="tpu_custom_call" | custom-call | flops 1 | bytes 1 | tf_op jit(solution)/shard_map/pallas_call | solution.py:299
  93.3 3.9 %shard_map.315 = (bf16[256,384]{1,0:T(8,128)(2,1)S(1)}, f32[24,256]{1,0:T(8,128)S(1)}) custom-call(s32[2]{0:T(128)S(1)} %pad_add_fusion.place_ref, bf16[256,768]{1,0:T(8,128)(2,1)S(1)} %get-tuple-element.123.q_ref, bf16[512,768]{1,0:T(8,128)(2,1)S(1)} %get-tuple-element.124.k_ref, bf16[512,768]{1,0:T(8,128)(2,1)S(1)} %get-tuple-element.125.v_ref), custom_call_target="tpu_custom_call" | custom-call | flops 1 | bytes 1 | tf_op jit(solution)/shard_map/pallas_call | solution.py:440
  104.0 4.1 %shard_map.316 = (bf16[256,384]{1,0:T(8,128)(2,1)S(1)}, f32[24,256]{1,0:T(8,128)S(1)}) custom-call(s32[2]{0:T(128)S(1)} %pad_add_fusion.place_ref, bf16[256,768]{1,0:T(8,128)(2,1)S(1)} %get-tuple-element.123.q_ref, bf16[512,768]{1,0:T(8,128)(2,1)S(1)} %get-tuple-element.124.k_ref, bf16[512,768]{1,0:T(8,128)(2,1)S(1)} %get-tuple-element.125.v_ref, ...), custom_call_target="tpu_custom_call" | custom-call | flops 1 | bytes 1 | tf_op jit(solution)/shard_map/pallas_call | solution.py:440
  117.1 3.0 %collective-permute-done.18 = bf16[1536,768]{1,0:T(8,128)(2,1)S(1)} collective-permute-done((bf16[1536,768]{1,0:T(8,128)(2,1)S(1)}, bf16[1536,768]{1,0:T(8,128)(2,1)S(1)}, u32[]{:S(2)}, u32[]{:S(2)}) %collective-permute-start.18) | collective-permute-done | bytes 2359328 | tf_op jit(solution)/shard_map/ppermute | solution.py:33
  128.2 9.1 %shard_map.330 = (bf16[256,768]{1,0:T(8,128)(2,1)S(1)}, bf16[512,768]{1,0:T(8,128)(2,1)S(1)}, bf16[512,768]{1,0:T(8,128)(2,1)S(1)}) custom-call(s32[2]{0:T(128)S(1)} %pad_add_fusion.place_ref, bf16[256,768]{1,0:T(8,128)(2,1)S(1)} %get-tuple-element.123.q_ref, bf16[512,768]{1,0:T(8,128)(2,1)S(1)} %get-tuple-element.124.k_ref, ...), custom_call_target="tpu_custom_call" | custom-call | flops 1 | bytes 1 | tf_op jit(solution)/shard_map/pallas_call | solution.py:466
  139.4 5.5 %shard_map.334 = (bf16[4,4,96,896]{3,2,1,0:T(8,128)(2,1)S(1)}, bf16[4,4,96,896]{3,2,1,0:T(8,128)(2,1)S(1)}) custom-call(s32[2]{0:T(128)S(1)} %pad_add_fusion.1.place_ref, bf16[256,768]{1,0:T(8,128)(2,1)S(1)} %get-tuple-element.154.dq_ref.refs_4_, bf16[512,768]{1,0:T(8,128)(2,1)S(1)} %get-tuple-element.155.dk_ref, ...), custom_call_target="tpu_custom_call" | custom-call | flops 1 | bytes 1 | tf_op jit(solution)/shard_map/pallas_call | solution.py:573
  152.1 2.8 %collective-permute-done.27.refs_3_ = bf16[2,96,768]{2,1,0:T(8,128)(2,1)S(1)} collective-permute-done((bf16[2,96,768]{2,1,0:T(8,128)(2,1)S(1)}, bf16[2,96,768]{2,1,0:T(8,128)(2,1)S(1)}, u32[]{:S(2)}, u32[]{:S(2)}) %collective-permute-start.27) | collective-permute-done | bytes 294944 | tf_op jit(solution)/shard_map/ppermute | solution.py:33
  157.0 4.2 %collective-permute-done.20.more_ref.refs_5_ = bf16[256,768]{1,0:T(8,128)(2,1)S(1)} collective-permute-done((bf16[256,768]{1,0:T(8,128)(2,1)S(1)}, bf16[256,768]{1,0:T(8,128)(2,1)S(1)}, u32[]{:S(2)}, u32[]{:S(2)}) %collective-permute-start.20) | collective-permute-done | bytes 393248 | tf_op jit(solution)/shard_map/ppermute | solution.py:33
  162.2 5.8 %collective-permute-done.34.refs_3_ = bf16[2,2,96,768]{3,2,1,0:T(8,128)(2,1)S(1)} collective-permute-done((bf16[2,2,96,768]{3,2,1,0:T(8,128)(2,1)S(1)}, bf16[2,2,96,768]{3,2,1,0:T(8,128)(2,1)S(1)}, u32[]{:S(2)}, u32[]{:S(2)}) %collective-permute-start.34) | collective-permute-done | bytes 589856 | tf_op jit(solution)/shard_map/ppermute | solution.py:33
  172.0 4.2 %collective-permute-done.29.b_ref = bf16[96,768]{1,0:T(8,128)(2,1)S(1)} collective-permute-done((bf16[96,768]{1,0:T(8,128)(2,1)S(1)}, bf16[96,768]{1,0:T(8,128)(2,1)S(1)}, u32[]{:S(2)}, u32[]{:S(2)}) %collective-permute-start.29) | collective-permute-done | bytes 147488 | tf_op jit(solution)/shard_map/ppermute | solution.py:33
  177.6 5.5 %collective-permute-done.30.c_ref = bf16[96,768]{1,0:T(8,128)(2,1)S(1)} collective-permute-done((bf16[96,768]{1,0:T(8,128)(2,1)S(1)}, bf16[96,768]{1,0:T(8,128)(2,1)S(1)}, u32[]{:S(2)}, u32[]{:S(2)}) %collective-permute-start.30) | collective-permute-done | bytes 147488 | tf_op jit(solution)/shard_map/ppermute | solution.py:33
  189.9 2.9 %collective-permute-start.38 = (bf16[96,768]{1,0:T(8,128)(2,1)S(1)}, bf16[96,768]{1,0:T(8,128)(2,1)S(1)}, u32[]{:S(2)}, u32[]{:S(2)}) collective-permute-start(bf16[96,768]{1,0:T(8,128)(2,1)S(1)} %get-tuple-element.196), channel_id=1, source_target_pairs={{0,2},{1,3},{2,0},{3,1},{4,6},{5,7},{6,4},{7,5},{8,10},{9,11},{10,... | collective-permute-start | bytes 442376 | tf_op jit(solution)/shard_map/ppermute | solution.py:33
  196.9 6.2 %collective-permute-done.38.b_ref = bf16[96,768]{1,0:T(8,128)(2,1)S(1)} collective-permute-done((bf16[96,768]{1,0:T(8,128)(2,1)S(1)}, bf16[96,768]{1,0:T(8,128)(2,1)S(1)}, u32[]{:S(2)}, u32[]{:S(2)}) %collective-permute-start.38) | collective-permute-done | bytes 147488 | tf_op jit(solution)/shard_map/ppermute | solution.py:33
  214.6 8.8 %collective-permute-done.41.b_ref = bf16[96,896]{1,0:T(8,128)(2,1)S(1)} collective-permute-done((bf16[96,896]{1,0:T(8,128)(2,1)S(1)}, bf16[96,896]{1,0:T(8,128)(2,1)S(1)}, u32[]{:S(2)}, u32[]{:S(2)}) %collective-permute-start.41) | collective-permute-done | bytes 172064 | tf_op jit(solution)/shard_map/ppermute | solution.py:33
  225.4 3.9 %collective-permute-done.48.refs_3_ = bf16[2,48,768]{2,1,0:T(8,128)(2,1)S(1)} collective-permute-done((bf16[2,48,768]{2,1,0:T(8,128)(2,1)S(1)}, bf16[2,48,768]{2,1,0:T(8,128)(2,1)S(1)}, u32[]{:S(2)}, u32[]{:S(2)}) %collective-permute-start.48) | collective-permute-done | bytes 147488 | tf_op jit(solution)/shard_map/ppermute | solution.py:33
  235.2 4.2 %shard_map.347 = (f32[768,768]{1,0:T(8,128)}, f32[768,768]{1,0:T(8,128)}) custom-call(s32[2]{0:T(128)} %copy-done.18, bf16[4,2,96,768]{3,2,1,0:T(8,128)(2,1)} %copy-done.3, bf16[4,2,96,768]{3,2,1,0:T(8,128)(2,1)} %copy-done.20), custom_call_target="tpu_custom_call" | custom-call | tf_op jit(solution)/shard_map/pallas_call | solution.py:365
  (202 shorter events, 111.7 us)
Async XLA Ops:
  5.0 13.6 %collective-permute-start.2 = (bf16[208,768]{1,0:T(8,128)(2,1)S(1)}, bf16[208,768]{1,0:T(8,128)(2,1)S(1)}, u32[]{:S(2)}, u32[]{:S(2)}) collective-permute-start(bf16[208,768]{1,0:T(8,128)(2,1)S(1)} %shard_map.306.refs_0_), channel_id=1, source_target_pairs={{0,3},{1,2},{2,1},{3,0},{4,7},{5,6},{6,5},{7,4},{8,11},{9,10},{10,... | collective-permute-start | bytes 958472 | tf_op jit(solution)/shard_map/ppermute | solution.py:33
  10.1 27.2 %collective-permute-start.1 = (bf16[208,768]{1,0:T(8,128)(2,1)S(1)}, bf16[208,768]{1,0:T(8,128)(2,1)S(1)}, u32[]{:S(2)}, u32[]{:S(2)}) collective-permute-start(bf16[208,768]{1,0:T(8,128)(2,1)S(1)} %shard_map.306.refs_0_), channel_id=1, source_target_pairs={{0,2},{1,3},{2,0},{3,1},{4,6},{5,7},{6,4},{7,5},{8,10},{9,11},{10,... | collective-permute-start | bytes 958472 | tf_op jit(solution)/shard_map/ppermute | solution.py:33
  10.1 27.2 %collective-permute-start = (bf16[208,768]{1,0:T(8,128)(2,1)S(1)}, bf16[208,768]{1,0:T(8,128)(2,1)S(1)}, u32[]{:S(2)}, u32[]{:S(2)}) collective-permute-start(bf16[208,768]{1,0:T(8,128)(2,1)S(1)} %shard_map.306.refs_0_), channel_id=1, source_target_pairs={{0,1},{1,0},{2,3},{3,2},{4,5},{5,4},{6,7},{7,6},{8,9},{9,8},{10,11... | collective-permute-start | bytes 958472 | tf_op jit(solution)/shard_map/ppermute | solution.py:33
  39.0 33.4 %collective-permute-start.9 = (bf16[3,192,768]{2,1,0:T(8,128)(2,1)}, bf16[3,192,768]{2,1,0:T(8,128)(2,1)S(1)}, u32[]{:S(2)}, u32[]{:S(2)}) collective-permute-start(bf16[3,192,768]{2,1,0:T(8,128)(2,1)} %get-tuple-element.118.refs_1_), channel_id=1, source_target_pairs={{0,16},{4,20},{8,24},{12,28},{16,0},{20,4},{24,8},{28,12},{1,17},{... | collective-permute-start | bytes 2654216 | tf_op jit(solution)/shard_map/ppermute | solution.py:33
  40.6 31.8 %collective-permute-start.8 = (bf16[3,192,768]{2,1,0:T(8,128)(2,1)}, bf16[3,192,768]{2,1,0:T(8,128)(2,1)S(1)}, u32[]{:S(2)}, u32[]{:S(2)}) collective-permute-start(bf16[3,192,768]{2,1,0:T(8,128)(2,1)} %get-tuple-element.118.refs_1_), channel_id=1, source_target_pairs={{0,8},{4,12},{8,0},{12,4},{16,24},{20,28},{24,16},{28,20},{1,9},{5... | collective-permute-start | bytes 2654216 | tf_op jit(solution)/shard_map/ppermute | solution.py:33
  60.6 11.6 %collective-permute-start.7 = (bf16[3,96,768]{2,1,0:T(8,128)(2,1)}, bf16[3,96,768]{2,1,0:T(8,128)(2,1)}, u32[]{:S(2)}, u32[]{:S(2)}) collective-permute-start(bf16[3,96,768]{2,1,0:T(8,128)(2,1)} %shard_map.308), channel_id=1, source_target_pairs={{0,16},{4,20},{8,24},{12,28},{16,0},{20,4},{24,8},{28,12},{1,17},{... | collective-permute-start | bytes 1327112 | tf_op jit(solution)/shard_map/ppermute | solution.py:33
  63.3 12.5 %collective-permute-start.12 = (bf16[256,768]{1,0:T(8,128)(2,1)}, bf16[256,768]{1,0:T(8,128)(2,1)S(1)}, u32[]{:S(2)}, u32[]{:S(2)}) collective-permute-start(bf16[256,768]{1,0:T(8,128)(2,1)} %shard_map.312), channel_id=1, source_target_pairs={{0,1},{1,0},{2,3},{3,2},{4,5},{5,4},{6,7},{7,6},{8,9},{9,8},{10,11... | collective-permute-start | bytes 1179656 | tf_op jit(solution)/shard_map/ppermute | solution.py:33
  85.6 12.9 %collective-permute-start.14 = (bf16[3,96,768]{2,1,0:T(8,128)(2,1)}, bf16[3,96,768]{2,1,0:T(8,128)(2,1)}, u32[]{:S(2)}, u32[]{:S(2)}) collective-permute-start(bf16[3,96,768]{2,1,0:T(8,128)(2,1)} %get-tuple-element.130), channel_id=1, source_target_pairs={{0,16},{4,20},{8,24},{12,28},{16,0},{20,4},{24,8},{28,12},{1,17},{... | collective-permute-start | bytes 1327112 | tf_op jit(solution)/shard_map/ppermute | solution.py:33
  86.2 14.8 %collective-permute-start.16 = (bf16[3,96,768]{2,1,0:T(8,128)(2,1)}, bf16[3,96,768]{2,1,0:T(8,128)(2,1)}, u32[]{:S(2)}, u32[]{:S(2)}) collective-permute-start(bf16[3,96,768]{2,1,0:T(8,128)(2,1)} %get-tuple-element.134), channel_id=1, source_target_pairs={{0,8},{4,12},{8,0},{12,4},{16,24},{20,28},{24,16},{28,20},{1,9},{5... | collective-permute-start | bytes 1327112 | tf_op jit(solution)/shard_map/ppermute | solution.py:33
  122.7 15.6 %collective-permute-start.22 = (bf16[2,2,96,768]{3,2,1,0:T(8,128)(2,1)S(1)}, bf16[2,2,96,768]{3,2,1,0:T(8,128)(2,1)S(1)}, u32[]{:S(2)}, u32[]{:S(2)}) collective-permute-start(bf16[2,2,96,768]{3,2,1,0:T(8,128)(2,1)S(1)} %get-tuple-element.168), channel_id=1, source_target_pairs={{0,16},{4,20},{8,24},{12,28},{16,0},{20,4},{24,8},{28,12},{1,17},{... | collective-permute-start | bytes 1769480 | tf_op jit(solution)/shard_map/ppermute | solution.py:33
  123.3 15.3 %collective-permute-start.21 = (bf16[2,2,96,768]{3,2,1,0:T(8,128)(2,1)S(1)}, bf16[2,2,96,768]{3,2,1,0:T(8,128)(2,1)S(1)}, u32[]{:S(2)}, u32[]{:S(2)}) collective-permute-start(bf16[2,2,96,768]{3,2,1,0:T(8,128)(2,1)S(1)} %get-tuple-element.148.refs_3_), channel_id=1, source_target_pairs={{0,8},{4,12},{8,0},{12,4},{16,24},{20,28},{24,16},{28,20},{1,9},{5... | collective-permute-start | bytes 1769480 | tf_op jit(solution)/shard_map/ppermute | solution.py:33
  147.1 20.9 %collective-permute-start.34 = (bf16[2,2,96,768]{3,2,1,0:T(8,128)(2,1)S(1)}, bf16[2,2,96,768]{3,2,1,0:T(8,128)(2,1)S(1)}, u32[]{:S(2)}, u32[]{:S(2)}) collective-permute-start(bf16[2,2,96,768]{3,2,1,0:T(8,128)(2,1)S(1)} %get-tuple-element.189), channel_id=1, source_target_pairs={{0,16},{4,20},{8,24},{12,28},{16,0},{20,4},{24,8},{28,12},{1,17},{... | collective-permute-start | bytes 1769480 | tf_op jit(solution)/shard_map/ppermute | solution.py:33
  147.6 20.5 %collective-permute-start.33 = (bf16[2,2,96,768]{3,2,1,0:T(8,128)(2,1)S(1)}, bf16[2,2,96,768]{3,2,1,0:T(8,128)(2,1)S(1)}, u32[]{:S(2)}, u32[]{:S(2)}) collective-permute-start(bf16[2,2,96,768]{3,2,1,0:T(8,128)(2,1)S(1)} %get-tuple-element.153._), channel_id=1, source_target_pairs={{0,8},{4,12},{8,0},{12,4},{16,24},{20,28},{24,16},{28,20},{1,9},{5... | collective-permute-start | bytes 1769480 | tf_op jit(solution)/shard_map/ppermute | solution.py:33
  154.8 28.4 %collective-permute-start.24 = (bf16[2,2,96,896]{3,2,1,0:T(8,128)(2,1)S(1)}, bf16[2,2,96,896]{3,2,1,0:T(8,128)(2,1)S(1)}, u32[]{:S(2)}, u32[]{:S(2)}) collective-permute-start(bf16[2,2,96,896]{3,2,1,0:T(8,128)(2,1)S(1)} %get-tuple-element.173), channel_id=1, source_target_pairs={{0,8},{4,12},{8,0},{12,4},{16,24},{20,28},{24,16},{28,20},{1,9},{5... | collective-permute-start | bytes 2064392 | tf_op jit(solution)/shard_map/ppermute | solution.py:33
  155.4 27.8 %collective-permute-start.25 = (bf16[2,2,96,896]{3,2,1,0:T(8,128)(2,1)S(1)}, bf16[2,2,96,896]{3,2,1,0:T(8,128)(2,1)S(1)}, u32[]{:S(2)}, u32[]{:S(2)}) collective-permute-start(bf16[2,2,96,896]{3,2,1,0:T(8,128)(2,1)S(1)} %get-tuple-element.175), channel_id=1, source_target_pairs={{0,16},{4,20},{8,24},{12,28},{16,0},{20,4},{24,8},{28,12},{1,17},{... | collective-permute-start | bytes 2064392 | tf_op jit(solution)/shard_map/ppermute | solution.py:33
  168.9 20.2 %collective-permute-start.35 = (bf16[2,96,768]{2,1,0:T(8,128)(2,1)S(1)}, bf16[2,96,768]{2,1,0:T(8,128)(2,1)S(1)}, u32[]{:S(2)}, u32[]{:S(2)}) collective-permute-start(bf16[2,96,768]{2,1,0:T(8,128)(2,1)S(1)} %get-tuple-element.191), channel_id=1, source_target_pairs={{0,16},{4,20},{8,24},{12,28},{16,0},{20,4},{24,8},{28,12},{1,17},{... | collective-permute-start | bytes 884744 | tf_op jit(solution)/shard_map/ppermute | solution.py:33
  170.5 18.6 %collective-permute-start.36 = (bf16[2,96,768]{2,1,0:T(8,128)(2,1)S(1)}, bf16[2,96,768]{2,1,0:T(8,128)(2,1)S(1)}, u32[]{:S(2)}, u32[]{:S(2)}) collective-permute-start(bf16[2,96,768]{2,1,0:T(8,128)(2,1)S(1)} %get-tuple-element.193), channel_id=1, source_target_pairs={{0,8},{4,12},{8,0},{12,4},{16,24},{20,28},{24,16},{28,20},{1,9},{5... | collective-permute-start | bytes 884744 | tf_op jit(solution)/shard_map/ppermute | solution.py:33
  184.1 22.7 %collective-permute-start.31 = (bf16[2,96,896]{2,1,0:T(8,128)(2,1)S(1)}, bf16[2,96,896]{2,1,0:T(8,128)(2,1)S(1)}, u32[]{:S(2)}, u32[]{:S(2)}) collective-permute-start(bf16[2,96,896]{2,1,0:T(8,128)(2,1)S(1)} %get-tuple-element.184), channel_id=1, source_target_pairs={{0,16},{4,20},{8,24},{12,28},{16,0},{20,4},{24,8},{28,12},{1,17},{... | collective-permute-start | bytes 1032200 | tf_op jit(solution)/shard_map/ppermute | solution.py:33
  185.6 21.2 %collective-permute-start.32 = (bf16[2,96,896]{2,1,0:T(8,128)(2,1)S(1)}, bf16[2,96,896]{2,1,0:T(8,128)(2,1)S(1)}, u32[]{:S(2)}, u32[]{:S(2)}) collective-permute-start(bf16[2,96,896]{2,1,0:T(8,128)(2,1)S(1)} %get-tuple-element.186), channel_id=1, source_target_pairs={{0,8},{4,12},{8,0},{12,4},{16,24},{20,28},{24,16},{28,20},{1,9},{5... | collective-permute-start | bytes 1032200 | tf_op jit(solution)/shard_map/ppermute | solution.py:33
  189.9 13.2 %collective-permute-start.38 = (bf16[96,768]{1,0:T(8,128)(2,1)S(1)}, bf16[96,768]{1,0:T(8,128)(2,1)S(1)}, u32[]{:S(2)}, u32[]{:S(2)}) collective-permute-start(bf16[96,768]{1,0:T(8,128)(2,1)S(1)} %get-tuple-element.196), channel_id=1, source_target_pairs={{0,2},{1,3},{2,0},{3,1},{4,6},{5,7},{6,4},{7,5},{8,10},{9,11},{10,... | collective-permute-start | bytes 442376 | tf_op jit(solution)/shard_map/ppermute | solution.py:33
  203.8 19.7 %collective-permute-start.47 = (bf16[2,96,768]{2,1,0:T(8,128)(2,1)S(1)}, bf16[2,96,768]{2,1,0:T(8,128)(2,1)S(1)}, u32[]{:S(2)}, u32[]{:S(2)}) collective-permute-start(bf16[2,96,768]{2,1,0:T(8,128)(2,1)S(1)} %shard_map.344.refs_0_), channel_id=1, source_target_pairs={{0,16},{4,20},{8,24},{12,28},{16,0},{20,4},{24,8},{28,12},{1,17},{... | collective-permute-start | bytes 884744 | tf_op jit(solution)/shard_map/ppermute | solution.py:33
  205.3 18.2 %collective-permute-start.46 = (bf16[2,96,768]{2,1,0:T(8,128)(2,1)S(1)}, bf16[2,96,768]{2,1,0:T(8,128)(2,1)S(1)}, u32[]{:S(2)}, u32[]{:S(2)}) collective-permute-start(bf16[2,96,768]{2,1,0:T(8,128)(2,1)S(1)} %shard_map.344.refs_0_), channel_id=1, source_target_pairs={{0,8},{4,12},{8,0},{12,4},{16,24},{20,28},{24,16},{28,20},{1,9},{5... | collective-permute-start | bytes 884744 | tf_op jit(solution)/shard_map/ppermute | solution.py:33
  209.7 13.7 %collective-permute-start.41 = (bf16[96,896]{1,0:T(8,128)(2,1)S(1)}, bf16[96,896]{1,0:T(8,128)(2,1)S(1)}, u32[]{:S(2)}, u32[]{:S(2)}) collective-permute-start(bf16[96,896]{1,0:T(8,128)(2,1)S(1)} %get-tuple-element.200), channel_id=1, source_target_pairs={{0,2},{1,3},{2,0},{3,1},{4,6},{5,7},{6,4},{7,5},{8,10},{9,11},{10,... | collective-permute-start | bytes 516104 | tf_op jit(solution)/shard_map/ppermute | solution.py:33
  210.7 12.7 %collective-permute-start.42 = (bf16[96,896]{1,0:T(8,128)(2,1)S(1)}, bf16[96,896]{1,0:T(8,128)(2,1)S(1)}, u32[]{:S(2)}, u32[]{:S(2)}) collective-permute-start(bf16[96,896]{1,0:T(8,128)(2,1)S(1)} %get-tuple-element.201), channel_id=1, source_target_pairs={{0,3},{1,2},{2,1},{3,0},{4,7},{5,6},{6,5},{7,4},{8,11},{9,10},{10,... | collective-permute-start | bytes 516104 | tf_op jit(solution)/shard_map/ppermute | solution.py:33
  (56 other events, 591.9 us)
